TPU v7x, 128 devices: a whole 4x4x4 slice. The times are simulated.
128 devices in a mesh: tm: 4 (over x), space: 32 (over y, z, core).
Axes of the slice: x: 4, y: 4, z: 4, core: 2. Of those that a mesh axis runs over, the one named last changes fastest.
Arguments:
- slice_starts: float32 [4, 2, 64, 256, 256], P('tm', None, 'space'), may hold values from 0 to 1
- feed_rate: float32 [64, 256, 256], P('space'), may hold values from 0.01 to 0.1
- kill_rate: float32 [64, 256, 256], P('space'), may hold values from 0.03 to 0.12
Outputs:
- next_starts: float32 [4, 2, 64, 256, 256], P('tm', None, 'space')
All inputs are finite; a program needn't handle non-finite values.
Results may differ from a plain program's by a relative error of at most 0.0001.
Values sent between devices are 32-bit elements; how exact they have to be, the bound alone decides.
No kernel may reach another device: no remote copies, remote signals or barrier semaphores. Data moves between devices by JAX's collectives and lax.ppermute only.
A program may use at most 128 MiB of HBM per device.

v0:
```python
import jax
import jax.numpy as jnp
from jax import lax
from jax.sharding import PartitionSpec as P

FSTEPS = 4
CSTEPS = 2


diff_u = 0.16
diff_v = 0.08


def with_halo(cells, sides, width):
    for axis, dim in sides:
        count = lax.axis_size(axis)
        head = lax.slice_in_dim(cells, 0, width, axis=dim)
        tail = lax.slice_in_dim(cells, cells.shape[dim] - width, cells.shape[dim], axis=dim)
        cells = jnp.concatenate(
            [
                lax.ppermute(tail, axis, [(i, (i + 1) % count) for i in range(count)]),
                cells,
                lax.ppermute(head, axis, [((i + 1) % count, i) for i in range(count)]),
            ],
            axis=dim,
        )
    return cells


def laplacian(padded, spacing):
    center = padded[:, 1:-1]
    total = jnp.roll(center, -1, 3) + jnp.roll(center, 1, 3)
    total = total + jnp.roll(center, -1, 2) + jnp.roll(center, 1, 2)
    total = total + padded[:, 2:] + padded[:, :-2]
    return (total - 6.0 * center) / (spacing * spacing)


def rates(padded, feed_field, kill_field, spacing):
    lap_field = laplacian(padded, spacing)
    fields = padded[:, 1:-1]
    substrate = fields[0]
    catalyst = fields[1]
    uvv_term = substrate * catalyst * catalyst
    rate_u = diff_u * lap_field[0] - uvv_term + feed_field * (1.0 - substrate)
    rate_v = diff_v * lap_field[1] + uvv_term - (feed_field + kill_field) * catalyst
    return jnp.stack([rate_u, rate_v])


def restrict(field):
    shape = field.shape
    lead = shape[:-3]
    blocks = field.reshape(lead + (shape[-3] // 2, 2, shape[-2] // 2, 2, shape[-1] // 2, 2))
    return jnp.mean(blocks, axis=(-5, -3, -1))


def prolong(field):
    return jnp.repeat(jnp.repeat(jnp.repeat(field, 2, -3), 2, -2), 2, -1)


def fine_rim(state):
    return with_halo(state, (("space", 1),), 1)


def coarse_prop(current, coarse_feed, coarse_kill):
    for step_index in range(CSTEPS):
        padded = with_halo(current, (("space", 1),), 1)
        current = current + 2.0 * rates(padded, coarse_feed, coarse_kill, 2.0)
    return current


def body(slice_starts, feed_rate, kill_rate):
    start = slice_starts[0]
    current = start
    for step_index in range(FSTEPS):
        padded = fine_rim(current)
        first_rate = rates(padded, feed_rate, kill_rate, 1.0)
        midpoint = current + 1.0 * first_rate
        padded_mid = fine_rim(midpoint)
        second_rate = rates(padded_mid, feed_rate, kill_rate, 1.0)
        current = current + 0.5 * (first_rate + second_rate)
    coarse_feed = restrict(feed_rate)
    coarse_kill = restrict(kill_rate)
    coarse_end = restrict(current)
    coarse_start = restrict(start)
    coarse_jump = coarse_end - coarse_prop(coarse_start, coarse_feed, coarse_kill)
    slice_index = lax.axis_index("tm")
    slice_count = lax.axis_size("tm")
    chained = jnp.zeros_like(coarse_start)
    all_jumps, all_starts = (
        lax.all_gather(coarse_jump[None], "tm", axis=0, tiled=True),
        lax.all_gather(coarse_start[None], "tm", axis=0, tiled=True),
    )
    walker = all_starts[0]
    for position in range(slice_count):
        walker = coarse_prop(walker, coarse_feed, coarse_kill) + all_jumps[position]
        chained = jnp.where(slice_index == position, walker, chained)
    corrected = current + prolong(chained - coarse_end)
    return corrected[None]


def solution(mesh):
    in_specs = (P("tm", None, "space", None, None), P("space", None, None), P("space", None, None))
    out_specs = P("tm", None, "space", None, None)
    return jax.shard_map(body, mesh=mesh, in_specs=in_specs, out_specs=out_specs, check_vma=False)
```

profile of v0, /device:TPU:0, one launch (start us, length us, event | category | flops | bytes accessed | tf_op | source)
XLA Modules:
  0.0 385.4 jit_solution(2152619451712557413)
XLA Ops:
  2.3 6.0 %collective-permute-start = (f32[2,1,256,256]{3,2,1,0:T(8,128)}, f32[2,1,256,256]{3,2,1,0:T(8,128)S(1)}, u32[]{:S(2)}, u32[]{:S(2)}) collective-permute-start(f32[2,1,256,256]{3,2,1,0:T(8,128)} %get-tuple-element.105), channel_id=1, source_target_pairs={{1,0},{2,1},{3,2},{4,3},{5,4},{6,5},{7,6},{8,7},{9,8},{10,9},{11,1... | collective-permute-start | bytes 1572872 | tf_op jit(solution)/shard_map/ppermute | solution.py:23
  32.4 18.1 %reduce_sum.59 = f32[128,2,128,2]{3,2,1,0:T(8,128)} reshape(f32[256,256]{1,0:T(8,128)S(1)} %get-tuple-element.108) | data formatting | bytes 524288 | tf_op jit(solution)/shard_map/reduce_sum | solution.py:53
  50.5 8.0 %reduce_sum.72 = f32[128,128]{1,0:T(8,128)S(1)} reduce(f32[128,2,128,2]{3,2,1,0:T(8,128)} %reduce_sum.59, f32[]{:T(128)} %constant.47.clone.1), dimensions={1,3}, to_apply=%region_5.6 | reduce | flops 49152 | bytes 327684 | tf_op jit(solution)/shard_map/reduce_sum | solution.py:53
  69.3 5.9 %collective-permute-done.4 = f32[2,1,256,256]{3,2,1,0:T(8,128)S(1)} collective-permute-done((f32[2,1,256,256]{3,2,1,0:T(8,128)S(1)}, f32[2,1,256,256]{3,2,1,0:T(8,128)S(1)}, u32[]{:S(2)}, u32[]{:S(2)}) %collective-permute-start.4) | collective-permute-done | bytes 524320 | tf_op jit(solution)/shard_map/ppermute | solution.py:23
  75.2 5.7 %collective-permute-done.5 = f32[2,1,256,256]{3,2,1,0:T(8,128)S(1)} collective-permute-done((f32[2,1,256,256]{3,2,1,0:T(8,128)S(1)}, f32[2,1,256,256]{3,2,1,0:T(8,128)S(1)}, u32[]{:S(2)}, u32[]{:S(2)}) %collective-permute-start.5) | collective-permute-done | bytes 524320 | tf_op jit(solution)/shard_map/ppermute | solution.py:21
  83.5 6.0 %collective-permute-done.6 = f32[2,1,256,256]{3,2,1,0:T(8,128)S(1)} collective-permute-done((f32[2,1,256,256]{3,2,1,0:T(8,128)S(1)}, f32[2,1,256,256]{3,2,1,0:T(8,128)S(1)}, u32[]{:S(2)}, u32[]{:S(2)}) %collective-permute-start.6) | collective-permute-done | bytes 524320 | tf_op jit(solution)/shard_map/ppermute | solution.py:23
  89.5 5.3 %collective-permute-done.7 = f32[2,1,256,256]{3,2,1,0:T(8,128)S(1)} collective-permute-done((f32[2,1,256,256]{3,2,1,0:T(8,128)S(1)}, f32[2,1,256,256]{3,2,1,0:T(8,128)S(1)}, u32[]{:S(2)}, u32[]{:S(2)}) %collective-permute-start.7) | collective-permute-done | bytes 524320 | tf_op jit(solution)/shard_map/ppermute | solution.py:21
  97.5 5.8 %collective-permute-done.8 = f32[2,1,256,256]{3,2,1,0:T(8,128)S(1)} collective-permute-done((f32[2,1,256,256]{3,2,1,0:T(8,128)S(1)}, f32[2,1,256,256]{3,2,1,0:T(8,128)S(1)}, u32[]{:S(2)}, u32[]{:S(2)}) %collective-permute-start.8) | collective-permute-done | bytes 524320 | tf_op jit(solution)/shard_map/ppermute | solution.py:23
  103.3 5.3 %collective-permute-done.9 = f32[2,1,256,256]{3,2,1,0:T(8,128)S(1)} collective-permute-done((f32[2,1,256,256]{3,2,1,0:T(8,128)S(1)}, f32[2,1,256,256]{3,2,1,0:T(8,128)S(1)}, u32[]{:S(2)}, u32[]{:S(2)}) %collective-permute-start.9) | collective-permute-done | bytes 524320 | tf_op jit(solution)/shard_map/ppermute | solution.py:21
  111.3 6.0 %collective-permute-done.10 = f32[2,1,256,256]{3,2,1,0:T(8,128)S(1)} collective-permute-done((f32[2,1,256,256]{3,2,1,0:T(8,128)S(1)}, f32[2,1,256,256]{3,2,1,0:T(8,128)S(1)}, u32[]{:S(2)}, u32[]{:S(2)}) %collective-permute-start.10) | collective-permute-done | bytes 524320 | tf_op jit(solution)/shard_map/ppermute | solution.py:23
  117.3 5.3 %collective-permute-done.11 = f32[2,1,256,256]{3,2,1,0:T(8,128)S(1)} collective-permute-done((f32[2,1,256,256]{3,2,1,0:T(8,128)S(1)}, f32[2,1,256,256]{3,2,1,0:T(8,128)S(1)}, u32[]{:S(2)}, u32[]{:S(2)}) %collective-permute-start.11) | collective-permute-done | bytes 524320 | tf_op jit(solution)/shard_map/ppermute | solution.py:21
  125.6 5.7 %collective-permute-done.12 = f32[2,1,256,256]{3,2,1,0:T(8,128)S(1)} collective-permute-done((f32[2,1,256,256]{3,2,1,0:T(8,128)S(1)}, f32[2,1,256,256]{3,2,1,0:T(8,128)S(1)}, u32[]{:S(2)}, u32[]{:S(2)}) %collective-permute-start.12) | collective-permute-done | bytes 524320 | tf_op jit(solution)/shard_map/ppermute | solution.py:23
  131.3 5.5 %collective-permute-done.13 = f32[2,1,256,256]{3,2,1,0:T(8,128)S(1)} collective-permute-done((f32[2,1,256,256]{3,2,1,0:T(8,128)S(1)}, f32[2,1,256,256]{3,2,1,0:T(8,128)S(1)}, u32[]{:S(2)}, u32[]{:S(2)}) %collective-permute-start.13) | collective-permute-done | bytes 524320 | tf_op jit(solution)/shard_map/ppermute | solution.py:21
  142.7 18.1 %reduce_sum.53 = f32[128,2,128,2]{3,2,1,0:T(8,128)} reshape(f32[256,256]{1,0:T(8,128)S(1)} %get-tuple-element.109) | data formatting | bytes 524288 | tf_op jit(solution)/shard_map/reduce_sum | solution.py:53
  160.8 8.0 %reduce_sum.54 = f32[128,128]{1,0:T(8,128)S(1)} reduce(f32[128,2,128,2]{3,2,1,0:T(8,128)} %reduce_sum.53, f32[]{:T(128)} %constant.47.clone.1), dimensions={1,3}, to_apply=%region_3.4 | reduce | flops 49152 | bytes 327684 | tf_op jit(solution)/shard_map/reduce_sum | solution.py:53
  177.9 35.7 %reduce_sum.47 = f32[2,128,2,128,2]{4,3,2,1,0:T(8,128)} reshape(f32[2,256,256]{2,1,0:T(8,128)} %get-tuple-element.26) | data formatting | bytes 1048576 | tf_op jit(solution)/shard_map/reduce_sum | solution.py:53
  213.6 13.2 %reduce_sum.51 = f32[2,128,128]{2,1,0:T(8,128)S(1)} reduce(f32[2,128,2,128,2]{4,3,2,1,0:T(8,128)} %reduce_sum.47, f32[]{:T(128)} %constant.47.clone.1), dimensions={2,4}, to_apply=%region_1.2 | reduce | flops 98304 | bytes 655364 | tf_op jit(solution)/shard_map/reduce_sum | solution.py:53
  232.9 13.7 %all-gather = f32[8,128,128]{2,1,0:T(8,128)S(1)} all-gather(f32[2,128,128]{2,1,0:T(8,128)S(1)} %get-tuple-element.202), channel_id=2, replica_groups=mesh['tm'=4,'space'=32] {'tm'}, dimensions={0}, use_global_device_ids=true | all-gather | bytes 655360 | tf_op jit(solution)/shard_map/all_gather | solution.py:91
  246.7 5.3 %collective-permute-start.16 = (f32[2,1,128,128]{3,2,1,0:T(8,128)S(1)}, f32[2,1,128,128]{3,2,1,0:T(8,128)}, u32[]{:S(2)}, u32[]{:S(2)}) collective-permute-start(f32[2,1,128,128]{3,2,1,0:T(8,128)S(1)} %slice_bitcast_fusion.15), channel_id=1, source_target_pairs={{1,0},{2,1},{3,2},{4,3},{5,4},{6,5},{7,6},{8,7},{9,8},{10,9},{11,1... | collective-permute-start | bytes 393224 | tf_op jit(solution)/shard_map/ppermute | solution.py:23
  254.3 34.8 %reduce_sum.74 = f32[2,128,2,128,2]{4,3,2,1,0:T(8,128)} reshape(f32[2,256,256]{2,1,0:T(8,128)S(1)} %copy-done.15) | data formatting | bytes 1048576 | tf_op jit(solution)/shard_map/reduce_sum | solution.py:53
  289.1 13.3 %reduce_sum.75 = f32[2,128,128]{2,1,0:T(8,128)S(1)} reduce(f32[2,128,2,128,2]{4,3,2,1,0:T(8,128)} %reduce_sum.74, f32[]{:T(128)} %constant.47.clone.1), dimensions={2,4}, to_apply=%region_7.8 | reduce | flops 98304 | bytes 655364 | tf_op jit(solution)/shard_map/reduce_sum | solution.py:53
  320.0 12.8 %all_gather.7 = f32[4,2,1,128,128]{4,3,2,1,0:T(8,128)S(1)} all-gather(f32[1,2,1,128,128]{4,3,2,1,0:T(8,128)S(1)} %fusion.135), channel_id=1, replica_groups=mesh['tm'=4,'space'=32] {'tm'}, dimensions={0}, use_global_device_ids=true | all-gather | bytes 655360 | tf_op jit(solution)/shard_map/all_gather | solution.py:90
  353.7 5.3 %collective-permute-done.29 = f32[2,1,128,128]{3,2,1,0:T(8,128)S(1)} collective-permute-done((f32[2,1,128,128]{3,2,1,0:T(8,128)S(1)}, f32[2,1,128,128]{3,2,1,0:T(8,128)S(1)}, u32[]{:S(2)}, u32[]{:S(2)}) %collective-permute-start.29) | collective-permute-done | bytes 131104 | tf_op jit(solution)/shard_map/ppermute | solution.py:21
  369.9 5.3 %collective-permute-done.33 = f32[2,1,128,128]{3,2,1,0:T(8,128)S(1)} collective-permute-done((f32[2,1,128,128]{3,2,1,0:T(8,128)S(1)}, f32[2,1,128,128]{3,2,1,0:T(8,128)S(1)}, u32[]{:S(2)}, u32[]{:S(2)}) %collective-permute-start.33) | collective-permute-done | bytes 131104 | tf_op jit(solution)/shard_map/ppermute | solution.py:21
  (238 shorter events, 130.1 us)
Async XLA Ops:
  2.3 13.0 %collective-permute-start = (f32[2,1,256,256]{3,2,1,0:T(8,128)}, f32[2,1,256,256]{3,2,1,0:T(8,128)S(1)}, u32[]{:S(2)}, u32[]{:S(2)}) collective-permute-start(f32[2,1,256,256]{3,2,1,0:T(8,128)} %get-tuple-element.105), channel_id=1, source_target_pairs={{1,0},{2,1},{3,2},{4,3},{5,4},{6,5},{7,6},{8,7},{9,8},{10,9},{11,1... | collective-permute-start | bytes 1572872 | tf_op jit(solution)/shard_map/ppermute | solution.py:23
  8.3 12.1 %collective-permute-start.1 = (f32[2,1,256,256]{3,2,1,0:T(8,128)}, f32[2,1,256,256]{3,2,1,0:T(8,128)S(1)}, u32[]{:S(2)}, u32[]{:S(2)}) collective-permute-start(f32[2,1,256,256]{3,2,1,0:T(8,128)} %get-tuple-element.106), channel_id=1, source_target_pairs={{0,1},{1,2},{2,3},{3,4},{4,5},{5,6},{6,7},{7,8},{8,9},{9,10},{10,1... | collective-permute-start | bytes 1572872 | tf_op jit(solution)/shard_map/ppermute | solution.py:21
  31.9 26.8 %collective-permute-start.2 = (f32[2,1,256,256]{3,2,1,0:T(8,128)}, f32[2,1,256,256]{3,2,1,0:T(8,128)}, u32[]{:S(2)}, u32[]{:S(2)}) collective-permute-start(f32[2,1,256,256]{3,2,1,0:T(8,128)} %get-tuple-element.95), channel_id=1, source_target_pairs={{1,0},{2,1},{3,2},{4,3},{5,4},{6,5},{7,6},{8,7},{9,8},{10,9},{11,1... | collective-permute-start | bytes 1572872 | tf_op jit(solution)/shard_map/ppermute | solution.py:23
  32.0 26.7 %collective-permute-start.3 = (f32[2,1,256,256]{3,2,1,0:T(8,128)}, f32[2,1,256,256]{3,2,1,0:T(8,128)}, u32[]{:S(2)}, u32[]{:S(2)}) collective-permute-start(f32[2,1,256,256]{3,2,1,0:T(8,128)} %get-tuple-element.96), channel_id=1, source_target_pairs={{0,1},{1,2},{2,3},{3,4},{4,5},{5,6},{6,7},{7,8},{8,9},{9,10},{10,1... | collective-permute-start | bytes 1572872 | tf_op jit(solution)/shard_map/ppermute | solution.py:21
  63.7 11.5 %collective-permute-start.4 = (f32[2,1,256,256]{3,2,1,0:T(8,128)S(1)}, f32[2,1,256,256]{3,2,1,0:T(8,128)S(1)}, u32[]{:S(2)}, u32[]{:S(2)}) collective-permute-start(f32[2,1,256,256]{3,2,1,0:T(8,128)S(1)} %get-tuple-element.85), channel_id=1, source_target_pairs={{1,0},{2,1},{3,2},{4,3},{5,4},{6,5},{7,6},{8,7},{9,8},{10,9},{11,1... | collective-permute-start | bytes 1572872 | tf_op jit(solution)/shard_map/ppermute | solution.py:23
  68.5 12.4 %collective-permute-start.5 = (f32[2,1,256,256]{3,2,1,0:T(8,128)S(1)}, f32[2,1,256,256]{3,2,1,0:T(8,128)S(1)}, u32[]{:S(2)}, u32[]{:S(2)}) collective-permute-start(f32[2,1,256,256]{3,2,1,0:T(8,128)S(1)} %get-tuple-element.86), channel_id=1, source_target_pairs={{0,1},{1,2},{2,3},{3,4},{4,5},{5,6},{6,7},{7,8},{8,9},{9,10},{10,1... | collective-permute-start | bytes 1572872 | tf_op jit(solution)/shard_map/ppermute | solution.py:21
  82.8 12.0 %collective-permute-start.7 = (f32[2,1,256,256]{3,2,1,0:T(8,128)S(1)}, f32[2,1,256,256]{3,2,1,0:T(8,128)S(1)}, u32[]{:S(2)}, u32[]{:S(2)}) collective-permute-start(f32[2,1,256,256]{3,2,1,0:T(8,128)S(1)} %get-tuple-element.76), channel_id=1, source_target_pairs={{0,1},{1,2},{2,3},{3,4},{4,5},{5,6},{6,7},{7,8},{8,9},{9,10},{10,1... | collective-permute-start | bytes 1572872 | tf_op jit(solution)/shard_map/ppermute | solution.py:21
  96.6 12.0 %collective-permute-start.9 = (f32[2,1,256,256]{3,2,1,0:T(8,128)S(1)}, f32[2,1,256,256]{3,2,1,0:T(8,128)S(1)}, u32[]{:S(2)}, u32[]{:S(2)}) collective-permute-start(f32[2,1,256,256]{3,2,1,0:T(8,128)S(1)} %get-tuple-element.66), channel_id=1, source_target_pairs={{0,1},{1,2},{2,3},{3,4},{4,5},{5,6},{6,7},{7,8},{8,9},{9,10},{10,1... | collective-permute-start | bytes 1572872 | tf_op jit(solution)/shard_map/ppermute | solution.py:21
  110.6 12.0 %collective-permute-start.11 = (f32[2,1,256,256]{3,2,1,0:T(8,128)S(1)}, f32[2,1,256,256]{3,2,1,0:T(8,128)S(1)}, u32[]{:S(2)}, u32[]{:S(2)}) collective-permute-start(f32[2,1,256,256]{3,2,1,0:T(8,128)S(1)} %get-tuple-element.56), channel_id=1, source_target_pairs={{0,1},{1,2},{2,3},{3,4},{4,5},{5,6},{6,7},{7,8},{8,9},{9,10},{10,1... | collective-permute-start | bytes 1572872 | tf_op jit(solution)/shard_map/ppermute | solution.py:21
  124.6 12.2 %collective-permute-start.13 = (f32[2,1,256,256]{3,2,1,0:T(8,128)S(1)}, f32[2,1,256,256]{3,2,1,0:T(8,128)S(1)}, u32[]{:S(2)}, u32[]{:S(2)}) collective-permute-start(f32[2,1,256,256]{3,2,1,0:T(8,128)S(1)} %get-tuple-element.46), channel_id=1, source_target_pairs={{0,1},{1,2},{2,3},{3,4},{4,5},{5,6},{6,7},{7,8},{8,9},{9,10},{10,1... | collective-permute-start | bytes 1572872 | tf_op jit(solution)/shard_map/ppermute | solution.py:21
  142.2 26.8 %collective-permute-start.14 = (f32[2,1,256,256]{3,2,1,0:T(8,128)}, f32[2,1,256,256]{3,2,1,0:T(8,128)}, u32[]{:S(2)}, u32[]{:S(2)}) collective-permute-start(f32[2,1,256,256]{3,2,1,0:T(8,128)} %get-tuple-element.35), channel_id=1, source_target_pairs={{1,0},{2,1},{3,2},{4,3},{5,4},{6,5},{7,6},{8,7},{9,8},{10,9},{11,1... | collective-permute-start | bytes 1572872 | tf_op jit(solution)/shard_map/ppermute | solution.py:23
  142.2 26.8 %collective-permute-start.15 = (f32[2,1,256,256]{3,2,1,0:T(8,128)}, f32[2,1,256,256]{3,2,1,0:T(8,128)}, u32[]{:S(2)}, u32[]{:S(2)}) collective-permute-start(f32[2,1,256,256]{3,2,1,0:T(8,128)} %get-tuple-element.36), channel_id=1, source_target_pairs={{0,1},{1,2},{2,3},{3,4},{4,5},{5,6},{6,7},{7,8},{8,9},{9,10},{10,1... | collective-permute-start | bytes 1572872 | tf_op jit(solution)/shard_map/ppermute | solution.py:21
  226.9 77.8 %collective-permute-start.21 = (f32[2,1,128,128]{3,2,1,0:T(8,128)S(1)}, f32[2,1,128,128]{3,2,1,0:T(8,128)}, u32[]{:S(2)}, u32[]{:S(2)}) collective-permute-start(f32[2,1,128,128]{3,2,1,0:T(8,128)S(1)} %get-tuple-element.203), channel_id=1, source_target_pairs={{0,1},{1,2},{2,3},{3,4},{4,5},{5,6},{6,7},{7,8},{8,9},{9,10},{10,1... | collective-permute-start | bytes 393224 | tf_op jit(solution)/shard_map/ppermute | solution.py:21
  226.9 77.7 %collective-permute-start.20 = (f32[2,1,128,128]{3,2,1,0:T(8,128)S(1)}, f32[2,1,128,128]{3,2,1,0:T(8,128)}, u32[]{:S(2)}, u32[]{:S(2)}) collective-permute-start(f32[2,1,128,128]{3,2,1,0:T(8,128)S(1)} %get-tuple-element.203), channel_id=1, source_target_pairs={{1,0},{2,1},{3,2},{4,3},{5,4},{6,5},{7,6},{8,7},{9,8},{10,9},{11,1... | collective-permute-start | bytes 393224 | tf_op jit(solution)/shard_map/ppermute | solution.py:23
  246.7 55.8 %collective-permute-start.17 = (f32[2,1,128,128]{3,2,1,0:T(8,128)S(1)}, f32[2,1,128,128]{3,2,1,0:T(8,128)}, u32[]{:S(2)}, u32[]{:S(2)}) collective-permute-start(f32[2,1,128,128]{3,2,1,0:T(8,128)S(1)} %slice_bitcast_fusion.15), channel_id=1, source_target_pairs={{0,1},{1,2},{2,3},{3,4},{4,5},{5,6},{6,7},{7,8},{8,9},{9,10},{10,1... | collective-permute-start | bytes 393224 | tf_op jit(solution)/shard_map/ppermute | solution.py:21
  246.7 55.7 %collective-permute-start.16 = (f32[2,1,128,128]{3,2,1,0:T(8,128)S(1)}, f32[2,1,128,128]{3,2,1,0:T(8,128)}, u32[]{:S(2)}, u32[]{:S(2)}) collective-permute-start(f32[2,1,128,128]{3,2,1,0:T(8,128)S(1)} %slice_bitcast_fusion.15), channel_id=1, source_target_pairs={{1,0},{2,1},{3,2},{4,3},{5,4},{6,5},{7,6},{8,7},{9,8},{10,9},{11,1... | collective-permute-start | bytes 393224 | tf_op jit(solution)/shard_map/ppermute | solution.py:23
  303.9 7.8 %collective-permute-start.19 = (f32[2,1,128,128]{3,2,1,0:T(8,128)S(1)}, f32[2,1,128,128]{3,2,1,0:T(8,128)S(1)}, u32[]{:S(2)}, u32[]{:S(2)}) collective-permute-start(f32[2,1,128,128]{3,2,1,0:T(8,128)S(1)} %fusion.120), channel_id=1, source_target_pairs={{0,1},{1,2},{2,3},{3,4},{4,5},{5,6},{6,7},{7,8},{8,9},{9,10},{10,1... | collective-permute-start | bytes 393224 | tf_op jit(solution)/shard_map/ppermute | solution.py:21
  312.0 7.8 %collective-permute-start.23 = (f32[2,1,128,128]{3,2,1,0:T(8,128)S(1)}, f32[2,1,128,128]{3,2,1,0:T(8,128)S(1)}, u32[]{:S(2)}, u32[]{:S(2)}) collective-permute-start(f32[2,1,128,128]{3,2,1,0:T(8,128)S(1)} %fusion.136), channel_id=1, source_target_pairs={{0,1},{1,2},{2,3},{3,4},{4,5},{5,6},{6,7},{7,8},{8,9},{9,10},{10,1... | collective-permute-start | bytes 393224 | tf_op jit(solution)/shard_map/ppermute | solution.py:21
  335.1 7.7 %collective-permute-start.25 = (f32[2,1,128,128]{3,2,1,0:T(8,128)S(1)}, f32[2,1,128,128]{3,2,1,0:T(8,128)S(1)}, u32[]{:S(2)}, u32[]{:S(2)}) collective-permute-start(f32[2,1,128,128]{3,2,1,0:T(8,128)S(1)} %fusion.144), channel_id=1, source_target_pairs={{0,1},{1,2},{2,3},{3,4},{4,5},{5,6},{6,7},{7,8},{8,9},{9,10},{10,1... | collective-permute-start | bytes 393224 | tf_op jit(solution)/shard_map/ppermute | solution.py:21
  343.1 7.8 %collective-permute-start.27 = (f32[2,1,128,128]{3,2,1,0:T(8,128)S(1)}, f32[2,1,128,128]{3,2,1,0:T(8,128)S(1)}, u32[]{:S(2)}, u32[]{:S(2)}) collective-permute-start(f32[2,1,128,128]{3,2,1,0:T(8,128)S(1)} %fusion.154), channel_id=1, source_target_pairs={{0,1},{1,2},{2,3},{3,4},{4,5},{5,6},{6,7},{7,8},{8,9},{9,10},{10,1... | collective-permute-start | bytes 393224 | tf_op jit(solution)/shard_map/ppermute | solution.py:21
  351.2 7.8 %collective-permute-start.29 = (f32[2,1,128,128]{3,2,1,0:T(8,128)S(1)}, f32[2,1,128,128]{3,2,1,0:T(8,128)S(1)}, u32[]{:S(2)}, u32[]{:S(2)}) collective-permute-start(f32[2,1,128,128]{3,2,1,0:T(8,128)S(1)} %fusion.162), channel_id=1, source_target_pairs={{0,1},{1,2},{2,3},{3,4},{4,5},{5,6},{6,7},{7,8},{8,9},{9,10},{10,1... | collective-permute-start | bytes 393224 | tf_op jit(solution)/shard_map/ppermute | solution.py:21
  359.3 7.8 %collective-permute-start.31 = (f32[2,1,128,128]{3,2,1,0:T(8,128)S(1)}, f32[2,1,128,128]{3,2,1,0:T(8,128)S(1)}, u32[]{:S(2)}, u32[]{:S(2)}) collective-permute-start(f32[2,1,128,128]{3,2,1,0:T(8,128)S(1)} %fusion.172), channel_id=1, source_target_pairs={{0,1},{1,2},{2,3},{3,4},{4,5},{5,6},{6,7},{7,8},{8,9},{9,10},{10,1... | collective-permute-start | bytes 393224 | tf_op jit(solution)/shard_map/ppermute | solution.py:21
  367.4 7.8 %collective-permute-start.33 = (f32[2,1,128,128]{3,2,1,0:T(8,128)S(1)}, f32[2,1,128,128]{3,2,1,0:T(8,128)S(1)}, u32[]{:S(2)}, u32[]{:S(2)}) collective-permute-start(f32[2,1,128,128]{3,2,1,0:T(8,128)S(1)} %fusion.180), channel_id=1, source_target_pairs={{0,1},{1,2},{2,3},{3,4},{4,5},{5,6},{6,7},{7,8},{8,9},{9,10},{10,1... | collective-permute-start | bytes 393224 | tf_op jit(solution)/shard_map/ppermute | solution.py:21
  375.4 7.8 %collective-permute-start.35 = (f32[2,1,128,128]{3,2,1,0:T(8,128)S(1)}, f32[2,1,128,128]{3,2,1,0:T(8,128)S(1)}, u32[]{:S(2)}, u32[]{:S(2)}) collective-permute-start(f32[2,1,128,128]{3,2,1,0:T(8,128)S(1)} %fusion.189), channel_id=1, source_target_pairs={{0,1},{1,2},{2,3},{3,4},{4,5},{5,6},{6,7},{7,8},{8,9},{9,10},{10,1... | collective-permute-start | bytes 393224 | tf_op jit(solution)/shard_map/ppermute | solution.py:21
  (32 other events, 701.0 us)
where the time goes:
time: 393 us; the launch traced here: 385 us
  local copies, waits for them, and re-layouts  134 us (34%)
  waiting for transfers between devices  108 us (27%)
  other arithmetic  74.7 us (19%)
  starting transfers between devices  40.6 us (10%)
  blocking collectives  26.5 us (7%)
    reduce_sum x4, local copies, waits for them, and re-layouts, restrict(): return jnp.mean(blocks, axis=(-5, -3, -1))  107 us
    ppermute x18, waiting for transfers between devices, with_halo(): lax.ppermute(tail, axis, [(i, (i + 1) % count) for i in range(count)])  68.5 us
    reduce_sum x5, other arithmetic, restrict(): return jnp.mean(blocks, axis=(-5, -3, -1))  47.2 us
    ppermute x18, waiting for transfers between devices, with_halo(): lax.ppermute(head, axis, [((i + 1) % count, i) for i in range(count)])  39.6 us
    ppermute x18, starting transfers between devices, with_halo(): lax.ppermute(head, axis, [((i + 1) % count, i) for i in range(count)])  34.4 us
    slice x36, local copies, waits for them, and re-layouts, laplacian(): total = jnp.roll(center, -1, 3) + jnp.roll(center, 1, 3)  15.8 us
    all_gather x1, blocking collectives, body(): lax.all_gather(coarse_start[None], 'tm', axis=0, tiled=True)  13.7 us
    all_gather x1, blocking collectives, body(): lax.all_gather(coarse_jump[None], 'tm', axis=0, tiled=True)  12.8 us
  transfers between devices with their start and end apart: 36, of which 26 were waited for; matrix products, arithmetic and copies ran while one was open for 30% of the time, Pallas kernels for 0%

commit v1 on v0

v1 whole, which is shorter than its diff:
```python
import functools

import jax
import jax.numpy as jnp
from jax import lax
from jax.experimental import pallas as pl
from jax.experimental.pallas import tpu as pltpu
from jax.sharding import PartitionSpec as P

FSTEPS = 4
CSTEPS = 2
DU = 0.16
DV = 0.08
FIRST = 22
TILES = 32
F32 = jnp.float32
HIGH = lax.Precision.HIGHEST
VMEM_LIMIT = 40 * 1024 * 1024


def splitter(transposed):
    r = lax.broadcasted_iota(jnp.int32, (256, 256), 0)
    c = lax.broadcasted_iota(jnp.int32, (256, 256), 1)
    if transposed:
        r, c = c, r
    return jnp.where(r == 2 * (c % 128) + c // 128, 1.0, 0.0).astype(F32)


def prep_kernel(parity, x, feed, kill, pair_a, pair_b, cross_a, cross_b, rows):
    mat = splitter(False)
    flip = parity[0]

    def scatter(plane, targets):
        done = jnp.dot(plane, mat, precision=HIGH, preferred_element_type=F32)
        rows[0] = done[:, :128]
        rows[1] = done[:, 128:]
        for i in range(TILES):
            for h in range(2):
                tile = rows[h, pl.ds(i, 8, stride=32), :]
                for (a, b), q in targets:
                    if i < FIRST:
                        a[q, i, h] = tile
                    else:
                        b[q, i - FIRST, h] = tile

    pair, cross = (pair_a, pair_b), (cross_a, cross_b)
    for sp in range(2):
        for q in range(2):
            scatter(x[sp, q ^ flip], [(pair, 2 * sp + q), (cross, 2 * sp + q)])
    for q, target in ((0, cross), (1, pair)):
        f = feed[q ^ flip]
        scatter(f, [(target, 4)])
        scatter(0.52 - (f + kill[q ^ flip]), [(target, 5)])


def prep(parity, x, feed, kill):
    a = jax.ShapeDtypeStruct((6, FIRST, 2, 8, 128), F32)
    b = jax.ShapeDtypeStruct((6, TILES - FIRST, 2, 8, 128), F32)
    vm = pl.BlockSpec(memory_space=pltpu.VMEM)
    return pl.pallas_call(
        prep_kernel,
        out_shape=[a, b, a, b],
        in_specs=[pl.BlockSpec(memory_space=pltpu.SMEM), vm, vm, vm],
        out_specs=[vm] * 4,
        scratch_shapes=[pltpu.VMEM((2, 256, 128), F32)],
        compiler_params=pltpu.CompilerParams(vmem_limit_bytes=VMEM_LIMIT),
        name="prep",
    )(parity, x, feed, kill)


ORDER = (1, 0, 2, 3, 5, 4)


def heun_kernel(step, second, total, *refs):
    refs = list(refs)
    groups = 2 if second else 1
    state = [refs[3 * g:3 * g + 3] for g in range(groups)]
    refs = refs[3 * groups:]
    rate = [refs[4 * g:4 * g + 4] for g in range(groups)]
    refs = refs[4 * groups:]
    out, cells, mids, coef, sems = refs
    copies = []

    def copy(src, dst):
        c = pltpu.make_async_copy(src, dst, sems.at[len(copies)])
        c.start()
        copies.append(c)

    lo = FIRST - 2 * step - 4 if second else 2 * step
    if second:
        na = FIRST - 4 * step
        pieces = [(0, na - 4, 0, 4), (1, 0, 4, total - 8), (0, 0, total - 4, 4)]
        rate_pieces = [(0, lo, 0, FIRST - lo), (1, 0, FIRST - lo, TILES - FIRST), (0, 0, TILES - lo, total - TILES + lo)]
    else:
        pieces = [(0, 0, 0, total)]
        rate_pieces = [(0, lo, 0, total)]
    for g, at, to, n in pieces:
        for ref, slot in zip(state[g], (2, 0, 4)):
            for sp in range(2):
                copy(ref.at[pl.ds(2 * sp, 2), pl.ds(at, n)], cells.at[sp, pl.ds(slot, 2), pl.ds(to, n)])
    for g, at, to, n in rate_pieces:
        sent_cross, sent_pair, got_cross, got_pair = rate[g]
        for ref, place in ((got_cross, 0), (sent_cross, 1), (sent_pair, 2), (got_pair, 3)):
            copy(ref.at[pl.ds(4, 2), pl.ds(at, n)], coef.at[:, place, pl.ds(to, n)])
    for c in copies:
        c.wait()
    if second:
        for sp in range(2):
            for slot in range(6):
                for j in range(total - 4, total):
                    for h in range(2):
                        cells[sp, slot, j, h] = pltpu.roll(cells[sp, slot, j, h], 7, 0)
            for place in range(4):
                for j in range(TILES - lo, total):
                    for h in range(2):
                        coef[sp, place, j, h] = pltpu.roll(coef[sp, place, j, h], 7, 0)

    def beside(here, other, h):
        return other + pltpu.roll(other, 1 if h == 0 else 127, 1)

    @pl.loop(1, total - 1)
    def _(j):
        mid = [[cells[sp, ORDER[p], j, h] for h in range(2)] for sp in range(2) for p in range(6)]
        for p in range(1, 5):
            for h in range(2):
                new = []
                for sp in range(2):
                    at = sp * 6 + p
                    slot = ORDER[p]
                    total6 = beside(None, mid[at][1 - h], h) + (cells[sp, slot, j - 1, h] + cells[sp, slot, j + 1, h])
                    total6 = total6 + (mid[at - 1][h] + mid[at + 1][h])
                    new.append(total6)
                u, v = mid[p][h], mid[6 + p][h]
                uvv = u * v * v
                f, cv = coef[0, p - 1, j, h], coef[1, p - 1, j, h]
                mids[0, p - 1, j, h] = DU * new[0] + (1.0 - 6.0 * DU) * u + f * (1.0 - u) - uvv
                mids[1, p - 1, j, h] = DV * new[1] + cv * v + uvv

    @pl.loop(2, total - 2)
    def _(j):
        mid = [[mids[sp, p, j, h] for h in range(2)] for sp in range(2) for p in range(4)]
        for p in range(1, 3):
            for h in range(2):
                new = []
                for sp in range(2):
                    at = sp * 4 + p
                    total6 = beside(None, mid[at][1 - h], h) + (mids[sp, p, j - 1, h] + mids[sp, p, j + 1, h])
                    total6 = total6 + (mid[at - 1][h] + mid[at + 1][h])
                    new.append(total6)
                u, v = mid[p][h], mid[4 + p][h]
                uvv = u * v * v
                f, cv = coef[0, p, j, h], coef[1, p, j, h]
                ru = DU * new[0] + (1.0 - 6.0 * DU) * u + f * (1.0 - u) - uvv
                rv = DV * new[1] + cv * v + uvv
                out[p - 1, j - 2, h] = 0.5 * (cells[0, p + 1, j, h] + ru)
                out[2 + p - 1, j - 2, h] = 0.5 * (cells[1, p + 1, j, h] + rv)


def heun(step, second, state, rate):
    total = (TILES - FIRST + 4 * step + 8) if second else FIRST - 4 * step
    groups = len(state)
    ins = [r for g in state for r in g] + [r for g in rate for r in g]
    copies = (18 + 12) if second else 10
    return pl.pallas_call(
        functools.partial(heun_kernel, step, second, total),
        out_shape=jax.ShapeDtypeStruct((4, total - 4, 2, 8, 128), F32),
        in_specs=[pl.BlockSpec(memory_space=pl.ANY)] * len(ins),
        out_specs=pl.BlockSpec(memory_space=pltpu.VMEM),
        scratch_shapes=[
            pltpu.VMEM((2, 6, total, 2, 8, 128), F32),
            pltpu.VMEM((2, 4, total, 2, 8, 128), F32),
            pltpu.VMEM((2, 4, total, 2, 8, 128), F32),
            pltpu.SemaphoreType.DMA((copies,)),
        ],
        compiler_params=pltpu.CompilerParams(vmem_limit_bytes=VMEM_LIMIT),
        cost_estimate=pl.CostEstimate(flops=total * 2048 * 150, bytes_accessed=total * 8192 * 20, transcendentals=0),
        name="heun_b%d" % step if second else "heun_a%d" % step,
    )(*ins)


def finish_kernel(parity, state, shift, out, rows):
    mat = splitter(True)
    flip = parity[0]
    for sp in range(2):
        for q in range(2):
            for i in range(TILES):
                for h in range(2):
                    rows[h, pl.ds(i, 8, stride=32), :] = state[2 * sp + q, i, h] + shift[sp, i // 2]
            both = jnp.concatenate([rows[0], rows[1]], axis=1)
            out[sp, q ^ flip] = jnp.dot(both, mat, precision=HIGH, preferred_element_type=F32)


def finish(parity, state, shift):
    vm = pl.BlockSpec(memory_space=pltpu.VMEM)
    return pl.pallas_call(
        finish_kernel,
        out_shape=jax.ShapeDtypeStruct((2, 2, 256, 256), F32),
        in_specs=[pl.BlockSpec(memory_space=pltpu.SMEM), vm, vm],
        out_specs=vm,
        scratch_shapes=[pltpu.VMEM((2, 256, 128), F32)],
        compiler_params=pltpu.CompilerParams(vmem_limit_bytes=VMEM_LIMIT),
        name="finish",
    )(parity, state, shift)


def swap_pair(x):
    n = lax.axis_size("space")
    return lax.ppermute(x, "space", [(i, i ^ 1) for i in range(n)])


def swap_cross(x):
    n = lax.axis_size("space")
    return lax.ppermute(x, "space", [(i, (i + 1) % n if i % 2 else (i - 1) % n) for i in range(n)])


def joined(a, b, lead):
    head = jnp.roll(b[:, TILES - FIRST + lead:], 1, -2)
    return jnp.concatenate([head, a, b[:, :TILES - FIRST + lead]], axis=1)


def restrict(state):
    return 0.125 * state.reshape(2, 2, 16, 2, 2, 8, 128).sum((1, 3, 4))


def coarse_step(c, cf, ccv):
    total = jnp.roll(c, 1, 3) + jnp.roll(c, -1, 3)
    up = jnp.concatenate([c[:, 1:], jnp.roll(c[:, :1], -1, 2)], axis=1)
    down = jnp.concatenate([jnp.roll(c[:, -1:], 1, 2), c[:, :-1]], axis=1)
    total = total + up + down + swap_pair(c) + swap_cross(c)
    lap = 0.25 * (total - 6.0 * c)
    u, v = c[0], c[1]
    uvv = u * v * v
    ru = DU * lap[0] - uvv + cf * (1.0 - u)
    rv = DV * lap[1] + uvv - ccv * v
    return c + 2.0 * jnp.stack([ru, rv])


def coarse_prop(c, cf, ccv):
    for _ in range(CSTEPS):
        c = coarse_step(c, cf, ccv)
    return c


def body(slice_starts, feed, kill):
    start = slice_starts[0]
    parity = (lax.axis_index("space") % 2).astype(jnp.int32).reshape(1)
    pair_a, pair_b, cross_a, cross_b = prep(parity, start, feed, kill)
    got_pair_a, got_cross_a = swap_pair(pair_a), swap_cross(cross_a)
    got_pair_b, got_cross_b = swap_pair(pair_b), swap_cross(cross_b)
    rate_a = (cross_a, pair_a, got_cross_a, got_pair_a)
    rate_b = (cross_b, pair_b, got_cross_b, got_pair_b)
    state_a = (pair_a, got_cross_a, got_pair_a)
    state_b = (pair_b, got_cross_b, got_pair_b)
    for step in range(FSTEPS):
        new_a = heun(step, False, [state_a], [rate_a])
        last = step == FSTEPS - 1
        if not last:
            next_a = (new_a, swap_cross(new_a), swap_pair(new_a))
        new_b = heun(step, True, [state_a, state_b], [rate_a, rate_b])
        if not last:
            state_a = next_a
            state_b = (new_b, swap_cross(new_b), swap_pair(new_b))
    fine = joined(new_a, new_b, 2 * FSTEPS)
    first = jnp.concatenate([pair_a[:4], pair_b[:4]], axis=1)
    f = jnp.concatenate([jnp.stack([cross_a[4:], pair_a[4:]], 1), jnp.stack([cross_b[4:], pair_b[4:]], 1)], axis=2)
    means = restrict(f)
    cf, ccv = means[0], 0.52 - means[1]
    coarse_end = restrict(fine)
    coarse_start = restrict(first)
    jump = coarse_end - coarse_prop(coarse_start, cf, ccv)
    index = lax.axis_index("tm")
    count = lax.axis_size("tm")
    jumps, starts = (
        lax.all_gather(jump[None], "tm", axis=0, tiled=True),
        lax.all_gather(coarse_start[None], "tm", axis=0, tiled=True),
    )
    walker = starts[0]
    chained = jnp.zeros_like(walker)
    for position in range(count):
        walker = coarse_prop(walker, cf, ccv) + jumps[position]
        chained = jnp.where(index == position, walker, chained)
    return finish(parity, fine, chained - coarse_end)[None]


def solution(mesh):
    in_specs = (P("tm", None, "space", None, None), P("space", None, None), P("space", None, None))
    out_specs = P("tm", None, "space", None, None)
    return jax.shard_map(body, mesh=mesh, in_specs=in_specs, out_specs=out_specs, check_vma=False)
```

time: 393 us -> 205 us (0.52); the launches traced: 385 us -> 204 us
  local copies, waits for them, and re-layouts: 134 us -> 16.6 us
  other arithmetic: 74.7 us -> 10 us
  Pallas kernels: 0 us -> 46.4 us
  waiting for transfers between devices: 108 us -> 69.5 us
  starting transfers between devices: 40.6 us -> 33.8 us
    reduce_sum x4 -> x0, local copies, waits for them, and re-layouts: 107 us -> none  [restrict(): return jnp.mean(blocks, axis=(-5, -3, -1))]
    pallas_call x0 -> x10, Pallas kernels: none -> 46.4 us  [the longest x8 40.4 us: heun(): pl.pallas_call(functools.partial(heun_kernel, step, second, total), out_s...]
    reduce_sum x5 -> x6, other arithmetic: 47.2 us -> 3.99 us  [restrict(): return 0.125 * state.reshape(2, 2, 16, 2, 2, 8, 128).sum((1, 3, 4))]
    ppermute x36, waiting for transfers between devices: 108 us -> 69.5 us  [the longest x18 69.4 us: swap_cross(): lax.ppermute(x, 'space', [(i, (i + 1) % n if i % 2 else (i - 1) % n) for...]
    slice x80 -> x56, local copies, waits for them, and re-layouts: 26.1 us -> 7.02 us  [the longest x20 4.49 us: coarse_step(): total = jnp.roll(c, 1, 3) + jnp.roll(c, -1, 3)]
    sub x12 -> x2, other arithmetic: 14.5 us -> 0.12 us  [the longest x1 0.08 us: body(): return finish(parity, fine, chained - coarse_end)[None]]
    ppermute x36, starting transfers between devices: 40.6 us -> 33.8 us  [the longest x18 33.7 us: swap_cross(): lax.ppermute(x, 'space', [(i, (i + 1) % n if i % 2 else (i - 1) % n) for...]
    add x28 -> x16, other arithmetic: 7.68 us -> 2.08 us  [the longest x3 1.04 us: body(): walker = coarse_prop(walker, cf, ccv) + jumps[position]]
  transfers between devices with their start and end apart: 36 -> 36, of which waited for: 26 -> 10; matrix products, arithmetic and copies ran while one was open for 30% -> 9% of each run, Pallas kernels for 0% -> 16%
where the time goes in v1:
time: 205 us; the launch traced here: 204 us
  waiting for transfers between devices  69.5 us (34%)
  Pallas kernels  46.4 us (23%)
  starting transfers between devices  33.8 us (16%)
  blocking collectives  26.8 us (13%)
  local copies, waits for them, and re-layouts  16.6 us (8%)
  other arithmetic  10 us (5%)
    ppermute x18, waiting for transfers between devices, swap_cross(): lax.ppermute(x, 'space', [(i, (i + 1) % n if i % 2 else (i - 1) % n) for...  69.4 us
    pallas_call x8, Pallas kernels, heun(): pl.pallas_call(functools.partial(heun_kernel, step, second, total), out_s...  40.4 us
    ppermute x18, starting transfers between devices, swap_cross(): lax.ppermute(x, 'space', [(i, (i + 1) % n if i % 2 else (i - 1) % n) for...  33.7 us
    all_gather x1, blocking collectives, body(): lax.all_gather(coarse_start[None], 'tm', axis=0, tiled=True)  13.5 us
    all_gather x1, blocking collectives, body(): lax.all_gather(jump[None], 'tm', axis=0, tiled=True)  13.3 us
    unnamed x60, local copies, waits for them, and re-layouts  5.87 us
    slice x20, local copies, waits for them, and re-layouts, coarse_step(): total = jnp.roll(c, 1, 3) + jnp.roll(c, -1, 3)  4.49 us
  transfers between devices with their start and end apart: 36, of which 10 were waited for; matrix products, arithmetic and copies ran while one was open for 9% of the time, Pallas kernels for 16%

profile of v1, /device:TPU:0, one launch (start us, length us, event | category | flops | bytes accessed | tf_op | source)
XLA Modules:
  0.0 204.1 jit_solution(10813981007029578940)
XLA Ops:
  3.3 3.4 %prep.1 = (f32[6,22,2,8,128]{4,3,2,1,0:T(8,128)S(1)}, f32[6,10,2,8,128]{4,3,2,1,0:T(8,128)S(1)}, f32[6,22,2,8,128]{4,3,2,1,0:T(8,128)S(1)}, f32[6,10,2,8,128]{4,3,2,1,0:T(8,128)S(1)}) custom-call(s32[1]{0:T(128)} %bitcast.parity, f32[2,2,256,256]{3,2,1,0:T(8,128)S(1)} %bitcast.65, f32[2,256,256]{2,1,0:T(8,128)S(1)} %copy-done.7, f32[2,256,256]{2,1,0:T(8,128)S(1)} %copy-done.8), custom_call_target="tpu_custom_call" | custom-call | tf_op jit(solution)/shard_map/prep/pallas_call | solution.py:60
  8.7 13.5 %all-gather = f32[8,16,8,128]{3,2,1,0:T(8,128)S(1)} all-gather(f32[2,16,8,128]{3,2,1,0:T(8,128)S(1)} %broadcast_multiply_fusion.1), channel_id=2, replica_groups=mesh['tm'=4,'space'=32] {'tm'}, dimensions={0}, use_global_device_ids=true | all-gather | bytes 655360 | tf_op jit(solution)/shard_map/all_gather | solution.py:275
  22.9 4.1 %collective-permute-start.17 = (f32[2,16,8,128]{3,2,1,0:T(8,128)}, f32[2,16,8,128]{3,2,1,0:T(8,128)}, u32[]{:S(2)}, u32[]{:S(2)}) collective-permute-start(f32[2,16,8,128]{3,2,1,0:T(8,128)} %slice.715), channel_id=1, source_target_pairs={{0,31},{1,2},{2,1},{3,4},{4,3},{5,6},{6,5},{7,8},{8,7},{9,10},{10,... | collective-permute-start | bytes 393224 | tf_op jit(solution)/shard_map/ppermute | solution.py:213
  49.3 3.3 %collective-permute-done.21 = f32[2,16,8,128]{3,2,1,0:T(8,128)S(1)} collective-permute-done((f32[2,16,8,128]{3,2,1,0:T(8,128)S(1)}, f32[2,16,8,128]{3,2,1,0:T(8,128)S(1)}, u32[]{:S(2)}, u32[]{:S(2)}) %collective-permute-start.21) | collective-permute-done | bytes 131104 | tf_op jit(solution)/shard_map/ppermute | solution.py:213
  55.6 4.6 %heun_a0.1.refs_0_ = f32[4,18,2,8,128]{4,3,2,1,0:T(8,128)S(1)} custom-call(f32[6,22,2,8,128]{4,3,2,1,0:T(8,128)S(1)} %get-tuple-element.9.refs_0_.refs_4_.refs_7_, f32[6,22,2,8,128]{4,3,2,1,0:T(8,128)S(1)} %collective-permute-done.refs_1_.refs_5_.refs_8_, f32[6,22,2,8,128]{4,3,2,1,0:T(8,128)S(1)} %collective-permute-done.1.refs_2_.refs_6_.refs_9_, ...), custom_call_target="tpu_custom_call" | custom-call | flops 6758400 | bytes 3604480 | tf_op jit(solution)/shard_map/heun_a0/pallas_call | solution.py:164
  63.1 5.0 %heun_b0.1.refs_3_ = f32[4,14,2,8,128]{4,3,2,1,0:T(8,128)S(1)} custom-call(f32[6,22,2,8,128]{4,3,2,1,0:T(8,128)S(1)} %get-tuple-element.9.refs_0_.refs_4_.refs_7_, f32[6,22,2,8,128]{4,3,2,1,0:T(8,128)S(1)} %collective-permute-done.refs_1_.refs_5_.refs_8_, f32[6,22,2,8,128]{4,3,2,1,0:T(8,128)S(1)} %collective-permute-done.1.refs_2_.refs_6_.refs_9_, ...), custom_call_target="tpu_custom_call" | custom-call | flops 5529600 | bytes 2949120 | tf_op jit(solution)/shard_map/heun_b0/pallas_call | solution.py:164
  74.1 5.3 %collective-permute-done.10.refs_4_ = f32[4,14,2,8,128]{4,3,2,1,0:T(8,128)S(1)} collective-permute-done((f32[4,14,2,8,128]{4,3,2,1,0:T(8,128)S(1)}, f32[4,14,2,8,128]{4,3,2,1,0:T(8,128)S(1)}, u32[]{:S(2)}, u32[]{:S(2)}) %collective-permute-start.10) | collective-permute-done | bytes 458784 | tf_op jit(solution)/shard_map/ppermute | solution.py:213
  79.4 6.2 %heun_b1.1.refs_3_ = f32[4,18,2,8,128]{4,3,2,1,0:T(8,128)S(1)} custom-call(f32[4,18,2,8,128]{4,3,2,1,0:T(8,128)S(1)} %heun_a0.1.refs_0_, f32[4,18,2,8,128]{4,3,2,1,0:T(8,128)S(1)} %collective-permute-done.2.refs_1_, f32[4,18,2,8,128]{4,3,2,1,0:T(8,128)S(1)} %collective-permute-done.3.refs_2_, f32[4,14,2,8,128]{4,3,2,1,0:T(8,128)S(1)} %heun_b0.1.refs_3_, ...), custom_call_target="tpu_custom_call" | custom-call | flops 6758400 | bytes 3604480 | tf_op jit(solution)/shard_map/heun_b1/pallas_call | solution.py:164
  88.4 3.3 %heun_a1.1.refs_0_ = f32[4,14,2,8,128]{4,3,2,1,0:T(8,128)S(1)} custom-call(f32[4,18,2,8,128]{4,3,2,1,0:T(8,128)S(1)} %heun_a0.1.refs_0_, f32[4,18,2,8,128]{4,3,2,1,0:T(8,128)S(1)} %collective-permute-done.2.refs_1_, f32[4,18,2,8,128]{4,3,2,1,0:T(8,128)S(1)} %collective-permute-done.3.refs_2_, f32[6,22,2,8,128]{4,3,2,1,0:T(8,128)S(1)} %copy-done.1, ...), custom_call_target="tpu_custom_call" | custom-call | flops 5529600 | bytes 2949120 | tf_op jit(solution)/shard_map/heun_a1/pallas_call | solution.py:164
  94.4 8.9 %collective-permute-done.4.refs_1_ = f32[4,14,2,8,128]{4,3,2,1,0:T(8,128)S(1)} collective-permute-done((f32[4,14,2,8,128]{4,3,2,1,0:T(8,128)S(1)}, f32[4,14,2,8,128]{4,3,2,1,0:T(8,128)S(1)}, u32[]{:S(2)}, u32[]{:S(2)}) %collective-permute-start.4) | collective-permute-done | bytes 458784 | tf_op jit(solution)/shard_map/ppermute | solution.py:213
  103.3 6.4 %heun_b2.1.refs_3_ = f32[4,22,2,8,128]{4,3,2,1,0:T(8,128)S(1)} custom-call(f32[4,14,2,8,128]{4,3,2,1,0:T(8,128)S(1)} %heun_a1.1.refs_0_, f32[4,14,2,8,128]{4,3,2,1,0:T(8,128)S(1)} %collective-permute-done.4.refs_1_, f32[4,14,2,8,128]{4,3,2,1,0:T(8,128)S(1)} %collective-permute-done.5.refs_2_, f32[4,18,2,8,128]{4,3,2,1,0:T(8,128)S(1)} %heun_b1.1.refs_3_, ...), custom_call_target="tpu_custom_call" | custom-call | flops 7987200 | bytes 4259840 | tf_op jit(solution)/shard_map/heun_b2/pallas_call | solution.py:164
  112.4 4.4 %heun_a2.1.refs_0_ = f32[4,10,2,8,128]{4,3,2,1,0:T(8,128)S(1)} custom-call(f32[4,14,2,8,128]{4,3,2,1,0:T(8,128)S(1)} %heun_a1.1.refs_0_, f32[4,14,2,8,128]{4,3,2,1,0:T(8,128)S(1)} %collective-permute-done.4.refs_1_, f32[4,14,2,8,128]{4,3,2,1,0:T(8,128)S(1)} %collective-permute-done.5.refs_2_, f32[6,22,2,8,128]{4,3,2,1,0:T(8,128)S(1)} %copy-done.1, ...), custom_call_target="tpu_custom_call" | custom-call | flops 4300800 | bytes 2293760 | tf_op jit(solution)/shard_map/heun_a2/pallas_call | solution.py:164
  116.8 2.6 %collective-permute-start.6 = (f32[4,10,2,8,128]{4,3,2,1,0:T(8,128)S(1)}, f32[4,10,2,8,128]{4,3,2,1,0:T(8,128)S(1)}, u32[]{:S(2)}, u32[]{:S(2)}) collective-permute-start(f32[4,10,2,8,128]{4,3,2,1,0:T(8,128)S(1)} %heun_a2.1.refs_0_), channel_id=1, source_target_pairs={{0,31},{1,2},{2,1},{3,4},{4,3},{5,6},{6,5},{7,8},{8,7},{9,10},{10,... | collective-permute-start | bytes 983048 | tf_op jit(solution)/shard_map/ppermute | solution.py:213
  119.6 7.7 %collective-permute-done.6.refs_1_ = f32[4,10,2,8,128]{4,3,2,1,0:T(8,128)S(1)} collective-permute-done((f32[4,10,2,8,128]{4,3,2,1,0:T(8,128)S(1)}, f32[4,10,2,8,128]{4,3,2,1,0:T(8,128)S(1)}, u32[]{:S(2)}, u32[]{:S(2)}) %collective-permute-start.6) | collective-permute-done | bytes 327712 | tf_op jit(solution)/shard_map/ppermute | solution.py:213
  127.4 3.0 %heun_a3.1 = f32[4,6,2,8,128]{4,3,2,1,0:T(8,128)S(1)} custom-call(f32[4,10,2,8,128]{4,3,2,1,0:T(8,128)S(1)} %heun_a2.1.refs_0_, f32[4,10,2,8,128]{4,3,2,1,0:T(8,128)S(1)} %collective-permute-done.6.refs_1_, f32[4,10,2,8,128]{4,3,2,1,0:T(8,128)S(1)} %collective-permute-done.7.refs_2_, f32[6,22,2,8,128]{4,3,2,1,0:T(8,128)S(1)} %copy-done.1, ...), custom_call_target="tpu_custom_call" | custom-call | flops 3072000 | bytes 1638400 | tf_op jit(solution)/shard_map/heun_a3/pallas_call | solution.py:164
  130.4 7.4 %heun_b3.1 = f32[4,26,2,8,128]{4,3,2,1,0:T(8,128)S(1)} custom-call(f32[4,10,2,8,128]{4,3,2,1,0:T(8,128)S(1)} %heun_a2.1.refs_0_, f32[4,10,2,8,128]{4,3,2,1,0:T(8,128)S(1)} %collective-permute-done.6.refs_1_, f32[4,10,2,8,128]{4,3,2,1,0:T(8,128)S(1)} %collective-permute-done.7.refs_2_, f32[4,22,2,8,128]{4,3,2,1,0:T(8,128)S(1)} %heun_b2.1.refs_3_, ...), custom_call_target="tpu_custom_call" | custom-call | flops 9216000 | bytes 4915200 | tf_op jit(solution)/shard_map/heun_b3/pallas_call | solution.py:164
  138.9 13.3 %all_gather.7 = f32[4,2,16,8,128]{4,3,2,1,0:T(8,128)S(1)} all-gather(f32[1,2,16,8,128]{4,3,2,1,0:T(8,128)S(1)} %fusion.28), channel_id=1, replica_groups=mesh['tm'=4,'space'=32] {'tm'}, dimensions={0}, use_global_device_ids=true | all-gather | bytes 655360 | tf_op jit(solution)/shard_map/all_gather | solution.py:274
  153.7 7.4 %collective-permute-done.25 = f32[2,16,8,128]{3,2,1,0:T(8,128)S(1)} collective-permute-done((f32[2,16,8,128]{3,2,1,0:T(8,128)S(1)}, f32[2,16,8,128]{3,2,1,0:T(8,128)S(1)}, u32[]{:S(2)}, u32[]{:S(2)}) %collective-permute-start.25) | collective-permute-done | bytes 131104 | tf_op jit(solution)/shard_map/ppermute | solution.py:213
  161.7 7.4 %collective-permute-done.27 = f32[2,16,8,128]{3,2,1,0:T(8,128)S(1)} collective-permute-done((f32[2,16,8,128]{3,2,1,0:T(8,128)S(1)}, f32[2,16,8,128]{3,2,1,0:T(8,128)S(1)}, u32[]{:S(2)}, u32[]{:S(2)}) %collective-permute-start.27) | collective-permute-done | bytes 131104 | tf_op jit(solution)/shard_map/ppermute | solution.py:213
  169.7 7.4 %collective-permute-done.29 = f32[2,16,8,128]{3,2,1,0:T(8,128)S(1)} collective-permute-done((f32[2,16,8,128]{3,2,1,0:T(8,128)S(1)}, f32[2,16,8,128]{3,2,1,0:T(8,128)S(1)}, u32[]{:S(2)}, u32[]{:S(2)}) %collective-permute-start.29) | collective-permute-done | bytes 131104 | tf_op jit(solution)/shard_map/ppermute | solution.py:213
  177.7 7.4 %collective-permute-done.31 = f32[2,16,8,128]{3,2,1,0:T(8,128)S(1)} collective-permute-done((f32[2,16,8,128]{3,2,1,0:T(8,128)S(1)}, f32[2,16,8,128]{3,2,1,0:T(8,128)S(1)}, u32[]{:S(2)}, u32[]{:S(2)}) %collective-permute-start.31) | collective-permute-done | bytes 131104 | tf_op jit(solution)/shard_map/ppermute | solution.py:213
  185.8 7.4 %collective-permute-done.33 = f32[2,16,8,128]{3,2,1,0:T(8,128)S(1)} collective-permute-done((f32[2,16,8,128]{3,2,1,0:T(8,128)S(1)}, f32[2,16,8,128]{3,2,1,0:T(8,128)S(1)}, u32[]{:S(2)}, u32[]{:S(2)}) %collective-permute-start.33) | collective-permute-done | bytes 131104 | tf_op jit(solution)/shard_map/ppermute | solution.py:213
  193.8 7.4 %collective-permute-done.35 = f32[2,16,8,128]{3,2,1,0:T(8,128)S(1)} collective-permute-done((f32[2,16,8,128]{3,2,1,0:T(8,128)S(1)}, f32[2,16,8,128]{3,2,1,0:T(8,128)S(1)}, u32[]{:S(2)}, u32[]{:S(2)}) %collective-permute-start.35) | collective-permute-done | bytes 131104 | tf_op jit(solution)/shard_map/ppermute | solution.py:213
  201.5 2.7 %finish.1 = f32[2,2,256,256]{3,2,1,0:T(8,128)} custom-call(s32[1]{0:T(128)} %bitcast.parity, f32[4,32,2,8,128]{4,3,2,1,0:T(8,128)S(1)} %get-tuple-element.14.state, f32[2,16,8,128]{3,2,1,0:T(8,128)S(1)} %fusion.2.shift), custom_call_target="tpu_custom_call" | custom-call | tf_op jit(solution)/shard_map/finish/pallas_call | solution.py:195
  (215 shorter events, 53.7 us)
Async XLA Ops:
  8.5 47.1 %collective-permute-start.1 = (f32[6,22,2,8,128]{4,3,2,1,0:T(8,128)S(1)}, f32[6,22,2,8,128]{4,3,2,1,0:T(8,128)S(1)}, u32[]{:S(2)}, u32[]{:S(2)}) collective-permute-start(f32[6,22,2,8,128]{4,3,2,1,0:T(8,128)S(1)} %get-tuple-element.9.refs_0_.refs_4_.refs_7_), channel_id=1, source_target_pairs={{0,1},{1,0},{2,3},{3,2},{4,5},{5,4},{6,7},{7,6},{8,9},{9,8},{10,11... | collective-permute-start | bytes 3244040 | tf_op jit(solution)/shard_map/ppermute | solution.py:208
  22.9 21.9 %collective-permute-start.17 = (f32[2,16,8,128]{3,2,1,0:T(8,128)}, f32[2,16,8,128]{3,2,1,0:T(8,128)}, u32[]{:S(2)}, u32[]{:S(2)}) collective-permute-start(f32[2,16,8,128]{3,2,1,0:T(8,128)} %slice.715), channel_id=1, source_target_pairs={{0,31},{1,2},{2,1},{3,4},{4,3},{5,6},{6,5},{7,8},{8,7},{9,10},{10,... | collective-permute-start | bytes 393224 | tf_op jit(solution)/shard_map/ppermute | solution.py:213
  27.0 20.5 %collective-permute-start.16 = (f32[2,16,8,128]{3,2,1,0:T(8,128)}, f32[2,16,8,128]{3,2,1,0:T(8,128)}, u32[]{:S(2)}, u32[]{:S(2)}) collective-permute-start(f32[2,16,8,128]{3,2,1,0:T(8,128)} %slice.715), channel_id=1, source_target_pairs={{0,1},{1,0},{2,3},{3,2},{4,5},{5,4},{6,7},{7,6},{8,9},{9,8},{10,11... | collective-permute-start | bytes 393224 | tf_op jit(solution)/shard_map/ppermute | solution.py:208
  27.0 28.5 %collective-permute-start = (f32[6,22,2,8,128]{4,3,2,1,0:T(8,128)}, f32[6,22,2,8,128]{4,3,2,1,0:T(8,128)S(1)}, u32[]{:S(2)}, u32[]{:S(2)}) collective-permute-start(f32[6,22,2,8,128]{4,3,2,1,0:T(8,128)} %copy-done), channel_id=1, source_target_pairs={{0,31},{1,2},{2,1},{3,4},{4,3},{5,6},{6,5},{7,8},{8,7},{9,10},{10,... | collective-permute-start | bytes 3244040 | tf_op jit(solution)/shard_map/ppermute | solution.py:213
  29.5 33.6 %collective-permute-start.8 = (f32[6,10,2,8,128]{4,3,2,1,0:T(8,128)}, f32[6,10,2,8,128]{4,3,2,1,0:T(8,128)}, u32[]{:S(2)}, u32[]{:S(2)}) collective-permute-start(f32[6,10,2,8,128]{4,3,2,1,0:T(8,128)} %copy-done.4), channel_id=1, source_target_pairs={{0,31},{1,2},{2,1},{3,4},{4,3},{5,6},{6,5},{7,8},{8,7},{9,10},{10,... | collective-permute-start | bytes 1474568 | tf_op jit(solution)/shard_map/ppermute | solution.py:213
  44.8 7.8 %collective-permute-start.21 = (f32[2,16,8,128]{3,2,1,0:T(8,128)S(1)}, f32[2,16,8,128]{3,2,1,0:T(8,128)S(1)}, u32[]{:S(2)}, u32[]{:S(2)}) collective-permute-start(f32[2,16,8,128]{3,2,1,0:T(8,128)S(1)} %broadcast_multiply_fusion.1), channel_id=1, source_target_pairs={{0,31},{1,2},{2,1},{3,4},{4,3},{5,6},{6,5},{7,8},{8,7},{9,10},{10,... | collective-permute-start | bytes 393224 | tf_op jit(solution)/shard_map/ppermute | solution.py:213
  52.6 10.4 %collective-permute-start.9 = (f32[6,10,2,8,128]{4,3,2,1,0:T(8,128)S(1)}, f32[6,10,2,8,128]{4,3,2,1,0:T(8,128)S(1)}, u32[]{:S(2)}, u32[]{:S(2)}) collective-permute-start(f32[6,10,2,8,128]{4,3,2,1,0:T(8,128)S(1)} %copy-done.3), channel_id=1, source_target_pairs={{0,1},{1,0},{2,3},{3,2},{4,5},{5,4},{6,7},{7,6},{8,9},{9,8},{10,11... | collective-permute-start | bytes 1474568 | tf_op jit(solution)/shard_map/ppermute | solution.py:208
  52.6 10.2 %collective-permute-start.19 = (f32[2,16,8,128]{3,2,1,0:T(8,128)S(1)}, f32[2,16,8,128]{3,2,1,0:T(8,128)S(1)}, u32[]{:S(2)}, u32[]{:S(2)}) collective-permute-start(f32[2,16,8,128]{3,2,1,0:T(8,128)S(1)} %fusion.12), channel_id=1, source_target_pairs={{0,31},{1,2},{2,1},{3,4},{4,3},{5,6},{6,5},{7,8},{8,7},{9,10},{10,... | collective-permute-start | bytes 393224 | tf_op jit(solution)/shard_map/ppermute | solution.py:213
  60.2 19.2 %collective-permute-start.2 = (f32[4,18,2,8,128]{4,3,2,1,0:T(8,128)S(1)}, f32[4,18,2,8,128]{4,3,2,1,0:T(8,128)S(1)}, u32[]{:S(2)}, u32[]{:S(2)}) collective-permute-start(f32[4,18,2,8,128]{4,3,2,1,0:T(8,128)S(1)} %heun_a0.1.refs_0_), channel_id=1, source_target_pairs={{0,31},{1,2},{2,1},{3,4},{4,3},{5,6},{6,5},{7,8},{8,7},{9,10},{10,... | collective-permute-start | bytes 1769480 | tf_op jit(solution)/shard_map/ppermute | solution.py:213
  62.9 16.6 %collective-permute-start.3 = (f32[4,18,2,8,128]{4,3,2,1,0:T(8,128)S(1)}, f32[4,18,2,8,128]{4,3,2,1,0:T(8,128)S(1)}, u32[]{:S(2)}, u32[]{:S(2)}) collective-permute-start(f32[4,18,2,8,128]{4,3,2,1,0:T(8,128)S(1)} %heun_a0.1.refs_0_), channel_id=1, source_target_pairs={{0,1},{1,0},{2,3},{3,2},{4,5},{5,4},{6,7},{7,6},{8,9},{9,8},{10,11... | collective-permute-start | bytes 1769480 | tf_op jit(solution)/shard_map/ppermute | solution.py:208
  68.1 11.3 %collective-permute-start.10 = (f32[4,14,2,8,128]{4,3,2,1,0:T(8,128)S(1)}, f32[4,14,2,8,128]{4,3,2,1,0:T(8,128)S(1)}, u32[]{:S(2)}, u32[]{:S(2)}) collective-permute-start(f32[4,14,2,8,128]{4,3,2,1,0:T(8,128)S(1)} %heun_b0.1.refs_3_), channel_id=1, source_target_pairs={{0,31},{1,2},{2,1},{3,4},{4,3},{5,6},{6,5},{7,8},{8,7},{9,10},{10,... | collective-permute-start | bytes 1376264 | tf_op jit(solution)/shard_map/ppermute | solution.py:213
  70.7 8.7 %collective-permute-start.11 = (f32[4,14,2,8,128]{4,3,2,1,0:T(8,128)S(1)}, f32[4,14,2,8,128]{4,3,2,1,0:T(8,128)S(1)}, u32[]{:S(2)}, u32[]{:S(2)}) collective-permute-start(f32[4,14,2,8,128]{4,3,2,1,0:T(8,128)S(1)} %heun_b0.1.refs_3_), channel_id=1, source_target_pairs={{0,1},{1,0},{2,3},{3,2},{4,5},{5,4},{6,7},{7,6},{8,9},{9,8},{10,11... | collective-permute-start | bytes 1376264 | tf_op jit(solution)/shard_map/ppermute | solution.py:208
  71.5 47.9 %collective-permute-start.23 = (f32[2,16,8,128]{3,2,1,0:T(8,128)S(1)}, f32[2,16,8,128]{3,2,1,0:T(8,128)S(1)}, u32[]{:S(2)}, u32[]{:S(2)}) collective-permute-start(f32[2,16,8,128]{3,2,1,0:T(8,128)S(1)} %fusion.29), channel_id=1, source_target_pairs={{0,31},{1,2},{2,1},{3,4},{4,3},{5,6},{6,5},{7,8},{8,7},{9,10},{10,... | collective-permute-start | bytes 393224 | tf_op jit(solution)/shard_map/ppermute | solution.py:213
  85.7 17.6 %collective-permute-start.12 = (f32[4,18,2,8,128]{4,3,2,1,0:T(8,128)S(1)}, f32[4,18,2,8,128]{4,3,2,1,0:T(8,128)S(1)}, u32[]{:S(2)}, u32[]{:S(2)}) collective-permute-start(f32[4,18,2,8,128]{4,3,2,1,0:T(8,128)S(1)} %heun_b1.1.refs_3_), channel_id=1, source_target_pairs={{0,31},{1,2},{2,1},{3,4},{4,3},{5,6},{6,5},{7,8},{8,7},{9,10},{10,... | collective-permute-start | bytes 1769480 | tf_op jit(solution)/shard_map/ppermute | solution.py:213
  88.3 15.0 %collective-permute-start.13 = (f32[4,18,2,8,128]{4,3,2,1,0:T(8,128)S(1)}, f32[4,18,2,8,128]{4,3,2,1,0:T(8,128)S(1)}, u32[]{:S(2)}, u32[]{:S(2)}) collective-permute-start(f32[4,18,2,8,128]{4,3,2,1,0:T(8,128)S(1)} %heun_b1.1.refs_3_), channel_id=1, source_target_pairs={{0,1},{1,0},{2,3},{3,2},{4,5},{5,4},{6,7},{7,6},{8,9},{9,8},{10,11... | collective-permute-start | bytes 1769480 | tf_op jit(solution)/shard_map/ppermute | solution.py:208
  91.7 11.7 %collective-permute-start.4 = (f32[4,14,2,8,128]{4,3,2,1,0:T(8,128)S(1)}, f32[4,14,2,8,128]{4,3,2,1,0:T(8,128)S(1)}, u32[]{:S(2)}, u32[]{:S(2)}) collective-permute-start(f32[4,14,2,8,128]{4,3,2,1,0:T(8,128)S(1)} %heun_a1.1.refs_0_), channel_id=1, source_target_pairs={{0,31},{1,2},{2,1},{3,4},{4,3},{5,6},{6,5},{7,8},{8,7},{9,10},{10,... | collective-permute-start | bytes 1376264 | tf_op jit(solution)/shard_map/ppermute | solution.py:213
  94.3 9.0 %collective-permute-start.5 = (f32[4,14,2,8,128]{4,3,2,1,0:T(8,128)S(1)}, f32[4,14,2,8,128]{4,3,2,1,0:T(8,128)S(1)}, u32[]{:S(2)}, u32[]{:S(2)}) collective-permute-start(f32[4,14,2,8,128]{4,3,2,1,0:T(8,128)S(1)} %heun_a1.1.refs_0_), channel_id=1, source_target_pairs={{0,1},{1,0},{2,3},{3,2},{4,5},{5,4},{6,7},{7,6},{8,9},{9,8},{10,11... | collective-permute-start | bytes 1376264 | tf_op jit(solution)/shard_map/ppermute | solution.py:208
  103.3 16.1 %collective-permute-start.22 = (f32[2,16,8,128]{3,2,1,0:T(8,128)S(1)}, f32[2,16,8,128]{3,2,1,0:T(8,128)S(1)}, u32[]{:S(2)}, u32[]{:S(2)}) collective-permute-start(f32[2,16,8,128]{3,2,1,0:T(8,128)S(1)} %fusion.29), channel_id=1, source_target_pairs={{0,1},{1,0},{2,3},{3,2},{4,5},{5,4},{6,7},{7,6},{8,9},{9,8},{10,11... | collective-permute-start | bytes 393224 | tf_op jit(solution)/shard_map/ppermute | solution.py:208
  109.7 20.6 %collective-permute-start.14 = (f32[4,22,2,8,128]{4,3,2,1,0:T(8,128)S(1)}, f32[4,22,2,8,128]{4,3,2,1,0:T(8,128)S(1)}, u32[]{:S(2)}, u32[]{:S(2)}) collective-permute-start(f32[4,22,2,8,128]{4,3,2,1,0:T(8,128)S(1)} %heun_b2.1.refs_3_), channel_id=1, source_target_pairs={{0,31},{1,2},{2,1},{3,4},{4,3},{5,6},{6,5},{7,8},{8,7},{9,10},{10,... | collective-permute-start | bytes 2162696 | tf_op jit(solution)/shard_map/ppermute | solution.py:213
  112.3 18.1 %collective-permute-start.15 = (f32[4,22,2,8,128]{4,3,2,1,0:T(8,128)S(1)}, f32[4,22,2,8,128]{4,3,2,1,0:T(8,128)S(1)}, u32[]{:S(2)}, u32[]{:S(2)}) collective-permute-start(f32[4,22,2,8,128]{4,3,2,1,0:T(8,128)S(1)} %heun_b2.1.refs_3_), channel_id=1, source_target_pairs={{0,1},{1,0},{2,3},{3,2},{4,5},{5,4},{6,7},{7,6},{8,9},{9,8},{10,11... | collective-permute-start | bytes 2162696 | tf_op jit(solution)/shard_map/ppermute | solution.py:208
  116.8 10.6 %collective-permute-start.6 = (f32[4,10,2,8,128]{4,3,2,1,0:T(8,128)S(1)}, f32[4,10,2,8,128]{4,3,2,1,0:T(8,128)S(1)}, u32[]{:S(2)}, u32[]{:S(2)}) collective-permute-start(f32[4,10,2,8,128]{4,3,2,1,0:T(8,128)S(1)} %heun_a2.1.refs_0_), channel_id=1, source_target_pairs={{0,31},{1,2},{2,1},{3,4},{4,3},{5,6},{6,5},{7,8},{8,7},{9,10},{10,... | collective-permute-start | bytes 983048 | tf_op jit(solution)/shard_map/ppermute | solution.py:213
  119.4 8.0 %collective-permute-start.7 = (f32[4,10,2,8,128]{4,3,2,1,0:T(8,128)S(1)}, f32[4,10,2,8,128]{4,3,2,1,0:T(8,128)S(1)}, u32[]{:S(2)}, u32[]{:S(2)}) collective-permute-start(f32[4,10,2,8,128]{4,3,2,1,0:T(8,128)S(1)} %heun_a2.1.refs_0_), channel_id=1, source_target_pairs={{0,1},{1,0},{2,3},{3,2},{4,5},{5,4},{6,7},{7,6},{8,9},{9,8},{10,11... | collective-permute-start | bytes 983048 | tf_op jit(solution)/shard_map/ppermute | solution.py:208
  161.2 7.8 %collective-permute-start.27 = (f32[2,16,8,128]{3,2,1,0:T(8,128)S(1)}, f32[2,16,8,128]{3,2,1,0:T(8,128)S(1)}, u32[]{:S(2)}, u32[]{:S(2)}) collective-permute-start(f32[2,16,8,128]{3,2,1,0:T(8,128)S(1)} %fusion.42), channel_id=1, source_target_pairs={{0,31},{1,2},{2,1},{3,4},{4,3},{5,6},{6,5},{7,8},{8,7},{9,10},{10,... | collective-permute-start | bytes 393224 | tf_op jit(solution)/shard_map/ppermute | solution.py:213
  177.3 7.8 %collective-permute-start.31 = (f32[2,16,8,128]{3,2,1,0:T(8,128)S(1)}, f32[2,16,8,128]{3,2,1,0:T(8,128)S(1)}, u32[]{:S(2)}, u32[]{:S(2)}) collective-permute-start(f32[2,16,8,128]{3,2,1,0:T(8,128)S(1)} %fusion.56), channel_id=1, source_target_pairs={{0,31},{1,2},{2,1},{3,4},{4,3},{5,6},{6,5},{7,8},{8,7},{9,10},{10,... | collective-permute-start | bytes 393224 | tf_op jit(solution)/shard_map/ppermute | solution.py:213
  (42 other events, 375.4 us)

commit v2 on v1

v2 whole, which is shorter than its diff:
```python
import functools

import jax
import jax.numpy as jnp
from jax import lax
from jax.experimental import pallas as pl
from jax.experimental.pallas import tpu as pltpu
from jax.sharding import PartitionSpec as P

FSTEPS = 4
CSTEPS = 2
DU = 0.16
DV = 0.08
FIRST = 22
TILES = 32
F32 = jnp.float32
UNROLL = 4
HIGH = lax.Precision.HIGHEST
VMEM_LIMIT = 40 * 1024 * 1024


def splitter(transposed):
    r = lax.broadcasted_iota(jnp.int32, (256, 256), 0)
    c = lax.broadcasted_iota(jnp.int32, (256, 256), 1)
    if transposed:
        r, c = c, r
    return jnp.where(r == 2 * (c % 128) + c // 128, 1.0, 0.0).astype(F32)


def prep_kernel(parity, x, feed, kill, pair_a, pair_b, cross_a, cross_b, rows):
    mat = splitter(False)
    flip = parity[0]

    def scatter(plane, targets):
        done = jnp.dot(plane, mat, precision=HIGH, preferred_element_type=F32)
        rows[0] = done[:, :128]
        rows[1] = done[:, 128:]
        for i in range(TILES):
            for h in range(2):
                tile = rows[h, pl.ds(i, 8, stride=32), :]
                for (a, b), q in targets:
                    if i < FIRST:
                        a[q, i, h] = tile
                    else:
                        b[q, i - FIRST, h] = tile

    pair, cross = (pair_a, pair_b), (cross_a, cross_b)
    for sp in range(2):
        for q in range(2):
            scatter(x[sp, q ^ flip], [(pair, 2 * sp + q), (cross, 2 * sp + q)])
    for q, target in ((0, cross), (1, pair)):
        f = feed[q ^ flip]
        scatter(f, [(target, 4)])
        scatter(0.52 - (f + kill[q ^ flip]), [(target, 5)])


def prep(parity, x, feed, kill):
    a = jax.ShapeDtypeStruct((6, FIRST, 2, 8, 128), F32)
    b = jax.ShapeDtypeStruct((6, TILES - FIRST, 2, 8, 128), F32)
    vm = pl.BlockSpec(memory_space=pltpu.VMEM)
    return pl.pallas_call(
        prep_kernel,
        out_shape=[a, b, a, b],
        in_specs=[pl.BlockSpec(memory_space=pltpu.SMEM), vm, vm, vm],
        out_specs=[vm] * 4,
        scratch_shapes=[pltpu.VMEM((2, 256, 128), F32)],
        compiler_params=pltpu.CompilerParams(vmem_limit_bytes=VMEM_LIMIT),
        name="prep",
    )(parity, x, feed, kill)


LINE = ((1, 1), (1, 0), (0, 0), (0, 1), (2, 1), (2, 0))


def runs(lo, hi, key):
    out = []
    for v in range(lo, hi):
        k = key(v)
        if out and out[-1][2] == k:
            out[-1][1] = v + 1
        else:
            out.append([v, v + 1, k])
    return out


def over(lo, hi, key, work):
    for start, stop, k in runs(lo, hi, key):
        if stop - start < 4:
            for v in range(start, stop):
                work(v, k)
        else:
            @pl.loop(start, stop, unroll=min(UNROLL, stop - start))
            def _(v):
                work(v, k)


def moved(x, rolled):
    return pltpu.roll(x, 7, 0) if rolled else x


def beside(other, h):
    return other + pltpu.roll(other, 1 if h == 0 else 127, 1)


def heun_kernel(step, second, total, after, *refs):
    refs = list(refs)
    groups = 2 if second else 1
    state = [refs[3 * g:3 * g + 3] for g in range(groups)]
    rate = [refs[3 * groups + 4 * g:3 * groups + 4 * g + 4] for g in range(groups)]
    out, mids = refs[-2:]
    lo = FIRST - 2 * step - 4 if second else 2 * step
    hi = lo + total

    def find_state(v):
        if not second:
            return 0, -2 * step, False
        if v < FIRST - 2 * step:
            return 0, -2 * step, False
        if v < TILES + 2 * step:
            return 1, 2 * step - FIRST, False
        return 0, -TILES - 2 * step, True

    def find_rate(v):
        if v < FIRST:
            return 0, 0, False
        if v < TILES:
            return 1, -FIRST, False
        return 0, -TILES, True

    def cell(sp, p, v, h, at):
        g, off, rolled = at
        source, plane = LINE[p]
        return moved(state[g][source][2 * sp + plane, v + off, h], rolled)

    def coef(k, place, v, h, at):
        g, off, rolled = at
        return moved(rate[g][(2, 0, 1, 3)[place]][4 + k, v + off, h], rolled)

    def ahead(u, v, near_u, near_v, f, cv):
        uvv = u * v * v
        return DU * near_u + (1.0 - 6.0 * DU) * u + f * (1.0 - u) - uvv, DV * near_v + cv * v + uvv

    def first(v, key):
        below, here, above, at = key
        c = [[cell(sp, p, v, h, here) for h in range(2)] for sp in range(2) for p in range(6)]
        for p in range(1, 5):
            for h in range(2):
                near = []
                for sp in range(2):
                    i = 6 * sp + p
                    s = cell(sp, p, v - 1, h, below) + cell(sp, p, v + 1, h, above)
                    near.append(beside(c[i][1 - h], h) + (s + (c[i - 1][h] + c[i + 1][h])))
                nu, nv = ahead(c[p][h], c[6 + p][h], *near, coef(0, p - 1, v, h, at), coef(1, p - 1, v, h, at))
                mids[0, p - 1, v - lo, h] = nu
                mids[1, p - 1, v - lo, h] = nv

    def then(v, key):
        here, at = key
        c = [[mids[sp, p, v - lo, h] for h in range(2)] for sp in range(2) for p in range(4)]
        for p in range(1, 3):
            for h in range(2):
                near = []
                for sp in range(2):
                    i = 4 * sp + p
                    s = mids[sp, p, v - lo - 1, h] + mids[sp, p, v - lo + 1, h]
                    near.append(beside(c[i][1 - h], h) + (s + (c[i - 1][h] + c[i + 1][h])))
                nu, nv = ahead(c[p][h], c[4 + p][h], *near, coef(0, p, v, h, at), coef(1, p, v, h, at))
                out[p - 1, v - lo - 2, h] = 0.5 * (cell(0, p + 1, v, h, here) + nu)
                out[2 + p - 1, v - lo - 2, h] = 0.5 * (cell(1, p + 1, v, h, here) + nv)

    over(lo + 1, hi - 1, lambda v: (find_state(v - 1), find_state(v), find_state(v + 1), find_rate(v)), first)
    over(lo + 2, hi - 2, lambda v: (find_state(v), find_rate(v)), then)


VM = pl.BlockSpec(memory_space=pltpu.VMEM)
SM = pl.BlockSpec(memory_space=pltpu.SMEM)
ANY = pl.BlockSpec(memory_space=pl.ANY)
PARAMS = pltpu.CompilerParams(vmem_limit_bytes=VMEM_LIMIT)
COARSE = (2, 16, 8, 128)


def heun(step, second, state, rate, after):
    total = (TILES - FIRST + 4 * step + 8) if second else FIRST - 4 * step
    ins = [r for g in state for r in g] + [r for g in rate for r in g]
    return pl.pallas_call(
        functools.partial(heun_kernel, step, second, total),
        out_shape=jax.ShapeDtypeStruct((4, total - 4, 2, 8, 128), F32),
        in_specs=[ANY] + [VM] * len(ins),
        out_specs=VM,
        scratch_shapes=[pltpu.VMEM((2, 4, total, 2, 8, 128), F32)],
        compiler_params=PARAMS,
        cost_estimate=pl.CostEstimate(flops=total * 2048 * 150, bytes_accessed=total * 8192 * 20, transcendentals=0),
        name="heun_b%d" % step if second else "heun_a%d" % step,
    )(after, *ins)


def mean_tile(tiles):
    s = [tiles[i] + tiles[i + 1] for i in range(0, 8, 2)]
    return 0.125 * ((s[0] + s[1]) + (s[2] + s[3]))


def mean_of(a, b, j, rows):
    ref, off = (a, 0) if 2 * j < FIRST else (b, FIRST)
    return mean_tile([ref[q, 2 * j + i - off, h] for q in rows for i in range(2) for h in range(2)])


def euler(get, cf, ccv, j):
    new = []
    for sp in range(2):
        c = get(0, sp, j)
        up = get(0, sp, j + 1) if j < 15 else pltpu.roll(get(0, sp, 0), 7, 0)
        down = get(0, sp, j - 1) if j else pltpu.roll(get(0, sp, 15), 1, 0)
        s = pltpu.roll(c, 1, 1) + pltpu.roll(c, 127, 1) + (up + down)
        new.append((c, s + (get(-1, sp, j) + get(1, sp, j))))
    (u, su), (v, sv) = new
    uvv = u * v * v
    nu = u + 2.0 * (0.25 * DU * (su - 6.0 * u) - uvv + cf * (1.0 - u))
    nv = v + 2.0 * (0.25 * DV * (sv - 6.0 * v) + uvv - ccv * v)
    return nu, nv


def own_first_kernel(pa, pb, ca, cb, gpa, gpb, gca, gcb, out, line):
    for j in range(16):
        for sp in range(2):
            rows = (2 * sp, 2 * sp + 1)
            line[0, sp, j] = mean_of(gca, gcb, j, rows)
            line[1, sp, j] = mean_of(pa, pb, j, rows)
            line[2, sp, j] = mean_of(gpa, gpb, j, rows)
        for k in range(2):
            (x, off), (y, _) = ((pa, 0), (ca, 0)) if 2 * j < FIRST else ((pb, FIRST), (cb, FIRST))
            tiles = [r[4 + k, 2 * j + i - off, h] for r in (y, x) for i in range(2) for h in range(2)]
            m = mean_tile(tiles)
            out[2 + k, j] = m if k == 0 else 0.52 - m
    for j in range(16):
        out[0, j], out[1, j] = euler(lambda d, sp, i: line[1 + d, sp, i], out[2, j], out[3, j], j)


def own_first(*refs):
    return pl.pallas_call(
        own_first_kernel,
        out_shape=jax.ShapeDtypeStruct((4, 16, 8, 128), F32),
        in_specs=[VM] * 8,
        out_specs=VM,
        scratch_shapes=[pltpu.VMEM((3,) + COARSE, F32)],
        compiler_params=PARAMS,
        name="own_first",
    )(*refs)


def jump_kernel(slot, a, b, here, cross, pair, end, send):
    line = (cross, here, pair)
    for j in range(16):
        g = euler(lambda d, sp, i: line[1 + d][sp, i], here[2, j], here[3, j], j)
        for sp in range(2):
            tiles = []
            for q in range(2):
                for i in range(2):
                    for h in range(2):
                        v = 2 * j + i
                        if v < 2 * FSTEPS:
                            x = pltpu.roll(b[2 * sp + q, v + TILES - FIRST + 2 * FSTEPS, h], 1, 0)
                        elif v < FIRST - 2 * FSTEPS:
                            x = a[2 * sp + q, v - 2 * FSTEPS, h]
                        else:
                            x = b[2 * sp + q, v - FIRST + 2 * FSTEPS, h]
                        tiles.append(x)
            m = mean_tile(tiles)
            end[sp, j] = m
            jump = m - g[sp]
            send[sp, j] = jnp.where(slot[0] == 0, g[sp] + jump, jump)


def jump_of(slot, a, b, here, cross, pair):
    shape = jax.ShapeDtypeStruct(COARSE, F32)
    return pl.pallas_call(
        jump_kernel,
        out_shape=[shape, shape],
        in_specs=[SM] + [VM] * 5,
        out_specs=[VM, VM],
        compiler_params=PARAMS,
        name="jump",
    )(slot, a, b, here, cross, pair)


def walk_kernel(both, near, far, q_own, q_cross, q_pair, q_far, jumps, out, mid):
    line = ((near, 1), (near, 0), (both, 0), (both, 1), (far, 0), (far, 1))
    rates = (q_cross, q_own, q_pair, q_far)
    for p in range(1, 5):
        for j in range(16):
            q = rates[p - 1]
            new = euler(lambda d, sp, i: line[p + d][0][line[p + d][1], sp, i], q[2, j], q[3, j], j)
            mid[p - 1, 0, j], mid[p - 1, 1, j] = new
    for p in range(1, 3):
        for j in range(16):
            q = rates[p]
            new = euler(lambda d, sp, i: mid[p + d, sp, i], q[2, j], q[3, j], j)
            for sp in range(2):
                out[p - 1, sp, j] = new[sp] + jumps[p - 1, sp, j]


def walk(*refs):
    return pl.pallas_call(
        walk_kernel,
        out_shape=jax.ShapeDtypeStruct((2,) + COARSE, F32),
        in_specs=[VM] * 8,
        out_specs=VM,
        scratch_shapes=[pltpu.VMEM((4,) + COARSE, F32)],
        compiler_params=PARAMS,
        name="walk",
    )(*refs)


def finish_kernel(parity, a, b, end, chained, out, rows):
    mat = splitter(True)
    flip = parity[0]
    for sp in range(2):
        shift = [chained[0, sp, j] - end[sp, j] for j in range(16)]
        for q in range(2):
            for v in range(TILES):
                for h in range(2):
                    if v < 2 * FSTEPS:
                        x = pltpu.roll(b[2 * sp + q, v + TILES - FIRST + 2 * FSTEPS, h], 1, 0)
                    elif v < FIRST - 2 * FSTEPS:
                        x = a[2 * sp + q, v - 2 * FSTEPS, h]
                    else:
                        x = b[2 * sp + q, v - FIRST + 2 * FSTEPS, h]
                    rows[h, pl.ds(v, 8, stride=32), :] = x + shift[v // 2]
            both = jnp.concatenate([rows[0], rows[1]], axis=1)
            out[sp, q ^ flip] = jnp.dot(both, mat, precision=HIGH, preferred_element_type=F32)


def finish(parity, a, b, end, chained):
    return pl.pallas_call(
        finish_kernel,
        out_shape=jax.ShapeDtypeStruct((2, 2, 256, 256), F32),
        in_specs=[SM] + [VM] * 4,
        out_specs=VM,
        scratch_shapes=[pltpu.VMEM((2, 256, 128), F32)],
        compiler_params=PARAMS,
        name="finish",
    )(parity, a, b, end, chained)


def swap_pair(x):
    n = lax.axis_size("space")
    return lax.ppermute(x, "space", [(i, i ^ 1) for i in range(n)])


def swap_cross(x):
    n = lax.axis_size("space")
    return lax.ppermute(x, "space", [(i, (i + 1) % n if i % 2 else (i - 1) % n) for i in range(n)])


def later(x, distance):
    n = lax.axis_size("tm")
    return lax.ppermute(x, "tm", [(i, i + distance) for i in range(n - distance)])


def body(slice_starts, feed, kill):
    start = slice_starts[0]
    parity = (lax.axis_index("space") % 2).astype(jnp.int32).reshape(1)
    index = lax.axis_index("tm").astype(jnp.int32)
    pair_a, pair_b, cross_a, cross_b = prep(parity, start, feed, kill)
    got_pair_a, got_cross_a = swap_pair(pair_a), swap_cross(cross_a)
    got_pair_b, got_cross_b = swap_pair(pair_b), swap_cross(cross_b)
    rate_a = (cross_a, pair_a, got_cross_a, got_pair_a)
    rate_b = (cross_b, pair_b, got_cross_b, got_pair_b)
    state_a = (pair_a, got_cross_a, got_pair_a)
    state_b = (pair_b, got_cross_b, got_pair_b)
    new_b = parity
    for step in range(FSTEPS):
        new_a = heun(step, False, [state_a], [rate_a], new_b)
        last = step == FSTEPS - 1
        if not last:
            next_a = (new_a, swap_cross(new_a), swap_pair(new_a))
        new_b = heun(step, True, [state_a, state_b], [rate_a, rate_b], new_a)
        if not last:
            state_a = next_a
            state_b = (new_b, swap_cross(new_b), swap_pair(new_b))
        if step == 0:
            q_own = own_first(pair_a, pair_b, cross_a, cross_b, got_pair_a, got_pair_b, got_cross_a, got_cross_b)
            q_cross = swap_cross(q_own)
            q_pair, q_far = swap_pair(q_own), swap_pair(q_cross)
    end, send = jump_of(index.reshape(1), new_a, new_b, q_own, q_cross, q_pair)
    from3, from2, from1 = later(send, 3), later(send, 2), later(send, 1)
    pick = lambda *xs: lax.select_n(index, *xs)
    first = pick(send, from1, from2, from3)
    jumps = jnp.stack([pick(send, send, from1, from2), pick(send, send, send, from1)])
    other_jumps = swap_pair(jumps)
    both = jnp.stack([first, swap_pair(first)])
    chained = [both]
    for position in range(lax.axis_size("tm") - 1):
        near = swap_cross(both)
        far = swap_pair(near)
        if position < 2:
            jump = jnp.stack([jumps[position], other_jumps[position]])
        else:
            jump = jnp.stack([send, send])
        both = walk(both, near, far, q_own, q_cross, q_pair, q_far, jump)
        chained.append(both)
    return finish(parity, new_a, new_b, end, pick(*chained))[None]


def solution(mesh):
    in_specs = (P("tm", None, "space", None, None), P("space", None, None), P("space", None, None))
    out_specs = P("tm", None, "space", None, None)
    return jax.shard_map(body, mesh=mesh, in_specs=in_specs, out_specs=out_specs, check_vma=False)
```

time: 205 us -> 153 us (0.75)
  the two profiles are of different devices: /device:TPU:0 before, /device:TPU:7 now
where the time goes in v2:
time: 153 us; the launch traced here: 152 us
  starting transfers between devices  67.3 us (44%)
  waiting for transfers between devices  49.1 us (32%)
  Pallas kernels  26.9 us (18%)
  local copies, waits for them, and re-layouts  8.31 us (5%)
    ppermute x15, starting transfers between devices, swap_pair(): return lax.ppermute(x, 'space', [(i, i ^ 1) for i in range(n)])  57.4 us
    ppermute x12, waiting for transfers between devices, swap_cross(): lax.ppermute(x, 'space', [(i, (i + 1) % n if i % 2 else (i - 1) % n) for...  36.3 us
    pallas_call x8, Pallas kernels, heun(): pl.pallas_call(functools.partial(heun_kernel, step, second, total), out_s...  14.7 us
    ppermute x3, waiting for transfers between devices, later(): lax.ppermute(x, 'tm', [(i, i + distance) for i in range(n - distance)])  8.41 us
    unnamed x38, local copies, waits for them, and re-layouts  8.29 us
    ppermute x12, starting transfers between devices, swap_cross(): lax.ppermute(x, 'space', [(i, (i + 1) % n if i % 2 else (i - 1) % n) for...  6.06 us
    pallas_call x3, Pallas kernels, walk(): pl.pallas_call(walk_kernel, out_shape=jax.ShapeDtypeStruct((2,) + COARSE,...  4.72 us
    ppermute x15, waiting for transfers between devices, swap_pair(): return lax.ppermute(x, 'space', [(i, i ^ 1) for i in range(n)])  4.4 us
  transfers between devices with their start and end apart: 30, of which 14 were waited for; matrix products, arithmetic and copies ran while one was open for 0% of the time, Pallas kernels for 7%

profile of v2, /device:TPU:7, one launch (start us, length us, event | category | flops | bytes accessed | tf_op | source)
XLA Modules:
  0.0 152.2 jit_solution(7931688349556456925)
XLA Ops:
  3.3 3.4 %prep.1 = (f32[6,22,2,8,128]{4,3,2,1,0:T(8,128)S(1)}, f32[6,10,2,8,128]{4,3,2,1,0:T(8,128)S(1)}, f32[6,22,2,8,128]{4,3,2,1,0:T(8,128)S(1)}, f32[6,10,2,8,128]{4,3,2,1,0:T(8,128)S(1)}) custom-call(s32[1]{0:T(128)} %bitcast.parity.after, f32[2,2,256,256]{3,2,1,0:T(8,128)S(1)} %bitcast.11, f32[2,256,256]{2,1,0:T(8,128)S(1)} %copy-done.17, ...), custom_call_target="tpu_custom_call" | custom-call | tf_op jit(solution)/shard_map/prep/pallas_call | solution.py:61
  6.7 2.3 %collective-permute-start = (f32[6,22,2,8,128]{4,3,2,1,0:T(8,128)S(1)}, f32[6,22,2,8,128]{4,3,2,1,0:T(8,128)S(1)}, u32[]{:S(2)}, u32[]{:S(2)}) collective-permute-start(f32[6,22,2,8,128]{4,3,2,1,0:T(8,128)S(1)} %get-tuple-element.12.refs_3_.refs_6_.ca), channel_id=1, source_target_pairs={{0,31},{1,2},{2,1},{3,4},{4,3},{5,6},{6,5},{7,8},{8,7},{9,10},{10,... | collective-permute-start | bytes 3244040 | tf_op jit(solution)/shard_map/ppermute | solution.py:351
  9.0 4.4 %collective-permute-start.1 = (f32[6,22,2,8,128]{4,3,2,1,0:T(8,128)S(1)}, f32[6,22,2,8,128]{4,3,2,1,0:T(8,128)S(1)}, u32[]{:S(2)}, u32[]{:S(2)}) collective-permute-start(f32[6,22,2,8,128]{4,3,2,1,0:T(8,128)S(1)} %get-tuple-element.11.refs_0_.refs_4_.refs_7_.pa), channel_id=1, source_target_pairs={{0,1},{1,0},{2,3},{3,2},{4,5},{5,4},{6,7},{7,6},{8,9},{9,8},{10,11... | collective-permute-start | bytes 3244040 | tf_op jit(solution)/shard_map/ppermute | solution.py:346
  14.2 8.0 %collective-permute-done.refs_1_.refs_5_.refs_8_.gca = f32[6,22,2,8,128]{4,3,2,1,0:T(8,128)S(1)} collective-permute-done((f32[6,22,2,8,128]{4,3,2,1,0:T(8,128)S(1)}, f32[6,22,2,8,128]{4,3,2,1,0:T(8,128)S(1)}, u32[]{:S(2)}, u32[]{:S(2)}) %collective-permute-start) | collective-permute-done | bytes 1081376 | tf_op jit(solution)/shard_map/ppermute | solution.py:351
  25.0 7.7 %collective-permute-start.5 = (f32[4,18,2,8,128]{4,3,2,1,0:T(8,128)S(1)}, f32[4,18,2,8,128]{4,3,2,1,0:T(8,128)S(1)}, u32[]{:S(2)}, u32[]{:S(2)}) collective-permute-start(f32[4,18,2,8,128]{4,3,2,1,0:T(8,128)S(1)} %heun_a0.1.after.refs_0_), channel_id=1, source_target_pairs={{0,1},{1,0},{2,3},{3,2},{4,5},{5,4},{6,7},{7,6},{8,9},{9,8},{10,11... | collective-permute-start | bytes 1769480 | tf_op jit(solution)/shard_map/ppermute | solution.py:346
  34.0 3.8 %collective-permute-start.7 = (f32[4,14,2,8,128]{4,3,2,1,0:T(8,128)S(1)}, f32[4,14,2,8,128]{4,3,2,1,0:T(8,128)S(1)}, u32[]{:S(2)}, u32[]{:S(2)}) collective-permute-start(f32[4,14,2,8,128]{4,3,2,1,0:T(8,128)S(1)} %heun_b0.1.after.refs_3_), channel_id=1, source_target_pairs={{0,1},{1,0},{2,3},{3,2},{4,5},{5,4},{6,7},{7,6},{8,9},{9,8},{10,11... | collective-permute-start | bytes 1376264 | tf_op jit(solution)/shard_map/ppermute | solution.py:346
  39.0 3.2 %collective-permute-done.6.refs_4_ = f32[4,14,2,8,128]{4,3,2,1,0:T(8,128)S(1)} collective-permute-done((f32[4,14,2,8,128]{4,3,2,1,0:T(8,128)S(1)}, f32[4,14,2,8,128]{4,3,2,1,0:T(8,128)S(1)}, u32[]{:S(2)}, u32[]{:S(2)}) %collective-permute-start.6) | collective-permute-done | bytes 458784 | tf_op jit(solution)/shard_map/ppermute | solution.py:351
  43.7 8.1 %collective-permute-start.11 = (f32[4,18,2,8,128]{4,3,2,1,0:T(8,128)S(1)}, f32[4,18,2,8,128]{4,3,2,1,0:T(8,128)S(1)}, u32[]{:S(2)}, u32[]{:S(2)}) collective-permute-start(f32[4,18,2,8,128]{4,3,2,1,0:T(8,128)S(1)} %heun_b1.1.after.refs_3_), channel_id=1, source_target_pairs={{0,1},{1,0},{2,3},{3,2},{4,5},{5,4},{6,7},{7,6},{8,9},{9,8},{10,11... | collective-permute-start | bytes 1769480 | tf_op jit(solution)/shard_map/ppermute | solution.py:346
  52.0 8.0 %collective-permute-done.8.refs_1_ = f32[4,14,2,8,128]{4,3,2,1,0:T(8,128)S(1)} collective-permute-done((f32[4,14,2,8,128]{4,3,2,1,0:T(8,128)S(1)}, f32[4,14,2,8,128]{4,3,2,1,0:T(8,128)S(1)}, u32[]{:S(2)}, u32[]{:S(2)}) %collective-permute-start.8) | collective-permute-done | bytes 458784 | tf_op jit(solution)/shard_map/ppermute | solution.py:351
  61.6 2.4 %heun_b2.1.after.refs_3_ = f32[4,22,2,8,128]{4,3,2,1,0:T(8,128)} custom-call(f32[4,10,2,8,128]{4,3,2,1,0:T(8,128)} %heun_a2.1.after.refs_0_, f32[4,14,2,8,128]{4,3,2,1,0:T(8,128)S(1)} %heun_a1.1.after.refs_0_, f32[4,14,2,8,128]{4,3,2,1,0:T(8,128)S(1)} %collective-permute-done.8.refs_1_, f32[4,14,2,8,128]{4,3,2,1,0:T(8,128)S(1)} %collective-permute-done.9.refs_2_, ...), custom_call_target="tpu_custom_call" | custom-call | flops 7987200 | bytes 4259840 | tf_op jit(solution)/shard_map/heun_b2/pallas_call | solution.py:185
  64.1 9.3 %collective-permute-start.15 = (f32[4,22,2,8,128]{4,3,2,1,0:T(8,128)}, f32[4,22,2,8,128]{4,3,2,1,0:T(8,128)}, u32[]{:S(2)}, u32[]{:S(2)}) collective-permute-start(f32[4,22,2,8,128]{4,3,2,1,0:T(8,128)} %heun_b2.1.after.refs_3_), channel_id=1, source_target_pairs={{0,1},{1,0},{2,3},{3,2},{4,5},{5,4},{6,7},{7,6},{8,9},{9,8},{10,11... | collective-permute-start | bytes 2162696 | tf_op jit(solution)/shard_map/ppermute | solution.py:346
  75.5 5.0 %collective-permute-done.12.refs_1_ = f32[4,10,2,8,128]{4,3,2,1,0:T(8,128)S(1)} collective-permute-done((f32[4,10,2,8,128]{4,3,2,1,0:T(8,128)}, f32[4,10,2,8,128]{4,3,2,1,0:T(8,128)S(1)}, u32[]{:S(2)}, u32[]{:S(2)}) %collective-permute-start.12) | collective-permute-done | bytes 327712 | tf_op jit(solution)/shard_map/ppermute | solution.py:351
  81.3 5.6 %collective-permute-start.17 = (f32[4,16,8,128]{3,2,1,0:T(8,128)S(1)}, f32[4,16,8,128]{3,2,1,0:T(8,128)}, u32[]{:S(2)}, u32[]{:S(2)}) collective-permute-start(f32[4,16,8,128]{3,2,1,0:T(8,128)S(1)} %own_first.1.here.q_own), channel_id=1, source_target_pairs={{0,1},{1,0},{2,3},{3,2},{4,5},{5,4},{6,7},{7,6},{8,9},{9,8},{10,11... | collective-permute-start | bytes 786440 | tf_op jit(solution)/shard_map/ppermute | solution.py:346
  90.9 3.8 %heun_b3.1.b = f32[4,26,2,8,128]{4,3,2,1,0:T(8,128)S(1)} custom-call(f32[4,6,2,8,128]{4,3,2,1,0:T(8,128)S(1)} %heun_a3.1.after.a, f32[4,10,2,8,128]{4,3,2,1,0:T(8,128)} %heun_a2.1.after.refs_0_, f32[4,10,2,8,128]{4,3,2,1,0:T(8,128)S(1)} %copy-done.15, f32[4,10,2,8,128]{4,3,2,1,0:T(8,128)} %collective-permute-done.13.refs_2_, ...), custom_call_target="tpu_custom_call" | custom-call | flops 9216000 | bytes 4915200 | tf_op jit(solution)/shard_map/heun_b3/pallas_call | solution.py:185
  100.7 3.1 %collective-permute-done.18 = f32[2,16,8,128]{3,2,1,0:T(8,128)S(1)} collective-permute-done((f32[2,16,8,128]{3,2,1,0:T(8,128)S(1)}, f32[2,16,8,128]{3,2,1,0:T(8,128)S(1)}, u32[]{:S(2)}, u32[]{:S(2)}) %collective-permute-start.18) | collective-permute-done | bytes 131104 | tf_op jit(solution)/shard_map/ppermute | solution.py:356
  103.8 2.8 %collective-permute-done.19 = f32[2,16,8,128]{3,2,1,0:T(8,128)S(1)} collective-permute-done((f32[2,16,8,128]{3,2,1,0:T(8,128)S(1)}, f32[2,16,8,128]{3,2,1,0:T(8,128)S(1)}, u32[]{:S(2)}, u32[]{:S(2)}) %collective-permute-start.19) | collective-permute-done | bytes 131104 | tf_op jit(solution)/shard_map/ppermute | solution.py:356
  106.6 2.5 %collective-permute-done.20 = f32[2,16,8,128]{3,2,1,0:T(8,128)S(1)} collective-permute-done((f32[2,16,8,128]{3,2,1,0:T(8,128)S(1)}, f32[2,16,8,128]{3,2,1,0:T(8,128)S(1)}, u32[]{:S(2)}, u32[]{:S(2)}) %collective-permute-start.20) | collective-permute-done | bytes 131104 | tf_op jit(solution)/shard_map/ppermute | solution.py:356
  111.5 5.1 %collective-permute-start.25 = (f32[2,2,16,8,128]{4,3,2,1,0:T(8,128)S(1)}, f32[2,2,16,8,128]{4,3,2,1,0:T(8,128)S(1)}, u32[]{:S(2)}, u32[]{:S(2)}) collective-permute-start(f32[2,2,16,8,128]{4,3,2,1,0:T(8,128)S(1)} %pad_maximum_fusion), channel_id=1, source_target_pairs={{0,1},{1,0},{2,3},{3,2},{4,5},{5,4},{6,7},{7,6},{8,9},{9,8},{10,11... | collective-permute-start | bytes 786440 | tf_op jit(solution)/shard_map/ppermute | solution.py:346
  117.2 3.7 %collective-permute-start.23 = (f32[2,2,16,8,128]{4,3,2,1,0:T(8,128)S(1)}, f32[2,2,16,8,128]{4,3,2,1,0:T(8,128)S(1)}, u32[]{:S(2)}, u32[]{:S(2)}) collective-permute-start(f32[2,2,16,8,128]{4,3,2,1,0:T(8,128)S(1)} %collective-permute-done.22.near), channel_id=1, source_target_pairs={{0,1},{1,0},{2,3},{3,2},{4,5},{5,4},{6,7},{7,6},{8,9},{9,8},{10,11... | collective-permute-start | bytes 786440 | tf_op jit(solution)/shard_map/ppermute | solution.py:346
  123.8 5.8 %collective-permute-done.26.near = f32[2,2,16,8,128]{4,3,2,1,0:T(8,128)S(1)} collective-permute-done((f32[2,2,16,8,128]{4,3,2,1,0:T(8,128)S(1)}, f32[2,2,16,8,128]{4,3,2,1,0:T(8,128)S(1)}, u32[]{:S(2)}, u32[]{:S(2)}) %collective-permute-start.26) | collective-permute-done | bytes 262176 | tf_op jit(solution)/shard_map/ppermute | solution.py:351
  129.5 3.7 %collective-permute-start.27 = (f32[2,2,16,8,128]{4,3,2,1,0:T(8,128)S(1)}, f32[2,2,16,8,128]{4,3,2,1,0:T(8,128)S(1)}, u32[]{:S(2)}, u32[]{:S(2)}) collective-permute-start(f32[2,2,16,8,128]{4,3,2,1,0:T(8,128)S(1)} %collective-permute-done.26.near), channel_id=1, source_target_pairs={{0,1},{1,0},{2,3},{3,2},{4,5},{5,4},{6,7},{7,6},{8,9},{9,8},{10,11... | collective-permute-start | bytes 786440 | tf_op jit(solution)/shard_map/ppermute | solution.py:346
  136.1 5.8 %collective-permute-done.28.near = f32[2,2,16,8,128]{4,3,2,1,0:T(8,128)S(1)} collective-permute-done((f32[2,2,16,8,128]{4,3,2,1,0:T(8,128)S(1)}, f32[2,2,16,8,128]{4,3,2,1,0:T(8,128)S(1)}, u32[]{:S(2)}, u32[]{:S(2)}) %collective-permute-start.28) | collective-permute-done | bytes 262176 | tf_op jit(solution)/shard_map/ppermute | solution.py:351
  141.9 3.7 %collective-permute-start.29 = (f32[2,2,16,8,128]{4,3,2,1,0:T(8,128)S(1)}, f32[2,2,16,8,128]{4,3,2,1,0:T(8,128)S(1)}, u32[]{:S(2)}, u32[]{:S(2)}) collective-permute-start(f32[2,2,16,8,128]{4,3,2,1,0:T(8,128)S(1)} %collective-permute-done.28.near), channel_id=1, source_target_pairs={{0,1},{1,0},{2,3},{3,2},{4,5},{5,4},{6,7},{7,6},{8,9},{9,8},{10,11... | collective-permute-start | bytes 786440 | tf_op jit(solution)/shard_map/ppermute | solution.py:346
  149.5 2.7 %finish.1 = f32[2,2,256,256]{3,2,1,0:T(8,128)} custom-call(s32[1]{0:T(128)} %bitcast.parity.after, f32[4,6,2,8,128]{4,3,2,1,0:T(8,128)S(1)} %copy-done.13, f32[4,26,2,8,128]{4,3,2,1,0:T(8,128)S(1)} %copy-done.11, f32[2,16,8,128]{3,2,1,0:T(8,128)S(1)} %get-tuple-element.15.end, f32[2,2,16,8,128]{4,3,2,1,0:T(8,128)S(1)} %select_select_fusion.chained), custom_call_target="tpu_custom_call" | custom-call | tf_op jit(solution)/shard_map/finish/pallas_call | solution.py:333
  (97 shorter events, 38.0 us)
Async XLA Ops:
  6.7 15.4 %collective-permute-start = (f32[6,22,2,8,128]{4,3,2,1,0:T(8,128)S(1)}, f32[6,22,2,8,128]{4,3,2,1,0:T(8,128)S(1)}, u32[]{:S(2)}, u32[]{:S(2)}) collective-permute-start(f32[6,22,2,8,128]{4,3,2,1,0:T(8,128)S(1)} %get-tuple-element.12.refs_3_.refs_6_.ca), channel_id=1, source_target_pairs={{0,31},{1,2},{2,1},{3,4},{4,3},{5,6},{6,5},{7,8},{8,7},{9,10},{10,... | collective-permute-start | bytes 3244040 | tf_op jit(solution)/shard_map/ppermute | solution.py:351
  9.0 13.1 %collective-permute-start.1 = (f32[6,22,2,8,128]{4,3,2,1,0:T(8,128)S(1)}, f32[6,22,2,8,128]{4,3,2,1,0:T(8,128)S(1)}, u32[]{:S(2)}, u32[]{:S(2)}) collective-permute-start(f32[6,22,2,8,128]{4,3,2,1,0:T(8,128)S(1)} %get-tuple-element.11.refs_0_.refs_4_.refs_7_.pa), channel_id=1, source_target_pairs={{0,1},{1,0},{2,3},{3,2},{4,5},{5,4},{6,7},{7,6},{8,9},{9,8},{10,11... | collective-permute-start | bytes 3244040 | tf_op jit(solution)/shard_map/ppermute | solution.py:346
  13.4 19.3 %collective-permute-start.2 = (f32[6,10,2,8,128]{4,3,2,1,0:T(8,128)S(1)}, f32[6,10,2,8,128]{4,3,2,1,0:T(8,128)S(1)}, u32[]{:S(2)}, u32[]{:S(2)}) collective-permute-start(f32[6,10,2,8,128]{4,3,2,1,0:T(8,128)S(1)} %get-tuple-element.14.refs_10_.cb), channel_id=1, source_target_pairs={{0,31},{1,2},{2,1},{3,4},{4,3},{5,6},{6,5},{7,8},{8,7},{9,10},{10,... | collective-permute-start | bytes 1474568 | tf_op jit(solution)/shard_map/ppermute | solution.py:351
  13.4 19.3 %collective-permute-start.3 = (f32[6,10,2,8,128]{4,3,2,1,0:T(8,128)S(1)}, f32[6,10,2,8,128]{4,3,2,1,0:T(8,128)S(1)}, u32[]{:S(2)}, u32[]{:S(2)}) collective-permute-start(f32[6,10,2,8,128]{4,3,2,1,0:T(8,128)S(1)} %get-tuple-element.13.refs_3_.refs_11_.pb), channel_id=1, source_target_pairs={{0,1},{1,0},{2,3},{3,2},{4,5},{5,4},{6,7},{7,6},{8,9},{9,8},{10,11... | collective-permute-start | bytes 1474568 | tf_op jit(solution)/shard_map/ppermute | solution.py:346
  23.5 14.3 %collective-permute-start.4 = (f32[4,18,2,8,128]{4,3,2,1,0:T(8,128)S(1)}, f32[4,18,2,8,128]{4,3,2,1,0:T(8,128)S(1)}, u32[]{:S(2)}, u32[]{:S(2)}) collective-permute-start(f32[4,18,2,8,128]{4,3,2,1,0:T(8,128)S(1)} %heun_a0.1.after.refs_0_), channel_id=1, source_target_pairs={{0,31},{1,2},{2,1},{3,4},{4,3},{5,6},{6,5},{7,8},{8,7},{9,10},{10,... | collective-permute-start | bytes 1769480 | tf_op jit(solution)/shard_map/ppermute | solution.py:351
  25.0 12.8 %collective-permute-start.5 = (f32[4,18,2,8,128]{4,3,2,1,0:T(8,128)S(1)}, f32[4,18,2,8,128]{4,3,2,1,0:T(8,128)S(1)}, u32[]{:S(2)}, u32[]{:S(2)}) collective-permute-start(f32[4,18,2,8,128]{4,3,2,1,0:T(8,128)S(1)} %heun_a0.1.after.refs_0_), channel_id=1, source_target_pairs={{0,1},{1,0},{2,3},{3,2},{4,5},{5,4},{6,7},{7,6},{8,9},{9,8},{10,11... | collective-permute-start | bytes 1769480 | tf_op jit(solution)/shard_map/ppermute | solution.py:346
  33.9 8.3 %collective-permute-start.6 = (f32[4,14,2,8,128]{4,3,2,1,0:T(8,128)S(1)}, f32[4,14,2,8,128]{4,3,2,1,0:T(8,128)S(1)}, u32[]{:S(2)}, u32[]{:S(2)}) collective-permute-start(f32[4,14,2,8,128]{4,3,2,1,0:T(8,128)S(1)} %heun_b0.1.after.refs_3_), channel_id=1, source_target_pairs={{0,31},{1,2},{2,1},{3,4},{4,3},{5,6},{6,5},{7,8},{8,7},{9,10},{10,... | collective-permute-start | bytes 1376264 | tf_op jit(solution)/shard_map/ppermute | solution.py:351
  34.0 8.2 %collective-permute-start.7 = (f32[4,14,2,8,128]{4,3,2,1,0:T(8,128)S(1)}, f32[4,14,2,8,128]{4,3,2,1,0:T(8,128)S(1)}, u32[]{:S(2)}, u32[]{:S(2)}) collective-permute-start(f32[4,14,2,8,128]{4,3,2,1,0:T(8,128)S(1)} %heun_b0.1.after.refs_3_), channel_id=1, source_target_pairs={{0,1},{1,0},{2,3},{3,2},{4,5},{5,4},{6,7},{7,6},{8,9},{9,8},{10,11... | collective-permute-start | bytes 1376264 | tf_op jit(solution)/shard_map/ppermute | solution.py:346
  43.6 18.0 %collective-permute-start.10 = (f32[4,18,2,8,128]{4,3,2,1,0:T(8,128)S(1)}, f32[4,18,2,8,128]{4,3,2,1,0:T(8,128)S(1)}, u32[]{:S(2)}, u32[]{:S(2)}) collective-permute-start(f32[4,18,2,8,128]{4,3,2,1,0:T(8,128)S(1)} %heun_b1.1.after.refs_3_), channel_id=1, source_target_pairs={{0,31},{1,2},{2,1},{3,4},{4,3},{5,6},{6,5},{7,8},{8,7},{9,10},{10,... | collective-permute-start | bytes 1769480 | tf_op jit(solution)/shard_map/ppermute | solution.py:351
  43.7 17.9 %collective-permute-start.11 = (f32[4,18,2,8,128]{4,3,2,1,0:T(8,128)S(1)}, f32[4,18,2,8,128]{4,3,2,1,0:T(8,128)S(1)}, u32[]{:S(2)}, u32[]{:S(2)}) collective-permute-start(f32[4,18,2,8,128]{4,3,2,1,0:T(8,128)S(1)} %heun_b1.1.after.refs_3_), channel_id=1, source_target_pairs={{0,1},{1,0},{2,3},{3,2},{4,5},{5,4},{6,7},{7,6},{8,9},{9,8},{10,11... | collective-permute-start | bytes 1769480 | tf_op jit(solution)/shard_map/ppermute | solution.py:346
  51.8 8.2 %collective-permute-start.8 = (f32[4,14,2,8,128]{4,3,2,1,0:T(8,128)S(1)}, f32[4,14,2,8,128]{4,3,2,1,0:T(8,128)S(1)}, u32[]{:S(2)}, u32[]{:S(2)}) collective-permute-start(f32[4,14,2,8,128]{4,3,2,1,0:T(8,128)S(1)} %heun_a1.1.after.refs_0_), channel_id=1, source_target_pairs={{0,31},{1,2},{2,1},{3,4},{4,3},{5,6},{6,5},{7,8},{8,7},{9,10},{10,... | collective-permute-start | bytes 1376264 | tf_op jit(solution)/shard_map/ppermute | solution.py:351
  51.8 8.2 %collective-permute-start.9 = (f32[4,14,2,8,128]{4,3,2,1,0:T(8,128)S(1)}, f32[4,14,2,8,128]{4,3,2,1,0:T(8,128)S(1)}, u32[]{:S(2)}, u32[]{:S(2)}) collective-permute-start(f32[4,14,2,8,128]{4,3,2,1,0:T(8,128)S(1)} %heun_a1.1.after.refs_0_), channel_id=1, source_target_pairs={{0,1},{1,0},{2,3},{3,2},{4,5},{5,4},{6,7},{7,6},{8,9},{9,8},{10,11... | collective-permute-start | bytes 1376264 | tf_op jit(solution)/shard_map/ppermute | solution.py:346
  64.1 26.8 %collective-permute-start.14 = (f32[4,22,2,8,128]{4,3,2,1,0:T(8,128)}, f32[4,22,2,8,128]{4,3,2,1,0:T(8,128)}, u32[]{:S(2)}, u32[]{:S(2)}) collective-permute-start(f32[4,22,2,8,128]{4,3,2,1,0:T(8,128)} %heun_b2.1.after.refs_3_), channel_id=1, source_target_pairs={{0,31},{1,2},{2,1},{3,4},{4,3},{5,6},{6,5},{7,8},{8,7},{9,10},{10,... | collective-permute-start | bytes 2162696 | tf_op jit(solution)/shard_map/ppermute | solution.py:351
  64.1 26.8 %collective-permute-start.15 = (f32[4,22,2,8,128]{4,3,2,1,0:T(8,128)}, f32[4,22,2,8,128]{4,3,2,1,0:T(8,128)}, u32[]{:S(2)}, u32[]{:S(2)}) collective-permute-start(f32[4,22,2,8,128]{4,3,2,1,0:T(8,128)} %heun_b2.1.after.refs_3_), channel_id=1, source_target_pairs={{0,1},{1,0},{2,3},{3,2},{4,5},{5,4},{6,7},{7,6},{8,9},{9,8},{10,11... | collective-permute-start | bytes 2162696 | tf_op jit(solution)/shard_map/ppermute | solution.py:346
  73.4 7.1 %collective-permute-start.12 = (f32[4,10,2,8,128]{4,3,2,1,0:T(8,128)}, f32[4,10,2,8,128]{4,3,2,1,0:T(8,128)S(1)}, u32[]{:S(2)}, u32[]{:S(2)}) collective-permute-start(f32[4,10,2,8,128]{4,3,2,1,0:T(8,128)} %heun_a2.1.after.refs_0_), channel_id=1, source_target_pairs={{0,31},{1,2},{2,1},{3,4},{4,3},{5,6},{6,5},{7,8},{8,7},{9,10},{10,... | collective-permute-start | bytes 983048 | tf_op jit(solution)/shard_map/ppermute | solution.py:351
  73.4 13.4 %collective-permute-start.13 = (f32[4,10,2,8,128]{4,3,2,1,0:T(8,128)}, f32[4,10,2,8,128]{4,3,2,1,0:T(8,128)}, u32[]{:S(2)}, u32[]{:S(2)}) collective-permute-start(f32[4,10,2,8,128]{4,3,2,1,0:T(8,128)} %heun_a2.1.after.refs_0_), channel_id=1, source_target_pairs={{0,1},{1,0},{2,3},{3,2},{4,5},{5,4},{6,7},{7,6},{8,9},{9,8},{10,11... | collective-permute-start | bytes 983048 | tf_op jit(solution)/shard_map/ppermute | solution.py:346
  73.7 21.0 %collective-permute-start.16 = (f32[4,16,8,128]{3,2,1,0:T(8,128)S(1)}, f32[4,16,8,128]{3,2,1,0:T(8,128)}, u32[]{:S(2)}, u32[]{:S(2)}) collective-permute-start(f32[4,16,8,128]{3,2,1,0:T(8,128)S(1)} %own_first.1.here.q_own), channel_id=1, source_target_pairs={{0,31},{1,2},{2,1},{3,4},{4,3},{5,6},{6,5},{7,8},{8,7},{9,10},{10,... | collective-permute-start | bytes 786440 | tf_op jit(solution)/shard_map/ppermute | solution.py:351
  81.3 13.5 %collective-permute-start.17 = (f32[4,16,8,128]{3,2,1,0:T(8,128)S(1)}, f32[4,16,8,128]{3,2,1,0:T(8,128)}, u32[]{:S(2)}, u32[]{:S(2)}) collective-permute-start(f32[4,16,8,128]{3,2,1,0:T(8,128)S(1)} %own_first.1.here.q_own), channel_id=1, source_target_pairs={{0,1},{1,0},{2,3},{3,2},{4,5},{5,4},{6,7},{7,6},{8,9},{9,8},{10,11... | collective-permute-start | bytes 786440 | tf_op jit(solution)/shard_map/ppermute | solution.py:346
  96.8 7.0 %collective-permute-start.18 = (f32[2,16,8,128]{3,2,1,0:T(8,128)S(1)}, f32[2,16,8,128]{3,2,1,0:T(8,128)S(1)}, u32[]{:S(2)}, u32[]{:S(2)}) collective-permute-start(f32[2,16,8,128]{3,2,1,0:T(8,128)S(1)} %get-tuple-element.16), channel_id=1, source_target_pairs={{0,32},{32,64},{64,96},{1,33},{33,65},{65,97},{2,34},{34,66},{66,9... | collective-permute-start | bytes 393224 | tf_op jit(solution)/shard_map/ppermute | solution.py:356
  98.1 8.5 %collective-permute-start.19 = (f32[2,16,8,128]{3,2,1,0:T(8,128)S(1)}, f32[2,16,8,128]{3,2,1,0:T(8,128)S(1)}, u32[]{:S(2)}, u32[]{:S(2)}) collective-permute-start(f32[2,16,8,128]{3,2,1,0:T(8,128)S(1)} %get-tuple-element.16), channel_id=1, source_target_pairs={{0,64},{32,96},{1,65},{33,97},{2,66},{34,98},{3,67},{35,99},{4,68}... | collective-permute-start | bytes 393224 | tf_op jit(solution)/shard_map/ppermute | solution.py:356
  99.4 9.7 %collective-permute-start.20 = (f32[2,16,8,128]{3,2,1,0:T(8,128)S(1)}, f32[2,16,8,128]{3,2,1,0:T(8,128)S(1)}, u32[]{:S(2)}, u32[]{:S(2)}) collective-permute-start(f32[2,16,8,128]{3,2,1,0:T(8,128)S(1)} %get-tuple-element.16), channel_id=1, source_target_pairs={{0,96},{1,97},{2,98},{3,99},{4,100},{5,101},{6,102},{7,103},{8,104... | collective-permute-start | bytes 393224 | tf_op jit(solution)/shard_map/ppermute | solution.py:356
  111.4 5.9 %collective-permute-start.22 = (f32[2,2,16,8,128]{4,3,2,1,0:T(8,128)S(1)}, f32[2,2,16,8,128]{4,3,2,1,0:T(8,128)S(1)}, u32[]{:S(2)}, u32[]{:S(2)}) collective-permute-start(f32[2,2,16,8,128]{4,3,2,1,0:T(8,128)S(1)} %pad_maximum_fusion.2.both), channel_id=1, source_target_pairs={{0,31},{1,2},{2,1},{3,4},{4,3},{5,6},{6,5},{7,8},{8,7},{9,10},{10,... | collective-permute-start | bytes 786440 | tf_op jit(solution)/shard_map/ppermute | solution.py:351
  111.5 9.4 %collective-permute-start.25 = (f32[2,2,16,8,128]{4,3,2,1,0:T(8,128)S(1)}, f32[2,2,16,8,128]{4,3,2,1,0:T(8,128)S(1)}, u32[]{:S(2)}, u32[]{:S(2)}) collective-permute-start(f32[2,2,16,8,128]{4,3,2,1,0:T(8,128)S(1)} %pad_maximum_fusion), channel_id=1, source_target_pairs={{0,1},{1,0},{2,3},{3,2},{4,5},{5,4},{6,7},{7,6},{8,9},{9,8},{10,11... | collective-permute-start | bytes 786440 | tf_op jit(solution)/shard_map/ppermute | solution.py:346
  136.0 5.9 %collective-permute-start.28 = (f32[2,2,16,8,128]{4,3,2,1,0:T(8,128)S(1)}, f32[2,2,16,8,128]{4,3,2,1,0:T(8,128)S(1)}, u32[]{:S(2)}, u32[]{:S(2)}) collective-permute-start(f32[2,2,16,8,128]{4,3,2,1,0:T(8,128)S(1)} %walk.4.both), channel_id=1, source_target_pairs={{0,31},{1,2},{2,1},{3,4},{4,3},{5,6},{6,5},{7,8},{8,7},{9,10},{10,... | collective-permute-start | bytes 786440 | tf_op jit(solution)/shard_map/ppermute | solution.py:351
  (25 other events, 329.3 us)

commit v3 on v2

v3 whole, which is shorter than its diff:
```python
import functools

import jax
import jax.numpy as jnp
from jax import lax
from jax.experimental import pallas as pl
from jax.experimental.pallas import tpu as pltpu
from jax.sharding import PartitionSpec as P

FSTEPS = 4
CSTEPS = 2
DU = 0.16
DV = 0.08
FIRST = 24
TILES = 32
F32 = jnp.float32
UNROLL = 8
VMEM_LIMIT = 16 * 1024 * 1024

VM = pl.BlockSpec(memory_space=pltpu.VMEM)
ANY = pl.BlockSpec(memory_space=pl.ANY)
PARAMS = pltpu.CompilerParams(vmem_limit_bytes=VMEM_LIMIT)
COARSE = (2, 16, 8, 128)
FLAT = 3
TAIL = 4 * (FIRST - 4 * FLAT) * 2


def splitter(transposed):
    r = lax.broadcasted_iota(jnp.int32, (256, 256), 0)
    c = lax.broadcasted_iota(jnp.int32, (256, 256), 1)
    if transposed:
        r, c = c, r
    return jnp.where(r == 2 * (c % 128) + c // 128, 1.0, 0.0).astype(jnp.bfloat16)


def permuted(x, mat):
    high = x.astype(jnp.bfloat16)
    rest = x - high.astype(F32)
    mid = rest.astype(jnp.bfloat16)
    low = (rest - mid.astype(F32)).astype(jnp.bfloat16)
    dot = lambda p: jnp.dot(p, mat, preferred_element_type=F32)
    return dot(high) + (dot(mid) + dot(low))


def odd():
    return lax.rem(lax.axis_index("space"), 2)


def prep_kernel(x, feed, kill, pair_a, pair_b, cross_a, cross_b, xs, rs, rows, sems):
    flip = odd()
    copies = []
    for i, (src, dst) in enumerate(
        [(x.at[sp, q], xs.at[2 * sp + q]) for sp in range(2) for q in range(2)]
        + [(src.at[q], rs.at[2 * k + q]) for q in range(2) for k, src in enumerate((feed, kill))]
    ):
        copies.append(pltpu.make_async_copy(src, dst, sems.at[i]))
        copies[-1].start()
    mat = splitter(False)

    def scatter(plane, k, targets):
        done = permuted(plane, mat)
        rows[k, 0] = done[:, :128]
        rows[k, 1] = done[:, 128:]
        for i in range(TILES):
            for h in range(2):
                tile = rows[k, h, pl.ds(i, 8, stride=32), :]
                for (a, b), q in targets:
                    if i < FIRST:
                        a[q, i, h] = tile
                    else:
                        b[q, i - FIRST, h] = tile

    pair, cross = (pair_a, pair_b), (cross_a, cross_b)
    for sp in range(2):
        copies[2 * sp].wait()
        copies[2 * sp + 1].wait()
        for q in range(2):
            scatter(xs[2 * sp + (q ^ flip)], 2 * sp + q, [(pair, 2 * sp + q), (cross, 2 * sp + q)])
    for c in copies[4:]:
        c.wait()
    for q, target in ((0, cross), (1, pair)):
        f = rs[q ^ flip]
        scatter(f, 4 + 2 * q, [(target, 4)])
        scatter(0.52 - (f + rs[2 + (q ^ flip)]), 5 + 2 * q, [(target, 5)])


def prep(x, feed, kill):
    a = jax.ShapeDtypeStruct((6, FIRST, 2, 8, 128), F32)
    b = jax.ShapeDtypeStruct((6, TILES - FIRST, 2, 8, 128), F32)
    hbm = pl.BlockSpec(memory_space=pltpu.HBM)
    return pl.pallas_call(
        prep_kernel,
        out_shape=[a, b, a, b],
        in_specs=[hbm] * 3,
        out_specs=[VM] * 4,
        scratch_shapes=[
            pltpu.VMEM((4, 256, 256), F32),
            pltpu.VMEM((4, 256, 256), F32),
            pltpu.VMEM((8, 2, 256, 128), F32),
            pltpu.SemaphoreType.DMA((8,)),
        ],
        compiler_params=PARAMS,
        name="prep",
    )(x, feed, kill)


LINE = ((1, 1), (1, 0), (0, 0), (0, 1), (2, 1), (2, 0))


def runs(lo, hi, key):
    out = []
    for v in range(lo, hi):
        k = key(v)
        if out and out[-1][2] == k:
            out[-1][1] = v + 1
        else:
            out.append([v, v + 1, k])
    return out


def over(lo, hi, key, work):
    for start, stop, k in runs(lo, hi, key):
        if stop - start < 4:
            for v in range(start, stop):
                work(v, k)
        else:
            @pl.loop(start, stop, unroll=min(UNROLL, stop - start))
            def _(v):
                work(v, k)


def moved(x, rolled):
    return pltpu.roll(x, 7, 0) if rolled else x


def beside(other, h):
    return other + pltpu.roll(other, 1 if h == 0 else 127, 1)


def heun_kernel(step, second, total, after, *refs):
    refs = list(refs)
    extra = refs.pop(0) if step == FLAT - 1 and not second else None
    groups = 2 if second else 1
    state = [refs[3 * g:3 * g + 3] for g in range(groups)]
    rate = [refs[3 * groups + 4 * g:3 * groups + 4 * g + 4] for g in range(groups)]
    out, mids = refs[-2:]
    lo = FIRST - 2 * step - 4 if second else 2 * step
    hi = lo + total

    def find_state(v):
        if not second:
            return 0, -2 * step, False
        if v < FIRST - 2 * step:
            return 0, -2 * step, False
        if v < TILES + 2 * step:
            return 1, 2 * step - FIRST, False
        return 0, -TILES - 2 * step, True

    def find_rate(v):
        if v < FIRST:
            return 0, 0, False
        if v < TILES:
            return 1, -FIRST, False
        return 0, -TILES, True

    def cell(sp, p, v, h, at):
        g, off, rolled = at
        source, plane = LINE[p]
        ref, q = state[g][source], 2 * sp + plane
        if g == 0 and step == FLAT:
            return moved(ref[(q * (FIRST - 4 * step) + v + off) * 2 + h], rolled)
        return moved(ref[q, v + off, h], rolled)

    def put(q, i, h, x):
        if extra is None:
            out[q, i, h] = x
        else:
            out[(q * (total - 4) + i) * 2 + h] = x

    def coef(k, place, v, h, at):
        g, off, rolled = at
        return moved(rate[g][(2, 0, 1, 3)[place]][4 + k, v + off, h], rolled)

    def ahead(u, v, near_u, near_v, f, cv):
        uvv = u * v * v
        return DU * near_u + (1.0 - 6.0 * DU) * u + f * (1.0 - u) - uvv, DV * near_v + cv * v + uvv

    def first(v, key):
        below, here, above, at = key
        c = [[cell(sp, p, v, h, here) for h in range(2)] for sp in range(2) for p in range(6)]
        for p in range(1, 5):
            for h in range(2):
                near = []
                for sp in range(2):
                    i = 6 * sp + p
                    s = cell(sp, p, v - 1, h, below) + cell(sp, p, v + 1, h, above)
                    near.append(beside(c[i][1 - h], h) + (s + (c[i - 1][h] + c[i + 1][h])))
                nu, nv = ahead(c[p][h], c[6 + p][h], *near, coef(0, p - 1, v, h, at), coef(1, p - 1, v, h, at))
                mids[0, p - 1, v - lo, h] = nu
                mids[1, p - 1, v - lo, h] = nv

    def then(v, key):
        here, at = key
        c = [[mids[sp, p, v - lo, h] for h in range(2)] for sp in range(2) for p in range(4)]
        for p in range(1, 3):
            for h in range(2):
                near = []
                for sp in range(2):
                    i = 4 * sp + p
                    s = mids[sp, p, v - lo - 1, h] + mids[sp, p, v - lo + 1, h]
                    near.append(beside(c[i][1 - h], h) + (s + (c[i - 1][h] + c[i + 1][h])))
                nu, nv = ahead(c[p][h], c[4 + p][h], *near, coef(0, p, v, h, at), coef(1, p, v, h, at))
                put(p - 1, v - lo - 2, h, 0.5 * (cell(0, p + 1, v, h, here) + nu))
                put(2 + p - 1, v - lo - 2, h, 0.5 * (cell(1, p + 1, v, h, here) + nv))

    if extra is not None:
        for k in range(4):
            for j in range(16):
                out[TAIL + 16 * k + j] = extra[k, j]

    over(lo + 1, hi - 1, lambda v: (find_state(v - 1), find_state(v), find_state(v + 1), find_rate(v)), first)
    over(lo + 2, hi - 2, lambda v: (find_state(v), find_rate(v)), then)


def heun(step, second, state, rate, after, extra=None):
    total = (TILES - FIRST + 4 * step + 8) if second else FIRST - 4 * step
    ins = [r for g in state for r in g] + [r for g in rate for r in g]
    shape = (4, total - 4, 2, 8, 128)
    if extra is not None:
        ins = [extra] + ins
        shape = (TAIL + 64, 8, 128)
    return pl.pallas_call(
        functools.partial(heun_kernel, step, second, total),
        out_shape=jax.ShapeDtypeStruct(shape, F32),
        in_specs=[ANY] + [VM] * len(ins),
        out_specs=VM,
        scratch_shapes=[pltpu.VMEM((2, 4, total, 2, 8, 128), F32)],
        compiler_params=PARAMS,
        cost_estimate=pl.CostEstimate(flops=total * 2048 * 150, bytes_accessed=total * 8192 * 20, transcendentals=0),
        name="heun_b%d" % step if second else "heun_a%d" % step,
    )(after, *ins)


def mean_tile(tiles):
    s = [tiles[i] + tiles[i + 1] for i in range(0, 8, 2)]
    return 0.125 * ((s[0] + s[1]) + (s[2] + s[3]))


def mean_of(a, b, j, rows):
    ref, off = (a, 0) if 2 * j < FIRST else (b, FIRST)
    return mean_tile([ref[q, 2 * j + i - off, h] for q in rows for i in range(2) for h in range(2)])


def euler(get, cf, ccv, j):
    new = []
    for sp in range(2):
        c = get(0, sp, j)
        up = get(0, sp, j + 1) if j < 15 else pltpu.roll(get(0, sp, 0), 7, 0)
        down = get(0, sp, j - 1) if j else pltpu.roll(get(0, sp, 15), 1, 0)
        s = pltpu.roll(c, 1, 1) + pltpu.roll(c, 127, 1) + (up + down)
        new.append((c, s + (get(-1, sp, j) + get(1, sp, j))))
    (u, su), (v, sv) = new
    uvv = u * v * v
    nu = u + 2.0 * (0.25 * DU * (su - 6.0 * u) - uvv + cf * (1.0 - u))
    nv = v + 2.0 * (0.25 * DV * (sv - 6.0 * v) + uvv - ccv * v)
    return nu, nv


def own_first_kernel(pa, pb, ca, cb, gpa, gpb, gca, gcb, out, line):
    for j in range(16):
        for sp in range(2):
            rows = (2 * sp, 2 * sp + 1)
            line[0, sp, j] = mean_of(gca, gcb, j, rows)
            line[1, sp, j] = mean_of(pa, pb, j, rows)
            line[2, sp, j] = mean_of(gpa, gpb, j, rows)
        for k in range(2):
            (x, off), (y, _) = ((pa, 0), (ca, 0)) if 2 * j < FIRST else ((pb, FIRST), (cb, FIRST))
            tiles = [r[4 + k, 2 * j + i - off, h] for r in (y, x) for i in range(2) for h in range(2)]
            m = mean_tile(tiles)
            out[2 + k, j] = m if k == 0 else 0.52 - m
    for j in range(16):
        out[0, j], out[1, j] = euler(lambda d, sp, i: line[1 + d, sp, i], out[2, j], out[3, j], j)


def own_first(*refs):
    return pl.pallas_call(
        own_first_kernel,
        out_shape=jax.ShapeDtypeStruct((4, 16, 8, 128), F32),
        in_specs=[VM] * 8,
        out_specs=VM,
        scratch_shapes=[pltpu.VMEM((3,) + COARSE, F32)],
        compiler_params=PARAMS,
        name="own_first",
    )(*refs)


def fine_tile(a, b, q, v, h):
    if v < 2 * FSTEPS:
        return pltpu.roll(b[q, v + TILES - FIRST + 2 * FSTEPS, h], 1, 0)
    if v < FIRST - 2 * FSTEPS:
        return a[q, v - 2 * FSTEPS, h]
    return b[q, v - FIRST + 2 * FSTEPS, h]


def jump_kernel(a, b, here, cross, pair, end, send, rate_cross, rate_pair):
    first = lax.axis_index("tm") == 0
    for k in range(2):
        for j in range(16):
            rate_cross[k, j] = cross[TAIL + 16 * (2 + k) + j]
            rate_pair[k, j] = pair[TAIL + 16 * (2 + k) + j]

    def get(d, sp, j):
        return here[sp, j] if d == 0 else (cross if d < 0 else pair)[TAIL + 16 * sp + j]

    for j in range(16):
        g = euler(get, here[2, j], here[3, j], j)
        for sp in range(2):
            m = mean_tile([fine_tile(a, b, 2 * sp + q, 2 * j + i, h) for q in range(2) for i in range(2) for h in range(2)])
            end[sp, j] = m
            jump = m - g[sp]
            send[sp, j] = jnp.where(first, g[sp] + jump, jump)


def jump_of(a, b, here, cross, pair):
    shape = jax.ShapeDtypeStruct(COARSE, F32)
    return pl.pallas_call(
        jump_kernel,
        out_shape=[shape] * 4,
        in_specs=[VM] * 5,
        out_specs=[VM] * 4,
        compiler_params=PARAMS,
        name="jump",
    )(a, b, here, cross, pair)


def pack_kernel(after, one, other, out):
    out[0] = one[...]
    out[1] = other[...]


def pack(one, other, after):
    return pl.pallas_call(
        pack_kernel,
        out_shape=jax.ShapeDtypeStruct((2,) + COARSE, F32),
        in_specs=[ANY, VM, VM],
        out_specs=VM,
        compiler_params=PARAMS,
        name="pack",
    )(after, one, other)


def walk_kernel(least, both, near, far, q_own, r_cross, r_pair, r_far, *refs):
    *jumps, out, mid = refs
    line = ((near, 1), (near, 0), (both, 0), (both, 1), (far, 0), (far, 1))
    rates = ((r_cross, 0), (q_own, 2), (r_pair, 0), (r_far, 0))
    counts = lax.axis_index("tm") >= least
    for p in range(1, 5):
        q, k = rates[p - 1]
        for j in range(16):
            new = euler(lambda d, sp, i: line[p + d][0][line[p + d][1], sp, i], q[k, j], q[k + 1, j], j)
            mid[p - 1, 0, j], mid[p - 1, 1, j] = new
    for n, jump in enumerate(jumps):
        q, k = rates[n + 1]
        for j in range(16):
            new = euler(lambda d, sp, i: mid[n + 1 + d, sp, i], q[k, j], q[k + 1, j], j)
            for sp in range(2):
                x = jnp.where(counts, new[sp], 0.0) + jump[sp, j]
                if len(jumps) == 2:
                    out[n, sp, j] = x
                else:
                    out[sp, j] = x


def walk(least, both, near, far, rates, jumps):
    return pl.pallas_call(
        functools.partial(walk_kernel, least),
        out_shape=jax.ShapeDtypeStruct(((2,) if len(jumps) == 2 else ()) + COARSE, F32),
        in_specs=[VM] * (7 + len(jumps)),
        out_specs=VM,
        scratch_shapes=[pltpu.VMEM((4,) + COARSE, F32)],
        compiler_params=PARAMS,
        name="walk%d" % least,
    )(both, near, far, *rates, *jumps)


def finish_kernel(a, b, end, chained, out, rows, done, sems):
    mat = splitter(True)
    flip = odd()
    copies = []
    for sp in range(2):
        shift = [chained[sp, j] - end[sp, j] for j in range(16)]
        for q in range(2):
            k = 2 * sp + q
            for v in range(TILES):
                for h in range(2):
                    rows[k, h, pl.ds(v, 8, stride=32), :] = fine_tile(a, b, k, v, h) + shift[v // 2]
            done[k] = permuted(jnp.concatenate([rows[k, 0], rows[k, 1]], axis=1), mat)
            copies.append(pltpu.make_async_copy(done.at[k], out.at[sp, q ^ flip], sems.at[k]))
            copies[-1].start()
    for c in copies:
        c.wait()


def finish(a, b, end, chained):
    return pl.pallas_call(
        finish_kernel,
        out_shape=jax.ShapeDtypeStruct((2, 2, 256, 256), F32),
        in_specs=[VM] * 4,
        out_specs=pl.BlockSpec(memory_space=pltpu.HBM),
        scratch_shapes=[
            pltpu.VMEM((4, 2, 256, 128), F32),
            pltpu.VMEM((4, 256, 256), F32),
            pltpu.SemaphoreType.DMA((4,)),
        ],
        compiler_params=PARAMS,
        name="finish",
    )(a, b, end, chained)


def swap_pair(x):
    n = lax.axis_size("space")
    return lax.ppermute(x, "space", [(i, i ^ 1) for i in range(n)])


def swap_cross(x):
    n = lax.axis_size("space")
    return lax.ppermute(x, "space", [(i, (i + 1) % n if i % 2 else (i - 1) % n) for i in range(n)])


def later(x, distance):
    n = lax.axis_size("tm")
    return lax.ppermute(x, "tm", [(i, i + distance) for i in range(n - distance)])


def body(slice_starts, feed, kill):
    pair_a, pair_b, cross_a, cross_b = prep(slice_starts[0], feed, kill)
    got_pair_a, got_cross_a = swap_pair(pair_a), swap_cross(cross_a)
    got_pair_b, got_cross_b = swap_pair(pair_b), swap_cross(cross_b)
    rate_a = (cross_a, pair_a, got_cross_a, got_pair_a)
    rate_b = (cross_b, pair_b, got_cross_b, got_pair_b)
    state_a = (pair_a, got_cross_a, got_pair_a)
    state_b = (pair_b, got_cross_b, got_pair_b)
    new_b = pair_b
    q_own = own_first(pair_a, pair_b, cross_a, cross_b, got_pair_a, got_pair_b, got_cross_a, got_cross_b)
    for step in range(FSTEPS):
        new_a = heun(step, False, [state_a], [rate_a], new_b, q_own if step == FLAT - 1 else None)
        last = step == FSTEPS - 1
        if not last:
            next_a = (new_a, swap_cross(new_a), swap_pair(new_a))
        new_b = heun(step, True, [state_a, state_b], [rate_a, rate_b], new_a)
        if not last:
            state_a = next_a
            state_b = (new_b, swap_cross(new_b), swap_pair(new_b))
    end, send, rate_cross, rate_pair = jump_of(new_a, new_b, q_own, state_a[1], state_a[2])
    rates = (q_own, rate_cross, rate_pair, swap_pair(rate_cross))
    from3, from2, from1 = later(send, 3), later(send, 2), later(send, 1)
    both = pack(from3, swap_pair(from3), rates[3])
    for least, jumps in ((3, (from2, swap_pair(from2))), (2, (from1, swap_pair(from1))), (1, (send,))):
        near = swap_cross(both)
        far = swap_pair(near)
        both = walk(least, both, near, far, rates, jumps)
    return finish(new_a, new_b, end, both)[None]


def solution(mesh):
    in_specs = (P("tm", None, "space", None, None), P("space", None, None), P("space", None, None))
    out_specs = P("tm", None, "space", None, None)
    return jax.shard_map(body, mesh=mesh, in_specs=in_specs, out_specs=out_specs, check_vma=False)
```

time: 153 us -> 127 us (0.83)
  Pallas kernels: 26.9 us -> 14.8 us
  starting transfers between devices: 67.3 us -> 58.4 us
  local copies, waits for them, and re-layouts: 8.31 us -> 3.31 us
    ppermute x12 -> x11, waiting for transfers between devices: 36.3 us -> 43.3 us  [swap_cross(): lax.ppermute(x, 'space', [(i, (i + 1) % n if i % 2 else (i - 1) % n) for...]
    pallas_call x8, Pallas kernels: 14.7 us -> 7.69 us  [heun(): pl.pallas_call(functools.partial(heun_kernel, step, second, total), out_s...]
    ppermute x3, waiting for transfers between devices: 8.41 us -> 2.43 us  [later(): lax.ppermute(x, 'tm', [(i, i + distance) for i in range(n - distance)])]
    unnamed x38 -> x6, local copies, waits for them, and re-layouts: 8.29 us -> 3.31 us
    ppermute x15, starting transfers between devices: 57.4 us -> 52.5 us  [swap_pair(): return lax.ppermute(x, 'space', [(i, i ^ 1) for i in range(n)])]
    pallas_call x5 -> x6, Pallas kernels: 9.31 us -> 4.81 us  [the longest x1 3.13 us: prep(): pl.pallas_call(prep_kernel, out_shape=[a, b, a, b], in_specs=[hbm] * 3, o...]
    ppermute x12 -> x11, starting transfers between devices: 6.06 us -> 2.02 us  [swap_cross(): lax.ppermute(x, 'space', [(i, (i + 1) % n if i % 2 else (i - 1) % n) for...]
  transfers between devices with their start and end apart: 30 -> 29, of which waited for: 14 -> 15; matrix products, arithmetic and copies ran while one was open for 0% -> 0% of each run, Pallas kernels for 7% -> 5%
where the time goes in v3:
time: 127 us
  starting transfers between devices  58.4 us (46%)
  waiting for transfers between devices  50.2 us (40%)
  Pallas kernels  14.8 us (12%)
  local copies, waits for them, and re-layouts  3.31 us (3%)
    ppermute x15, starting transfers between devices, swap_pair(): return lax.ppermute(x, 'space', [(i, i ^ 1) for i in range(n)])  52.5 us
    ppermute x11, waiting for transfers between devices, swap_cross(): lax.ppermute(x, 'space', [(i, (i + 1) % n if i % 2 else (i - 1) % n) for...  43.3 us
    pallas_call x8, Pallas kernels, heun(): pl.pallas_call(functools.partial(heun_kernel, step, second, total), out_s...  7.69 us
    ppermute x15, waiting for transfers between devices, swap_pair(): return lax.ppermute(x, 'space', [(i, i ^ 1) for i in range(n)])  4.5 us
    ppermute x3, starting transfers between devices, later(): lax.ppermute(x, 'tm', [(i, i + distance) for i in range(n - distance)])  3.88 us
    unnamed x6, local copies, waits for them, and re-layouts  3.31 us
    pallas_call x1, Pallas kernels, prep(): pl.pallas_call(prep_kernel, out_shape=[a, b, a, b], in_specs=[hbm] * 3, o...  3.13 us
  transfers between devices with their start and end apart: 29, of which 15 were waited for; matrix products, arithmetic and copies ran while one was open for 0% of the time, Pallas kernels for 5%

profile of v3, /device:TPU:7, one launch (start us, length us, event | category | flops | bytes accessed | tf_op | source)
XLA Modules:
  0.0 127.1 jit_solution(2217754606723843859)
XLA Ops:
  3.3 3.1 %prep.1 = (f32[6,24,2,8,128]{4,3,2,1,0:T(8,128)S(1)}, f32[6,8,2,8,128]{4,3,2,1,0:T(8,128)S(1)}, f32[6,24,2,8,128]{4,3,2,1,0:T(8,128)S(1)}, f32[6,8,2,8,128]{4,3,2,1,0:T(8,128)S(1)}) custom-call(f32[2,2,256,256]{3,2,1,0:T(8,128)S(1)} %bitcast.2, f32[2,256,256]{2,1,0:T(8,128)S(1)} %copy-done.1, f32[2,256,256]{2,1,0:T(8,128)S(1)} %copy-done.2), custom_call_target="tpu_custom_call" | custom-call | tf_op jit(solution)/shard_map/prep/pallas_call | solution.py:91
  9.0 4.9 %collective-permute-start.3 = (f32[6,8,2,8,128]{4,3,2,1,0:T(8,128)S(1)}, f32[6,8,2,8,128]{4,3,2,1,0:T(8,128)S(1)}, u32[]{:S(2)}, u32[]{:S(2)}) collective-permute-start(f32[6,8,2,8,128]{4,3,2,1,0:T(8,128)S(1)} %get-tuple-element.13.after.refs_3_.refs_11_.pb), channel_id=1, source_target_pairs={{0,1},{1,0},{2,3},{3,2},{4,5},{5,4},{6,7},{7,6},{8,9},{9,8},{10,11... | collective-permute-start | bytes 1179656 | tf_op jit(solution)/shard_map/ppermute | solution.py:422
  13.8 9.3 %collective-permute-done.refs_1_.refs_5_.refs_8_.gca.refs_6_ = f32[6,24,2,8,128]{4,3,2,1,0:T(8,128)S(1)} collective-permute-done((f32[6,24,2,8,128]{4,3,2,1,0:T(8,128)S(1)}, f32[6,24,2,8,128]{4,3,2,1,0:T(8,128)S(1)}, u32[]{:S(2)}, u32[]{:S(2)}) %collective-permute-start) | collective-permute-done | bytes 1179680 | tf_op jit(solution)/shard_map/ppermute | solution.py:427
  24.8 4.6 %collective-permute-start.5 = (f32[4,20,2,8,128]{4,3,2,1,0:T(8,128)S(1)}, f32[4,20,2,8,128]{4,3,2,1,0:T(8,128)S(1)}, u32[]{:S(2)}, u32[]{:S(2)}) collective-permute-start(f32[4,20,2,8,128]{4,3,2,1,0:T(8,128)S(1)} %heun_a0.1.after.refs_0_), channel_id=1, source_target_pairs={{0,1},{1,0},{2,3},{3,2},{4,5},{5,4},{6,7},{7,6},{8,9},{9,8},{10,11... | collective-permute-start | bytes 1966088 | tf_op jit(solution)/shard_map/ppermute | solution.py:422
  30.0 5.2 %collective-permute-start.7 = (f32[4,12,2,8,128]{4,3,2,1,0:T(8,128)S(1)}, f32[4,12,2,8,128]{4,3,2,1,0:T(8,128)S(1)}, u32[]{:S(2)}, u32[]{:S(2)}) collective-permute-start(f32[4,12,2,8,128]{4,3,2,1,0:T(8,128)S(1)} %heun_b0.1.after.refs_3_), channel_id=1, source_target_pairs={{0,1},{1,0},{2,3},{3,2},{4,5},{5,4},{6,7},{7,6},{8,9},{9,8},{10,11... | collective-permute-start | bytes 1179656 | tf_op jit(solution)/shard_map/ppermute | solution.py:422
  35.2 4.5 %collective-permute-done.4.refs_1_ = f32[4,20,2,8,128]{4,3,2,1,0:T(8,128)S(1)} collective-permute-done((f32[4,20,2,8,128]{4,3,2,1,0:T(8,128)S(1)}, f32[4,20,2,8,128]{4,3,2,1,0:T(8,128)S(1)}, u32[]{:S(2)}, u32[]{:S(2)}) %collective-permute-start.4) | collective-permute-done | bytes 655392 | tf_op jit(solution)/shard_map/ppermute | solution.py:427
  40.7 3.2 %collective-permute-start.9 = (f32[4,16,2,8,128]{4,3,2,1,0:T(8,128)S(1)}, f32[4,16,2,8,128]{4,3,2,1,0:T(8,128)S(1)}, u32[]{:S(2)}, u32[]{:S(2)}) collective-permute-start(f32[4,16,2,8,128]{4,3,2,1,0:T(8,128)S(1)} %heun_a1.1.after.refs_1_.refs_0_), channel_id=1, source_target_pairs={{0,1},{1,0},{2,3},{3,2},{4,5},{5,4},{6,7},{7,6},{8,9},{9,8},{10,11... | collective-permute-start | bytes 1572872 | tf_op jit(solution)/shard_map/ppermute | solution.py:422
  44.7 5.2 %collective-permute-start.11 = (f32[4,16,2,8,128]{4,3,2,1,0:T(8,128)S(1)}, f32[4,16,2,8,128]{4,3,2,1,0:T(8,128)S(1)}, u32[]{:S(2)}, u32[]{:S(2)}) collective-permute-start(f32[4,16,2,8,128]{4,3,2,1,0:T(8,128)S(1)} %heun_b1.1.after.refs_3_), channel_id=1, source_target_pairs={{0,1},{1,0},{2,3},{3,2},{4,5},{5,4},{6,7},{7,6},{8,9},{9,8},{10,11... | collective-permute-start | bytes 1572872 | tf_op jit(solution)/shard_map/ppermute | solution.py:422
  50.1 2.7 %collective-permute-done.8.refs_2_.refs_1_ = f32[4,16,2,8,128]{4,3,2,1,0:T(8,128)S(1)} collective-permute-done((f32[4,16,2,8,128]{4,3,2,1,0:T(8,128)S(1)}, f32[4,16,2,8,128]{4,3,2,1,0:T(8,128)S(1)}, u32[]{:S(2)}, u32[]{:S(2)}) %collective-permute-start.8) | collective-permute-done | bytes 524320 | tf_op jit(solution)/shard_map/ppermute | solution.py:427
  54.1 3.2 %collective-permute-start.13 = (f32[160,8,128]{2,1,0:T(8,128)S(1)}, f32[160,8,128]{2,1,0:T(8,128)S(1)}, u32[]{:S(2)}, u32[]{:S(2)}) collective-permute-start(f32[160,8,128]{2,1,0:T(8,128)S(1)} %heun_a2.1.after.refs_0_), channel_id=1, source_target_pairs={{0,1},{1,0},{2,3},{3,2},{4,5},{5,4},{6,7},{7,6},{8,9},{9,8},{10,11... | collective-permute-start | bytes 1966088 | tf_op jit(solution)/shard_map/ppermute | solution.py:422
  59.6 3.7 %collective-permute-start.15 = (f32[4,20,2,8,128]{4,3,2,1,0:T(8,128)S(1)}, f32[4,20,2,8,128]{4,3,2,1,0:T(8,128)S(1)}, u32[]{:S(2)}, u32[]{:S(2)}) collective-permute-start(f32[4,20,2,8,128]{4,3,2,1,0:T(8,128)S(1)} %heun_b2.1.after.refs_3_), channel_id=1, source_target_pairs={{0,1},{1,0},{2,3},{3,2},{4,5},{5,4},{6,7},{7,6},{8,9},{9,8},{10,11... | collective-permute-start | bytes 1966088 | tf_op jit(solution)/shard_map/ppermute | solution.py:422
  63.4 4.2 %collective-permute-done.12.refs_1_.cross = f32[160,8,128]{2,1,0:T(8,128)S(1)} collective-permute-done((f32[160,8,128]{2,1,0:T(8,128)S(1)}, f32[160,8,128]{2,1,0:T(8,128)S(1)}, u32[]{:S(2)}, u32[]{:S(2)}) %collective-permute-start.12) | collective-permute-done | bytes 655392 | tf_op jit(solution)/shard_map/ppermute | solution.py:427
  68.2 6.4 %collective-permute-done.14.refs_4_ = f32[4,20,2,8,128]{4,3,2,1,0:T(8,128)S(1)} collective-permute-done((f32[4,20,2,8,128]{4,3,2,1,0:T(8,128)S(1)}, f32[4,20,2,8,128]{4,3,2,1,0:T(8,128)S(1)}, u32[]{:S(2)}, u32[]{:S(2)}) %collective-permute-start.14) | collective-permute-done | bytes 655392 | tf_op jit(solution)/shard_map/ppermute | solution.py:427
  77.1 3.2 %collective-permute-start.16 = (f32[2,16,8,128]{3,2,1,0:T(8,128)S(1)}, f32[2,16,8,128]{3,2,1,0:T(8,128)S(1)}, u32[]{:S(2)}, u32[]{:S(2)}) collective-permute-start(f32[2,16,8,128]{3,2,1,0:T(8,128)S(1)} %get-tuple-element.18.r_cross), channel_id=1, source_target_pairs={{0,1},{1,0},{2,3},{3,2},{4,5},{5,4},{6,7},{7,6},{8,9},{9,8},{10,11... | collective-permute-start | bytes 393224 | tf_op jit(solution)/shard_map/ppermute | solution.py:422
  80.3 2.4 %collective-permute-done.17.one = f32[2,16,8,128]{3,2,1,0:T(8,128)S(1)} collective-permute-done((f32[2,16,8,128]{3,2,1,0:T(8,128)S(1)}, f32[2,16,8,128]{3,2,1,0:T(8,128)S(1)}, u32[]{:S(2)}, u32[]{:S(2)}) %collective-permute-start.17) | collective-permute-done | bytes 131104 | tf_op jit(solution)/shard_map/ppermute | solution.py:432
  82.7 4.3 %collective-permute-start.18 = (f32[2,16,8,128]{3,2,1,0:T(8,128)S(1)}, f32[2,16,8,128]{3,2,1,0:T(8,128)S(1)}, u32[]{:S(2)}, u32[]{:S(2)}) collective-permute-start(f32[2,16,8,128]{3,2,1,0:T(8,128)S(1)} %collective-permute-done.17.one), channel_id=1, source_target_pairs={{0,1},{1,0},{2,3},{3,2},{4,5},{5,4},{6,7},{7,6},{8,9},{9,8},{10,11... | collective-permute-start | bytes 393224 | tf_op jit(solution)/shard_map/ppermute | solution.py:422
  89.4 4.5 %collective-permute-done.19.near = f32[2,2,16,8,128]{4,3,2,1,0:T(8,128)S(1)} collective-permute-done((f32[2,2,16,8,128]{4,3,2,1,0:T(8,128)S(1)}, f32[2,2,16,8,128]{4,3,2,1,0:T(8,128)S(1)}, u32[]{:S(2)}, u32[]{:S(2)}) %collective-permute-start.19) | collective-permute-done | bytes 262176 | tf_op jit(solution)/shard_map/ppermute | solution.py:427
  93.9 3.7 %collective-permute-start.20 = (f32[2,2,16,8,128]{4,3,2,1,0:T(8,128)S(1)}, f32[2,2,16,8,128]{4,3,2,1,0:T(8,128)S(1)}, u32[]{:S(2)}, u32[]{:S(2)}) collective-permute-start(f32[2,2,16,8,128]{4,3,2,1,0:T(8,128)S(1)} %collective-permute-done.19.near), channel_id=1, source_target_pairs={{0,1},{1,0},{2,3},{3,2},{4,5},{5,4},{6,7},{7,6},{8,9},{9,8},{10,11... | collective-permute-start | bytes 786440 | tf_op jit(solution)/shard_map/ppermute | solution.py:422
  97.6 3.1 %collective-permute-start.22 = (f32[2,16,8,128]{3,2,1,0:T(8,128)S(1)}, f32[2,16,8,128]{3,2,1,0:T(8,128)S(1)}, u32[]{:S(2)}, u32[]{:S(2)}) collective-permute-start(f32[2,16,8,128]{3,2,1,0:T(8,128)S(1)} %collective-permute-done.21.refs_0_), channel_id=1, source_target_pairs={{0,1},{1,0},{2,3},{3,2},{4,5},{5,4},{6,7},{7,6},{8,9},{9,8},{10,11... | collective-permute-start | bytes 393224 | tf_op jit(solution)/shard_map/ppermute | solution.py:422
  103.7 4.5 %collective-permute-done.23.near = f32[2,2,16,8,128]{4,3,2,1,0:T(8,128)S(1)} collective-permute-done((f32[2,2,16,8,128]{4,3,2,1,0:T(8,128)S(1)}, f32[2,2,16,8,128]{4,3,2,1,0:T(8,128)S(1)}, u32[]{:S(2)}, u32[]{:S(2)}) %collective-permute-start.23) | collective-permute-done | bytes 262176 | tf_op jit(solution)/shard_map/ppermute | solution.py:427
  108.1 3.7 %collective-permute-start.24 = (f32[2,2,16,8,128]{4,3,2,1,0:T(8,128)S(1)}, f32[2,2,16,8,128]{4,3,2,1,0:T(8,128)S(1)}, u32[]{:S(2)}, u32[]{:S(2)}) collective-permute-start(f32[2,2,16,8,128]{4,3,2,1,0:T(8,128)S(1)} %collective-permute-done.23.near), channel_id=1, source_target_pairs={{0,1},{1,0},{2,3},{3,2},{4,5},{5,4},{6,7},{7,6},{8,9},{9,8},{10,11... | collective-permute-start | bytes 786440 | tf_op jit(solution)/shard_map/ppermute | solution.py:422
  113.8 5.8 %collective-permute-done.27.near = f32[2,2,16,8,128]{4,3,2,1,0:T(8,128)S(1)} collective-permute-done((f32[2,2,16,8,128]{4,3,2,1,0:T(8,128)S(1)}, f32[2,2,16,8,128]{4,3,2,1,0:T(8,128)S(1)}, u32[]{:S(2)}, u32[]{:S(2)}) %collective-permute-start.27) | collective-permute-done | bytes 262176 | tf_op jit(solution)/shard_map/ppermute | solution.py:427
  119.6 3.7 %collective-permute-start.28 = (f32[2,2,16,8,128]{4,3,2,1,0:T(8,128)S(1)}, f32[2,2,16,8,128]{4,3,2,1,0:T(8,128)S(1)}, u32[]{:S(2)}, u32[]{:S(2)}) collective-permute-start(f32[2,2,16,8,128]{4,3,2,1,0:T(8,128)S(1)} %collective-permute-done.27.near), channel_id=1, source_target_pairs={{0,1},{1,0},{2,3},{3,2},{4,5},{5,4},{6,7},{7,6},{8,9},{9,8},{10,11... | collective-permute-start | bytes 786440 | tf_op jit(solution)/shard_map/ppermute | solution.py:422
  124.9 2.0 %finish.1 = f32[2,2,256,256]{3,2,1,0:T(8,128)} custom-call(f32[4,8,2,8,128]{4,3,2,1,0:T(8,128)S(1)} %heun_a3.1.after.a, f32[4,24,2,8,128]{4,3,2,1,0:T(8,128)S(1)} %heun_b3.1.b, f32[2,16,8,128]{3,2,1,0:T(8,128)S(1)} %get-tuple-element.17.end, f32[2,16,8,128]{3,2,1,0:T(8,128)S(1)} %walk1.1.chained), custom_call_target="tpu_custom_call" | custom-call | tf_op jit(solution)/shard_map/finish/pallas_call | solution.py:405
  (56 shorter events, 25.6 us)
Async XLA Ops:
  6.5 7.4 %collective-permute-start.1 = (f32[6,24,2,8,128]{4,3,2,1,0:T(8,128)S(1)}, f32[6,24,2,8,128]{4,3,2,1,0:T(8,128)S(1)}, u32[]{:S(2)}, u32[]{:S(2)}) collective-permute-start(f32[6,24,2,8,128]{4,3,2,1,0:T(8,128)S(1)} %get-tuple-element.14.refs_0_.refs_4_.refs_7_.pa.refs_5_), channel_id=1, source_target_pairs={{0,1},{1,0},{2,3},{3,2},{4,5},{5,4},{6,7},{7,6},{8,9},{9,8},{10,11... | collective-permute-start | bytes 3538952 | tf_op jit(solution)/shard_map/ppermute | solution.py:422
  7.2 15.9 %collective-permute-start = (f32[6,24,2,8,128]{4,3,2,1,0:T(8,128)S(1)}, f32[6,24,2,8,128]{4,3,2,1,0:T(8,128)S(1)}, u32[]{:S(2)}, u32[]{:S(2)}) collective-permute-start(f32[6,24,2,8,128]{4,3,2,1,0:T(8,128)S(1)} %get-tuple-element.15.refs_3_.refs_6_.ca.refs_4_), channel_id=1, source_target_pairs={{0,31},{1,2},{2,1},{3,4},{4,3},{5,6},{6,5},{7,8},{8,7},{9,10},{10,... | collective-permute-start | bytes 3538952 | tf_op jit(solution)/shard_map/ppermute | solution.py:427
  8.8 20.6 %collective-permute-start.2 = (f32[6,8,2,8,128]{4,3,2,1,0:T(8,128)S(1)}, f32[6,8,2,8,128]{4,3,2,1,0:T(8,128)S(1)}, u32[]{:S(2)}, u32[]{:S(2)}) collective-permute-start(f32[6,8,2,8,128]{4,3,2,1,0:T(8,128)S(1)} %get-tuple-element.16.refs_10_.cb), channel_id=1, source_target_pairs={{0,31},{1,2},{2,1},{3,4},{4,3},{5,6},{6,5},{7,8},{8,7},{9,10},{10,... | collective-permute-start | bytes 1179656 | tf_op jit(solution)/shard_map/ppermute | solution.py:427
  9.0 20.5 %collective-permute-start.3 = (f32[6,8,2,8,128]{4,3,2,1,0:T(8,128)S(1)}, f32[6,8,2,8,128]{4,3,2,1,0:T(8,128)S(1)}, u32[]{:S(2)}, u32[]{:S(2)}) collective-permute-start(f32[6,8,2,8,128]{4,3,2,1,0:T(8,128)S(1)} %get-tuple-element.13.after.refs_3_.refs_11_.pb), channel_id=1, source_target_pairs={{0,1},{1,0},{2,3},{3,2},{4,5},{5,4},{6,7},{7,6},{8,9},{9,8},{10,11... | collective-permute-start | bytes 1179656 | tf_op jit(solution)/shard_map/ppermute | solution.py:422
  24.8 10.5 %collective-permute-start.5 = (f32[4,20,2,8,128]{4,3,2,1,0:T(8,128)S(1)}, f32[4,20,2,8,128]{4,3,2,1,0:T(8,128)S(1)}, u32[]{:S(2)}, u32[]{:S(2)}) collective-permute-start(f32[4,20,2,8,128]{4,3,2,1,0:T(8,128)S(1)} %heun_a0.1.after.refs_0_), channel_id=1, source_target_pairs={{0,1},{1,0},{2,3},{3,2},{4,5},{5,4},{6,7},{7,6},{8,9},{9,8},{10,11... | collective-permute-start | bytes 1966088 | tf_op jit(solution)/shard_map/ppermute | solution.py:422
  29.4 10.3 %collective-permute-start.4 = (f32[4,20,2,8,128]{4,3,2,1,0:T(8,128)S(1)}, f32[4,20,2,8,128]{4,3,2,1,0:T(8,128)S(1)}, u32[]{:S(2)}, u32[]{:S(2)}) collective-permute-start(f32[4,20,2,8,128]{4,3,2,1,0:T(8,128)S(1)} %heun_a0.1.after.refs_0_), channel_id=1, source_target_pairs={{0,31},{1,2},{2,1},{3,4},{4,3},{5,6},{6,5},{7,8},{8,7},{9,10},{10,... | collective-permute-start | bytes 1966088 | tf_op jit(solution)/shard_map/ppermute | solution.py:427
  30.0 13.9 %collective-permute-start.7 = (f32[4,12,2,8,128]{4,3,2,1,0:T(8,128)S(1)}, f32[4,12,2,8,128]{4,3,2,1,0:T(8,128)S(1)}, u32[]{:S(2)}, u32[]{:S(2)}) collective-permute-start(f32[4,12,2,8,128]{4,3,2,1,0:T(8,128)S(1)} %heun_b0.1.after.refs_3_), channel_id=1, source_target_pairs={{0,1},{1,0},{2,3},{3,2},{4,5},{5,4},{6,7},{7,6},{8,9},{9,8},{10,11... | collective-permute-start | bytes 1179656 | tf_op jit(solution)/shard_map/ppermute | solution.py:422
  35.2 8.7 %collective-permute-start.6 = (f32[4,12,2,8,128]{4,3,2,1,0:T(8,128)S(1)}, f32[4,12,2,8,128]{4,3,2,1,0:T(8,128)S(1)}, u32[]{:S(2)}, u32[]{:S(2)}) collective-permute-start(f32[4,12,2,8,128]{4,3,2,1,0:T(8,128)S(1)} %heun_b0.1.after.refs_3_), channel_id=1, source_target_pairs={{0,31},{1,2},{2,1},{3,4},{4,3},{5,6},{6,5},{7,8},{8,7},{9,10},{10,... | collective-permute-start | bytes 1179656 | tf_op jit(solution)/shard_map/ppermute | solution.py:427
  40.7 9.4 %collective-permute-start.9 = (f32[4,16,2,8,128]{4,3,2,1,0:T(8,128)S(1)}, f32[4,16,2,8,128]{4,3,2,1,0:T(8,128)S(1)}, u32[]{:S(2)}, u32[]{:S(2)}) collective-permute-start(f32[4,16,2,8,128]{4,3,2,1,0:T(8,128)S(1)} %heun_a1.1.after.refs_1_.refs_0_), channel_id=1, source_target_pairs={{0,1},{1,0},{2,3},{3,2},{4,5},{5,4},{6,7},{7,6},{8,9},{9,8},{10,11... | collective-permute-start | bytes 1572872 | tf_op jit(solution)/shard_map/ppermute | solution.py:422
  43.9 8.9 %collective-permute-start.8 = (f32[4,16,2,8,128]{4,3,2,1,0:T(8,128)S(1)}, f32[4,16,2,8,128]{4,3,2,1,0:T(8,128)S(1)}, u32[]{:S(2)}, u32[]{:S(2)}) collective-permute-start(f32[4,16,2,8,128]{4,3,2,1,0:T(8,128)S(1)} %heun_a1.1.after.refs_1_.refs_0_), channel_id=1, source_target_pairs={{0,31},{1,2},{2,1},{3,4},{4,3},{5,6},{6,5},{7,8},{8,7},{9,10},{10,... | collective-permute-start | bytes 1572872 | tf_op jit(solution)/shard_map/ppermute | solution.py:427
  44.7 12.6 %collective-permute-start.11 = (f32[4,16,2,8,128]{4,3,2,1,0:T(8,128)S(1)}, f32[4,16,2,8,128]{4,3,2,1,0:T(8,128)S(1)}, u32[]{:S(2)}, u32[]{:S(2)}) collective-permute-start(f32[4,16,2,8,128]{4,3,2,1,0:T(8,128)S(1)} %heun_b1.1.after.refs_3_), channel_id=1, source_target_pairs={{0,1},{1,0},{2,3},{3,2},{4,5},{5,4},{6,7},{7,6},{8,9},{9,8},{10,11... | collective-permute-start | bytes 1572872 | tf_op jit(solution)/shard_map/ppermute | solution.py:422
  49.8 8.9 %collective-permute-start.10 = (f32[4,16,2,8,128]{4,3,2,1,0:T(8,128)S(1)}, f32[4,16,2,8,128]{4,3,2,1,0:T(8,128)S(1)}, u32[]{:S(2)}, u32[]{:S(2)}) collective-permute-start(f32[4,16,2,8,128]{4,3,2,1,0:T(8,128)S(1)} %heun_b1.1.after.refs_3_), channel_id=1, source_target_pairs={{0,31},{1,2},{2,1},{3,4},{4,3},{5,6},{6,5},{7,8},{8,7},{9,10},{10,... | collective-permute-start | bytes 1572872 | tf_op jit(solution)/shard_map/ppermute | solution.py:427
  54.1 9.3 %collective-permute-start.13 = (f32[160,8,128]{2,1,0:T(8,128)S(1)}, f32[160,8,128]{2,1,0:T(8,128)S(1)}, u32[]{:S(2)}, u32[]{:S(2)}) collective-permute-start(f32[160,8,128]{2,1,0:T(8,128)S(1)} %heun_a2.1.after.refs_0_), channel_id=1, source_target_pairs={{0,1},{1,0},{2,3},{3,2},{4,5},{5,4},{6,7},{7,6},{8,9},{9,8},{10,11... | collective-permute-start | bytes 1966088 | tf_op jit(solution)/shard_map/ppermute | solution.py:422
  57.3 10.3 %collective-permute-start.12 = (f32[160,8,128]{2,1,0:T(8,128)S(1)}, f32[160,8,128]{2,1,0:T(8,128)S(1)}, u32[]{:S(2)}, u32[]{:S(2)}) collective-permute-start(f32[160,8,128]{2,1,0:T(8,128)S(1)} %heun_a2.1.after.refs_0_), channel_id=1, source_target_pairs={{0,31},{1,2},{2,1},{3,4},{4,3},{5,6},{6,5},{7,8},{8,7},{9,10},{10,... | collective-permute-start | bytes 1966088 | tf_op jit(solution)/shard_map/ppermute | solution.py:427
  59.6 8.5 %collective-permute-start.15 = (f32[4,20,2,8,128]{4,3,2,1,0:T(8,128)S(1)}, f32[4,20,2,8,128]{4,3,2,1,0:T(8,128)S(1)}, u32[]{:S(2)}, u32[]{:S(2)}) collective-permute-start(f32[4,20,2,8,128]{4,3,2,1,0:T(8,128)S(1)} %heun_b2.1.after.refs_3_), channel_id=1, source_target_pairs={{0,1},{1,0},{2,3},{3,2},{4,5},{5,4},{6,7},{7,6},{8,9},{9,8},{10,11... | collective-permute-start | bytes 1966088 | tf_op jit(solution)/shard_map/ppermute | solution.py:422
  63.4 11.2 %collective-permute-start.14 = (f32[4,20,2,8,128]{4,3,2,1,0:T(8,128)S(1)}, f32[4,20,2,8,128]{4,3,2,1,0:T(8,128)S(1)}, u32[]{:S(2)}, u32[]{:S(2)}) collective-permute-start(f32[4,20,2,8,128]{4,3,2,1,0:T(8,128)S(1)} %heun_b2.1.after.refs_3_), channel_id=1, source_target_pairs={{0,31},{1,2},{2,1},{3,4},{4,3},{5,6},{6,5},{7,8},{8,7},{9,10},{10,... | collective-permute-start | bytes 1966088 | tf_op jit(solution)/shard_map/ppermute | solution.py:427
  75.8 6.9 %collective-permute-start.17 = (f32[2,16,8,128]{3,2,1,0:T(8,128)S(1)}, f32[2,16,8,128]{3,2,1,0:T(8,128)S(1)}, u32[]{:S(2)}, u32[]{:S(2)}) collective-permute-start(f32[2,16,8,128]{3,2,1,0:T(8,128)S(1)} %get-tuple-element.19.refs_0_), channel_id=1, source_target_pairs={{0,96},{1,97},{2,98},{3,99},{4,100},{5,101},{6,102},{7,103},{8,104... | collective-permute-start | bytes 393224 | tf_op jit(solution)/shard_map/ppermute | solution.py:432
  77.1 9.9 %collective-permute-start.16 = (f32[2,16,8,128]{3,2,1,0:T(8,128)S(1)}, f32[2,16,8,128]{3,2,1,0:T(8,128)S(1)}, u32[]{:S(2)}, u32[]{:S(2)}) collective-permute-start(f32[2,16,8,128]{3,2,1,0:T(8,128)S(1)} %get-tuple-element.18.r_cross), channel_id=1, source_target_pairs={{0,1},{1,0},{2,3},{3,2},{4,5},{5,4},{6,7},{7,6},{8,9},{9,8},{10,11... | collective-permute-start | bytes 393224 | tf_op jit(solution)/shard_map/ppermute | solution.py:422
  88.0 5.9 %collective-permute-start.19 = (f32[2,2,16,8,128]{4,3,2,1,0:T(8,128)S(1)}, f32[2,2,16,8,128]{4,3,2,1,0:T(8,128)S(1)}, u32[]{:S(2)}, u32[]{:S(2)}) collective-permute-start(f32[2,2,16,8,128]{4,3,2,1,0:T(8,128)S(1)} %pack.1.both), channel_id=1, source_target_pairs={{0,31},{1,2},{2,1},{3,4},{4,3},{5,6},{6,5},{7,8},{8,7},{9,10},{10,... | collective-permute-start | bytes 786440 | tf_op jit(solution)/shard_map/ppermute | solution.py:427
  88.1 9.5 %collective-permute-start.21 = (f32[2,16,8,128]{3,2,1,0:T(8,128)S(1)}, f32[2,16,8,128]{3,2,1,0:T(8,128)S(1)}, u32[]{:S(2)}, u32[]{:S(2)}) collective-permute-start(f32[2,16,8,128]{3,2,1,0:T(8,128)S(1)} %get-tuple-element.19.refs_0_), channel_id=1, source_target_pairs={{0,64},{32,96},{1,65},{33,97},{2,66},{34,98},{3,67},{35,99},{4,68}... | collective-permute-start | bytes 393224 | tf_op jit(solution)/shard_map/ppermute | solution.py:432
  93.9 7.8 %collective-permute-start.20 = (f32[2,2,16,8,128]{4,3,2,1,0:T(8,128)S(1)}, f32[2,2,16,8,128]{4,3,2,1,0:T(8,128)S(1)}, u32[]{:S(2)}, u32[]{:S(2)}) collective-permute-start(f32[2,2,16,8,128]{4,3,2,1,0:T(8,128)S(1)} %collective-permute-done.19.near), channel_id=1, source_target_pairs={{0,1},{1,0},{2,3},{3,2},{4,5},{5,4},{6,7},{7,6},{8,9},{9,8},{10,11... | collective-permute-start | bytes 786440 | tf_op jit(solution)/shard_map/ppermute | solution.py:422
  102.3 5.9 %collective-permute-start.23 = (f32[2,2,16,8,128]{4,3,2,1,0:T(8,128)S(1)}, f32[2,2,16,8,128]{4,3,2,1,0:T(8,128)S(1)}, u32[]{:S(2)}, u32[]{:S(2)}) collective-permute-start(f32[2,2,16,8,128]{4,3,2,1,0:T(8,128)S(1)} %walk3.1.both), channel_id=1, source_target_pairs={{0,31},{1,2},{2,1},{3,4},{4,3},{5,6},{6,5},{7,8},{8,7},{9,10},{10,... | collective-permute-start | bytes 786440 | tf_op jit(solution)/shard_map/ppermute | solution.py:427
  102.4 9.5 %collective-permute-start.25 = (f32[2,16,8,128]{3,2,1,0:T(8,128)S(1)}, f32[2,16,8,128]{3,2,1,0:T(8,128)S(1)}, u32[]{:S(2)}, u32[]{:S(2)}) collective-permute-start(f32[2,16,8,128]{3,2,1,0:T(8,128)S(1)} %get-tuple-element.19.refs_0_), channel_id=1, source_target_pairs={{0,32},{32,64},{64,96},{1,33},{33,65},{65,97},{2,34},{34,66},{66,9... | collective-permute-start | bytes 393224 | tf_op jit(solution)/shard_map/ppermute | solution.py:432
  113.7 5.9 %collective-permute-start.27 = (f32[2,2,16,8,128]{4,3,2,1,0:T(8,128)S(1)}, f32[2,2,16,8,128]{4,3,2,1,0:T(8,128)S(1)}, u32[]{:S(2)}, u32[]{:S(2)}) collective-permute-start(f32[2,2,16,8,128]{4,3,2,1,0:T(8,128)S(1)} %walk2.1.both), channel_id=1, source_target_pairs={{0,31},{1,2},{2,1},{3,4},{4,3},{5,6},{6,5},{7,8},{8,7},{9,10},{10,... | collective-permute-start | bytes 786440 | tf_op jit(solution)/shard_map/ppermute | solution.py:427
  (8 other events, 23.9 us)

commit v4 on v3

v4 whole, which is shorter than its diff:
```python
import functools

import jax
import jax.numpy as jnp
from jax import lax
from jax.experimental import pallas as pl
from jax.experimental.pallas import tpu as pltpu
from jax.sharding import PartitionSpec as P

FSTEPS = 4
CSTEPS = 2
DU = 0.16
DV = 0.08
CUTS = (0, 18, 26, 32)
TILES = 32
STRIDE = 33
CHUNKS = len(CUTS) - 1
F32 = jnp.float32
UNROLL = 8
VMEM_LIMIT = 16 * 1024 * 1024

VM = pl.BlockSpec(memory_space=pltpu.VMEM)
ANY = pl.BlockSpec(memory_space=pl.ANY)
PARAMS = pltpu.CompilerParams(vmem_limit_bytes=VMEM_LIMIT)
COARSE = (2, 16, 8, 128)
PACK_COST = 10**10
COST = ((2 * 10**9,) * 4, (2 * 10**9,) * 2 + (4 * 10**9,) * 2, (2 * 10**9,) * 4)
FLAT = 3
TAIL = 4 * (CUTS[1] - 4 * FLAT) * 2


def splitter(transposed):
    r = lax.broadcasted_iota(jnp.int32, (256, 256), 0)
    c = lax.broadcasted_iota(jnp.int32, (256, 256), 1)
    if transposed:
        r, c = c, r
    return jnp.where(r == 2 * (c % 128) + c // 128, 1.0, 0.0).astype(jnp.bfloat16)


def permuted(x, mat):
    high = x.astype(jnp.bfloat16)
    rest = x - high.astype(F32)
    mid = rest.astype(jnp.bfloat16)
    low = (rest - mid.astype(F32)).astype(jnp.bfloat16)
    dot = lambda p: jnp.dot(p, mat, preferred_element_type=F32)
    return dot(high) + (dot(mid) + dot(low))


def odd():
    return lax.rem(lax.axis_index("space"), 2)


def chunk_of(v):
    return max(c for c in range(CHUNKS) if CUTS[c] <= v)


def scatter(plane, rows, mat, targets):
    done = permuted(plane, mat)
    for band in range(8):
        for h in range(2):
            rows[h, pl.ds(STRIDE * band, TILES), :] = done[TILES * band:TILES * (band + 1), 128 * h:128 * (h + 1)]
    for i in range(TILES):
        c = chunk_of(i)
        for h in range(2):
            tile = rows[h, pl.ds(i, 8, stride=STRIDE), :]
            for refs, q in targets:
                refs[c][q, i - CUTS[c], h] = tile


def prep_kernel(x, *refs):
    pair, cross, rows = refs[:CHUNKS], refs[CHUNKS:2 * CHUNKS], refs[-1]
    flip = odd()
    mat = splitter(False)
    for sp in range(2):
        for q in range(2):
            k = 2 * sp + q
            scatter(x[sp, q ^ flip], rows.at[k], mat, [(pair, k), (cross, k)])


def prep_rates_kernel(feed, kill, *refs):
    pair, cross, rows = refs[2 * CHUNKS:3 * CHUNKS], refs[3 * CHUNKS:4 * CHUNKS], refs[-1]
    flip = odd()
    mat = splitter(False)
    for q, target in ((0, cross), (1, pair)):
        f = feed[q ^ flip]
        scatter(f, rows.at[2 * q], mat, [(target, 4)])
        scatter(0.52 - (f + kill[q ^ flip]), rows.at[2 * q + 1], mat, [(target, 5)])


def prep(x, feed, kill):
    shapes = [jax.ShapeDtypeStruct((6, CUTS[c + 1] - CUTS[c], 2, 8, 128), F32) for c in range(CHUNKS)] * 2
    scratch = [pltpu.VMEM((4, 2, 8 * STRIDE, 128), F32)]
    sent = pl.pallas_call(
        prep_kernel,
        out_shape=shapes,
        in_specs=[VM],
        out_specs=[VM] * (2 * CHUNKS),
        scratch_shapes=scratch,
        compiler_params=PARAMS,
        name="prep",
    )(x)
    return pl.pallas_call(
        prep_rates_kernel,
        out_shape=shapes,
        in_specs=[VM, VM] + [VM] * (2 * CHUNKS),
        out_specs=[VM] * (2 * CHUNKS),
        scratch_shapes=scratch,
        input_output_aliases={2 + i: i for i in range(2 * CHUNKS)},
        compiler_params=PARAMS,
        name="prep_rates",
    )(feed, kill, *sent)


LINE = ((1, 1), (1, 0), (0, 0), (0, 1), (2, 1), (2, 0))


def runs(lo, hi, key):
    out = []
    for v in range(lo, hi):
        k = key(v)
        if out and out[-1][2] == k:
            out[-1][1] = v + 1
        else:
            out.append([v, v + 1, k])
    return out


def over(lo, hi, key, work):
    for start, stop, k in runs(lo, hi, key):
        if stop - start < 4:
            for v in range(start, stop):
                work(v, k)
        else:
            @pl.loop(start, stop, unroll=min(UNROLL, stop - start))
            def _(v):
                work(v, k)


def moved(x, rolled):
    return pltpu.roll(x, 7, 0) if rolled else x


def beside(other, h):
    return other + pltpu.roll(other, 1 if h == 0 else 127, 1)


def edges(step, c):
    lo = CUTS[c] + (2 * step if c == 0 else -2 * step)
    return lo, CUTS[c + 1] + (2 * step if c == CHUNKS - 1 else -2 * step)


def heun_kernel(step, c, after, *refs):
    refs = list(refs)
    extra = refs.pop(0) if step == FLAT - 1 and c == 0 else None
    state = [refs[3 * g:3 * g + 3] for g in range(c + 1)]
    refs = refs[3 * (c + 1):]
    rate = [refs[4 * g:4 * g + 4] for g in range(c + 1)]
    out, mids = refs[-2:]
    lo, hi = edges(step + 1, c)
    lo, hi = lo - 2, hi + 2
    total = hi - lo

    def find_state(v):
        for g in range(CHUNKS):
            start, stop = edges(step, g)
            if v < stop:
                return g, -start, False
        return 0, -TILES - 2 * step, True

    def find_rate(v):
        if v < TILES:
            return chunk_of(v), -CUTS[chunk_of(v)], False
        return 0, -TILES, True

    def cell(sp, p, v, h, at):
        g, off, rolled = at
        source, plane = LINE[p]
        ref, q = state[g][source], 2 * sp + plane
        if g == 0 and step == FLAT:
            return moved(ref[(q * (CUTS[1] - 4 * step) + v + off) * 2 + h], rolled)
        return moved(ref[q, v + off, h], rolled)

    def put(q, i, h, x):
        if extra is None:
            out[q, i, h] = x
        else:
            out[(q * (total - 4) + i) * 2 + h] = x

    def coef(k, place, v, h, at):
        g, off, rolled = at
        return moved(rate[g][(2, 0, 1, 3)[place]][4 + k, v + off, h], rolled)

    def ahead(u, v, near_u, near_v, f, cv):
        uvv = u * v * v
        return DU * near_u + (1.0 - 6.0 * DU) * u + f * (1.0 - u) - uvv, DV * near_v + cv * v + uvv

    def first(v, key):
        below, here, above, at = key
        c = [[cell(sp, p, v, h, here) for h in range(2)] for sp in range(2) for p in range(6)]
        for p in range(1, 5):
            for h in range(2):
                near = []
                for sp in range(2):
                    i = 6 * sp + p
                    s = cell(sp, p, v - 1, h, below) + cell(sp, p, v + 1, h, above)
                    near.append(beside(c[i][1 - h], h) + (s + (c[i - 1][h] + c[i + 1][h])))
                nu, nv = ahead(c[p][h], c[6 + p][h], *near, coef(0, p - 1, v, h, at), coef(1, p - 1, v, h, at))
                mids[0, p - 1, v - lo, h] = nu
                mids[1, p - 1, v - lo, h] = nv

    def then(v, key):
        here, at = key
        c = [[mids[sp, p, v - lo, h] for h in range(2)] for sp in range(2) for p in range(4)]
        for p in range(1, 3):
            for h in range(2):
                near = []
                for sp in range(2):
                    i = 4 * sp + p
                    s = mids[sp, p, v - lo - 1, h] + mids[sp, p, v - lo + 1, h]
                    near.append(beside(c[i][1 - h], h) + (s + (c[i - 1][h] + c[i + 1][h])))
                nu, nv = ahead(c[p][h], c[4 + p][h], *near, coef(0, p, v, h, at), coef(1, p, v, h, at))
                put(p - 1, v - lo - 2, h, 0.5 * (cell(0, p + 1, v, h, here) + nu))
                put(2 + p - 1, v - lo - 2, h, 0.5 * (cell(1, p + 1, v, h, here) + nv))

    if extra is not None:
        for k in range(4):
            for j in range(16):
                out[TAIL + 16 * k + j] = extra[k, j]

    over(lo + 1, hi - 1, lambda v: (find_state(v - 1), find_state(v), find_state(v + 1), find_rate(v)), first)
    over(lo + 2, hi - 2, lambda v: (find_state(v), find_rate(v)), then)


def heun(step, c, state, rate, after, extra=None):
    lo, hi = edges(step + 1, c)
    ins = [r for g in state[:c + 1] for r in g] + [r for g in rate[:c + 1] for r in g]
    shape = (4, hi - lo, 2, 8, 128)
    if extra is not None:
        ins = [extra] + ins
        shape = (TAIL + 64, 8, 128)
    return pl.pallas_call(
        functools.partial(heun_kernel, step, c),
        out_shape=jax.ShapeDtypeStruct(shape, F32),
        in_specs=[ANY] + [VM] * len(ins),
        out_specs=VM,
        scratch_shapes=[pltpu.VMEM((2, 4, hi - lo + 4, 2, 8, 128), F32)],
        compiler_params=PARAMS,
        cost_estimate=pl.CostEstimate(flops=COST[c][step], bytes_accessed=1000, transcendentals=0),
        name="heun_%s%d" % ("abcd"[c], step),
    )(after, *ins)


def mean_tile(tiles):
    s = [tiles[i] + tiles[i + 1] for i in range(0, 8, 2)]
    return 0.125 * ((s[0] + s[1]) + (s[2] + s[3]))


def mean_of(chunks, j, rows):
    c = chunk_of(2 * j)
    return mean_tile([chunks[c][q, 2 * j + i - CUTS[c], h] for q in rows for i in range(2) for h in range(2)])


def euler(get, cf, ccv, j):
    new = []
    for sp in range(2):
        c = get(0, sp, j)
        up = get(0, sp, j + 1) if j < 15 else pltpu.roll(get(0, sp, 0), 7, 0)
        down = get(0, sp, j - 1) if j else pltpu.roll(get(0, sp, 15), 1, 0)
        s = pltpu.roll(c, 1, 1) + pltpu.roll(c, 127, 1) + (up + down)
        new.append((c, s + (get(-1, sp, j) + get(1, sp, j))))
    (u, su), (v, sv) = new
    uvv = u * v * v
    nu = u + 2.0 * (0.25 * DU * (su - 6.0 * u) - uvv + cf * (1.0 - u))
    nv = v + 2.0 * (0.25 * DV * (sv - 6.0 * v) + uvv - ccv * v)
    return nu, nv


def own_first_kernel(*refs):
    pair, cross, got_pair, got_cross = [refs[CHUNKS * i:CHUNKS * (i + 1)] for i in range(4)]
    out, line = refs[4 * CHUNKS:]
    for j in range(16):
        for sp in range(2):
            rows = (2 * sp, 2 * sp + 1)
            line[0, sp, j] = mean_of(got_cross, j, rows)
            line[1, sp, j] = mean_of(pair, j, rows)
            line[2, sp, j] = mean_of(got_pair, j, rows)
        for k in range(2):
            c = chunk_of(2 * j)
            m = mean_tile([r[c][4 + k, 2 * j + i - CUTS[c], h] for r in (cross, pair) for i in range(2) for h in range(2)])
            out[2 + k, j] = m if k == 0 else 0.52 - m
    for j in range(16):
        out[0, j], out[1, j] = euler(lambda d, sp, i: line[1 + d, sp, i], out[2, j], out[3, j], j)


def own_first(*refs):
    return pl.pallas_call(
        own_first_kernel,
        out_shape=jax.ShapeDtypeStruct((4, 16, 8, 128), F32),
        in_specs=[VM] * (4 * CHUNKS),
        out_specs=VM,
        scratch_shapes=[pltpu.VMEM((3,) + COARSE, F32)],
        compiler_params=PARAMS,
        name="own_first",
    )(*refs)


def fine_tile(ends, q, v, h):
    rolled = v < 2 * FSTEPS
    v = v + TILES if rolled else v
    c = min(c for c in range(CHUNKS) if v < edges(FSTEPS, c)[1])
    x = ends[c][q, v - edges(FSTEPS, c)[0], h]
    return pltpu.roll(x, 1, 0) if rolled else x


def tails_kernel(after, cross, pair, cross_rate, pair_rate):
    for k in range(2):
        for j in range(16):
            cross_rate[k, j] = cross[TAIL + 16 * (2 + k) + j]
            pair_rate[k, j] = pair[TAIL + 16 * (2 + k) + j]


def tails(cross, pair, after):
    shape = jax.ShapeDtypeStruct(COARSE, F32)
    return pl.pallas_call(
        tails_kernel,
        out_shape=[shape] * 2,
        in_specs=[ANY, VM, VM],
        out_specs=[VM] * 2,
        compiler_params=PARAMS,
        name="tails",
    )(after, cross, pair)


def jump_kernel(here, cross, pair, *refs):
    ends, (end, send) = refs[:CHUNKS], refs[CHUNKS:]
    first = lax.axis_index("tm") == 0

    def get(d, sp, j):
        return here[sp, j] if d == 0 else (cross if d < 0 else pair)[TAIL + 16 * sp + j]

    for j in range(16):
        g = euler(get, here[2, j], here[3, j], j)
        for sp in range(2):
            m = mean_tile([fine_tile(ends, 2 * sp + q, 2 * j + i, h) for q in range(2) for i in range(2) for h in range(2)])
            end[sp, j] = m
            jump = m - g[sp]
            send[sp, j] = jnp.where(first, g[sp] + jump, jump)


def jump_of(ends, here, cross, pair):
    shape = jax.ShapeDtypeStruct(COARSE, F32)
    return pl.pallas_call(
        jump_kernel,
        out_shape=[shape] * 2,
        in_specs=[VM] * (3 + CHUNKS),
        out_specs=[VM] * 2,
        compiler_params=PARAMS,
        name="jump",
    )(here, cross, pair, *ends)


def pack_kernel(after, one, other, out):
    out[0] = one[...]
    out[1] = other[...]


def pack(one, other, after, flops=1000):
    return pl.pallas_call(
        pack_kernel,
        out_shape=jax.ShapeDtypeStruct((2,) + COARSE, F32),
        in_specs=[ANY, VM, VM],
        out_specs=VM,
        compiler_params=PARAMS,
        cost_estimate=pl.CostEstimate(flops=flops, bytes_accessed=1000, transcendentals=0),
        name="pack",
    )(after, one, other)


def walk_kernel(least, both, near, far, q_own, r_cross, r_pair, r_far, jumps, out, mid):
    line = ((near, 1), (near, 0), (both, 0), (both, 1), (far, 0), (far, 1))
    rates = ((r_cross, 0), (q_own, 2), (r_pair, 0), (r_far, 0))
    counts = lax.axis_index("tm") >= least
    for p in range(1, 5):
        q, k = rates[p - 1]
        for j in range(16):
            new = euler(lambda d, sp, i: line[p + d][0][line[p + d][1], sp, i], q[k, j], q[k + 1, j], j)
            mid[p - 1, 0, j], mid[p - 1, 1, j] = new
    single = len(jumps.shape) == 3 + 1
    for n in range(1 if single else 2):
        q, k = rates[n + 1]
        for j in range(16):
            new = euler(lambda d, sp, i: mid[n + 1 + d, sp, i], q[k, j], q[k + 1, j], j)
            for sp in range(2):
                x = jnp.where(counts, new[sp], 0.0)
                if single:
                    out[sp, j] = x + jumps[sp, j]
                else:
                    out[n, sp, j] = x + jumps[n, sp, j]


def walk(least, both, near, far, rates, jumps):
    return pl.pallas_call(
        functools.partial(walk_kernel, least),
        out_shape=jax.ShapeDtypeStruct(jumps.shape, F32),
        in_specs=[VM] * 8,
        out_specs=VM,
        scratch_shapes=[pltpu.VMEM((4,) + COARSE, F32)],
        compiler_params=PARAMS,
        name="walk%d" % least,
    )(both, near, far, *rates, jumps)


def finish_kernel(end, chained, *refs):
    ends, (out, rows, done, sems) = refs[:CHUNKS], refs[CHUNKS:]
    mat = splitter(True)
    flip = odd()
    copies = []
    for sp in range(2):
        shift = [chained[sp, j] - end[sp, j] for j in range(16)]
        for q in range(2):
            k = 2 * sp + q
            for v in range(TILES):
                for h in range(2):
                    rows[k, h, pl.ds(v, 8, stride=STRIDE), :] = fine_tile(ends, k, v, h) + shift[v // 2]
            halves = [jnp.concatenate([rows[k, h, pl.ds(STRIDE * band, TILES), :] for band in range(8)], axis=0) for h in range(2)]
            done[k] = permuted(jnp.concatenate(halves, axis=1), mat)
            copies.append(pltpu.make_async_copy(done.at[k], out.at[sp, q ^ flip], sems.at[k]))
            copies[-1].start()
    for c in copies:
        c.wait()


def finish(ends, end, chained):
    return pl.pallas_call(
        finish_kernel,
        out_shape=jax.ShapeDtypeStruct((2, 2, 256, 256), F32),
        in_specs=[VM] * (2 + CHUNKS),
        out_specs=pl.BlockSpec(memory_space=pltpu.HBM),
        scratch_shapes=[
            pltpu.VMEM((4, 2, 8 * STRIDE, 128), F32),
            pltpu.VMEM((4, 256, 256), F32),
            pltpu.SemaphoreType.DMA((4,)),
        ],
        compiler_params=PARAMS,
        name="finish",
    )(end, chained, *ends)


def swap_pair(x):
    n = lax.axis_size("space")
    return lax.ppermute(x, "space", [(i, i ^ 1) for i in range(n)])


def swap_cross(x):
    n = lax.axis_size("space")
    return lax.ppermute(x, "space", [(i, (i + 1) % n if i % 2 else (i - 1) % n) for i in range(n)])


def later(x, distance):
    n = lax.axis_size("tm")
    return lax.ppermute(x, "tm", [(i, i + distance) for i in range(n - distance)])


def body(slice_starts, feed, kill):
    sent = prep(slice_starts[0], feed, kill)
    pair, cross = sent[:CHUNKS], sent[CHUNKS:]
    got = [(swap_pair(p), swap_cross(c)) for p, c in zip(pair, cross)]
    got_pair, got_cross = [g[0] for g in got], [g[1] for g in got]
    rate = list(zip(cross, pair, got_cross, got_pair))
    state = list(zip(pair, got_cross, got_pair))
    own = own_first(*pair, *cross, *got_pair, *got_cross)
    before = pair[0]
    for step in range(FSTEPS):
        last = step == FSTEPS - 1
        made = []
        for c in range(CHUNKS):
            if last and c == CHUNKS - 1:
                tail = state[0][1:]
                rate_cross, rate_pair = tails(*tail, before)
                before = rate_far = swap_pair(rate_cross)
            new = heun(step, c, state, rate, before, own if step == FLAT - 1 and c == 0 else None)
            before = new
            made.append((new,) if last else (new, swap_cross(new), swap_pair(new)))
        state = made
    ends = [m[0] for m in state]
    end, send = jump_of(ends, own, *tail)
    rates = (own, rate_cross, rate_pair, rate_far)
    from3, from2, from1 = later(send, 3), later(send, 2), later(send, 1)
    both = pack(from3, swap_pair(from3), rate_far)
    jumps2 = pack(from2, swap_pair(from2), rate_far, PACK_COST)
    jumps1 = pack(from1, swap_pair(from1), rate_far, PACK_COST)
    for least, jumps in ((3, jumps2), (2, jumps1), (1, send)):
        near = swap_cross(both)
        far = swap_pair(near)
        both = walk(least, both, near, far, rates, jumps)
    return finish(ends, end, both)[None]


def solution(mesh):
    in_specs = (P("tm", None, "space", None, None), P("space", None, None), P("space", None, None))
    out_specs = P("tm", None, "space", None, None)
    return jax.shard_map(body, mesh=mesh, in_specs=in_specs, out_specs=out_specs, check_vma=False)
```

time: 127 us -> 115 us (0.906)
  waiting for transfers between devices: 50.2 us -> 36 us
  starting transfers between devices: 58.4 us -> 65.1 us
  Pallas kernels: 14.8 us -> 11.9 us
  local copies, waits for them, and re-layouts: 3.31 us -> 1.7 us
    ppermute x11 -> x15, waiting for transfers between devices: 43.3 us -> 13.7 us  [swap_cross(): lax.ppermute(x, 'space', [(i, (i + 1) % n if i % 2 else (i - 1) % n) for...]
    ppermute x3, waiting for transfers between devices: 2.43 us -> 16.2 us  [later(): lax.ppermute(x, 'tm', [(i, i + distance) for i in range(n - distance)])]
    ppermute x15 -> x19, starting transfers between devices: 52.5 us -> 56.1 us  [swap_pair(): return lax.ppermute(x, 'space', [(i, i ^ 1) for i in range(n)])]
    ppermute x11 -> x15, starting transfers between devices: 2.02 us -> 5.19 us  [swap_cross(): lax.ppermute(x, 'space', [(i, (i + 1) % n if i % 2 else (i - 1) % n) for...]
    pallas_call x10 -> x16, Pallas kernels: 11 us -> 8.58 us  [the longest x12 7.03 us: heun(): pl.pallas_call(functools.partial(heun_kernel, step, c), out_shape=jax.Sha...]
    unnamed x6, local copies, waits for them, and re-layouts: 3.31 us -> 1.7 us
    ppermute x15 -> x19, waiting for transfers between devices: 4.5 us -> 5.97 us  [swap_pair(): return lax.ppermute(x, 'space', [(i, i ^ 1) for i in range(n)])]
  transfers between devices with their start and end apart: 29 -> 37, of which waited for: 15 -> 15; matrix products, arithmetic and copies ran while one was open for 0% -> 0% of each run, Pallas kernels for 5% -> 6%
where the time goes in v4:
time: 115 us
  starting transfers between devices  65.1 us (57%)
  waiting for transfers between devices  36 us (31%)
  Pallas kernels  11.9 us (10%)
  local copies, waits for them, and re-layouts  1.7 us (1%)
    ppermute x19, starting transfers between devices, swap_pair(): return lax.ppermute(x, 'space', [(i, i ^ 1) for i in range(n)])  56.1 us
    ppermute x3, waiting for transfers between devices, later(): lax.ppermute(x, 'tm', [(i, i + distance) for i in range(n - distance)])  16.2 us
    ppermute x15, waiting for transfers between devices, swap_cross(): lax.ppermute(x, 'space', [(i, (i + 1) % n if i % 2 else (i - 1) % n) for...  13.7 us
    pallas_call x12, Pallas kernels, heun(): pl.pallas_call(functools.partial(heun_kernel, step, c), out_shape=jax.Sha...  7.03 us
    ppermute x19, waiting for transfers between devices, swap_pair(): return lax.ppermute(x, 'space', [(i, i ^ 1) for i in range(n)])  5.97 us
    ppermute x15, starting transfers between devices, swap_cross(): lax.ppermute(x, 'space', [(i, (i + 1) % n if i % 2 else (i - 1) % n) for...  5.19 us
    ppermute x3, starting transfers between devices, later(): lax.ppermute(x, 'tm', [(i, i + distance) for i in range(n - distance)])  3.88 us
  transfers between devices with their start and end apart: 37, of which 15 were waited for; matrix products, arithmetic and copies ran while one was open for 0% of the time, Pallas kernels for 6%

profile of v4, /device:TPU:7, one launch (start us, length us, event | category | flops | bytes accessed | tf_op | source)
XLA Modules:
  0.0 115.2 jit_solution(2622612522863054290)
XLA Ops:
  3.8 1.6 %collective-permute-start.3 = (f32[6,18,2,8,128]{4,3,2,1,0:T(8,128)S(1)}, f32[6,18,2,8,128]{4,3,2,1,0:T(8,128)S(1)}, u32[]{:S(2)}, u32[]{:S(2)}) collective-permute-start(f32[6,18,2,8,128]{4,3,2,1,0:T(8,128)S(1)} %get-tuple-element.30.refs_3_.refs_6_.refs_9_.refs_4_), channel_id=1, source_target_pairs={{0,31},{1,2},{2,1},{3,4},{4,3},{5,6},{6,5},{7,8},{8,7},{9,10},{10,... | collective-permute-start | bytes 2654216 | tf_op jit(solution)/shard_map/ppermute | solution.py:456
  5.5 5.0 %collective-permute-start.1 = (f32[6,8,2,8,128]{4,3,2,1,0:T(8,128)S(1)}, f32[6,8,2,8,128]{4,3,2,1,0:T(8,128)S(1)}, u32[]{:S(2)}, u32[]{:S(2)}) collective-permute-start(f32[6,8,2,8,128]{4,3,2,1,0:T(8,128)S(1)} %get-tuple-element.28.refs_1_.refs_3_.refs_11_.refs_14_), channel_id=1, source_target_pairs={{0,1},{1,0},{2,3},{3,2},{4,5},{5,4},{6,7},{7,6},{8,9},{9,8},{10,11... | collective-permute-start | bytes 1179656 | tf_op jit(solution)/shard_map/ppermute | solution.py:451
  12.2 4.4 %collective-permute-done.3.refs_9_.refs_1_.refs_5_.refs_8_.refs_11_.refs_6_ = f32[6,18,2,8,128]{4,3,2,1,0:T(8,128)S(1)} collective-permute-done((f32[6,18,2,8,128]{4,3,2,1,0:T(8,128)S(1)}, f32[6,18,2,8,128]{4,3,2,1,0:T(8,128)S(1)}, u32[]{:S(2)}, u32[]{:S(2)}) %collective-permute-start.3) | collective-permute-done | bytes 884768 | tf_op jit(solution)/shard_map/ppermute | solution.py:456
  17.7 1.4 %collective-permute-start.6 = (f32[4,14,2,8,128]{4,3,2,1,0:T(8,128)S(1)}, f32[4,14,2,8,128]{4,3,2,1,0:T(8,128)S(1)}, u32[]{:S(2)}, u32[]{:S(2)}) collective-permute-start(f32[4,14,2,8,128]{4,3,2,1,0:T(8,128)S(1)} %heun_a0.1.after.refs_0_), channel_id=1, source_target_pairs={{0,31},{1,2},{2,1},{3,4},{4,3},{5,6},{6,5},{7,8},{8,7},{9,10},{10,... | collective-permute-start | bytes 1376264 | tf_op jit(solution)/shard_map/ppermute | solution.py:456
  19.1 8.3 %collective-permute-start.7 = (f32[4,14,2,8,128]{4,3,2,1,0:T(8,128)S(1)}, f32[4,14,2,8,128]{4,3,2,1,0:T(8,128)S(1)}, u32[]{:S(2)}, u32[]{:S(2)}) collective-permute-start(f32[4,14,2,8,128]{4,3,2,1,0:T(8,128)S(1)} %heun_a0.1.after.refs_0_), channel_id=1, source_target_pairs={{0,1},{1,0},{2,3},{3,2},{4,5},{5,4},{6,7},{7,6},{8,9},{9,8},{10,11... | collective-permute-start | bytes 1376264 | tf_op jit(solution)/shard_map/ppermute | solution.py:451
  28.0 3.0 %collective-permute-start.9 = (f32[4,8,2,8,128]{4,3,2,1,0:T(8,128)S(1)}, f32[4,8,2,8,128]{4,3,2,1,0:T(8,128)S(1)}, u32[]{:S(2)}, u32[]{:S(2)}) collective-permute-start(f32[4,8,2,8,128]{4,3,2,1,0:T(8,128)S(1)} %heun_b0.1.after.refs_3_), channel_id=1, source_target_pairs={{0,1},{1,0},{2,3},{3,2},{4,5},{5,4},{6,7},{7,6},{8,9},{9,8},{10,11... | collective-permute-start | bytes 786440 | tf_op jit(solution)/shard_map/ppermute | solution.py:451
  31.8 2.7 %collective-permute-start.11 = (f32[4,10,2,8,128]{4,3,2,1,0:T(8,128)S(1)}, f32[4,10,2,8,128]{4,3,2,1,0:T(8,128)S(1)}, u32[]{:S(2)}, u32[]{:S(2)}) collective-permute-start(f32[4,10,2,8,128]{4,3,2,1,0:T(8,128)S(1)} %heun_c0.1.after.refs_6_), channel_id=1, source_target_pairs={{0,1},{1,0},{2,3},{3,2},{4,5},{5,4},{6,7},{7,6},{8,9},{9,8},{10,11... | collective-permute-start | bytes 983048 | tf_op jit(solution)/shard_map/ppermute | solution.py:451
  35.6 4.1 %collective-permute-start.13 = (f32[4,10,2,8,128]{4,3,2,1,0:T(8,128)S(1)}, f32[4,10,2,8,128]{4,3,2,1,0:T(8,128)S(1)}, u32[]{:S(2)}, u32[]{:S(2)}) collective-permute-start(f32[4,10,2,8,128]{4,3,2,1,0:T(8,128)S(1)} %heun_a1.1.after.refs_1_.refs_0_), channel_id=1, source_target_pairs={{0,1},{1,0},{2,3},{3,2},{4,5},{5,4},{6,7},{7,6},{8,9},{9,8},{10,11... | collective-permute-start | bytes 983048 | tf_op jit(solution)/shard_map/ppermute | solution.py:451
  40.2 1.8 %collective-permute-start.17 = (f32[4,8,2,8,128]{4,3,2,1,0:T(8,128)S(1)}, f32[4,8,2,8,128]{4,3,2,1,0:T(8,128)S(1)}, u32[]{:S(2)}, u32[]{:S(2)}) collective-permute-start(f32[4,8,2,8,128]{4,3,2,1,0:T(8,128)S(1)} %heun_b1.1.after.refs_3_), channel_id=1, source_target_pairs={{0,1},{1,0},{2,3},{3,2},{4,5},{5,4},{6,7},{7,6},{8,9},{9,8},{10,11... | collective-permute-start | bytes 786440 | tf_op jit(solution)/shard_map/ppermute | solution.py:451
  42.7 3.3 %collective-permute-start.19 = (f32[4,14,2,8,128]{4,3,2,1,0:T(8,128)S(1)}, f32[4,14,2,8,128]{4,3,2,1,0:T(8,128)S(1)}, u32[]{:S(2)}, u32[]{:S(2)}) collective-permute-start(f32[4,14,2,8,128]{4,3,2,1,0:T(8,128)S(1)} %heun_c1.1.after.refs_6_), channel_id=1, source_target_pairs={{0,1},{1,0},{2,3},{3,2},{4,5},{5,4},{6,7},{7,6},{8,9},{9,8},{10,11... | collective-permute-start | bytes 1376264 | tf_op jit(solution)/shard_map/ppermute | solution.py:451
  46.4 3.5 %collective-permute-start.15 = (f32[112,8,128]{2,1,0:T(8,128)S(1)}, f32[112,8,128]{2,1,0:T(8,128)S(1)}, u32[]{:S(2)}, u32[]{:S(2)}) collective-permute-start(f32[112,8,128]{2,1,0:T(8,128)S(1)} %heun_a2.1.after.refs_0_), channel_id=1, source_target_pairs={{0,1},{1,0},{2,3},{3,2},{4,5},{5,4},{6,7},{7,6},{8,9},{9,8},{10,11... | collective-permute-start | bytes 1376264 | tf_op jit(solution)/shard_map/ppermute | solution.py:451
  51.2 3.0 %collective-permute-start.21 = (f32[4,8,2,8,128]{4,3,2,1,0:T(8,128)S(1)}, f32[4,8,2,8,128]{4,3,2,1,0:T(8,128)S(1)}, u32[]{:S(2)}, u32[]{:S(2)}) collective-permute-start(f32[4,8,2,8,128]{4,3,2,1,0:T(8,128)S(1)} %heun_b2.1.after.refs_3_), channel_id=1, source_target_pairs={{0,1},{1,0},{2,3},{3,2},{4,5},{5,4},{6,7},{7,6},{8,9},{9,8},{10,11... | collective-permute-start | bytes 786440 | tf_op jit(solution)/shard_map/ppermute | solution.py:451
  56.1 3.0 %collective-permute-start.24 = (f32[4,18,2,8,128]{4,3,2,1,0:T(8,128)S(1)}, f32[4,18,2,8,128]{4,3,2,1,0:T(8,128)S(1)}, u32[]{:S(2)}, u32[]{:S(2)}) collective-permute-start(f32[4,18,2,8,128]{4,3,2,1,0:T(8,128)S(1)} %heun_c2.1.after.refs_6_), channel_id=1, source_target_pairs={{0,1},{1,0},{2,3},{3,2},{4,5},{5,4},{6,7},{7,6},{8,9},{9,8},{10,11... | collective-permute-start | bytes 1769480 | tf_op jit(solution)/shard_map/ppermute | solution.py:451
  59.8 2.7 %collective-permute-start.22 = (f32[2,16,8,128]{3,2,1,0:T(8,128)S(1)}, f32[2,16,8,128]{3,2,1,0:T(8,128)S(1)}, u32[]{:S(2)}, u32[]{:S(2)}) collective-permute-start(f32[2,16,8,128]{3,2,1,0:T(8,128)S(1)} %get-tuple-element.33.r_cross), channel_id=1, source_target_pairs={{0,1},{1,0},{2,3},{3,2},{4,5},{5,4},{6,7},{7,6},{8,9},{9,8},{10,11... | collective-permute-start | bytes 393224 | tf_op jit(solution)/shard_map/ppermute | solution.py:451
  63.4 1.8 %collective-permute-done.23.refs_7_ = f32[4,18,2,8,128]{4,3,2,1,0:T(8,128)S(1)} collective-permute-done((f32[4,18,2,8,128]{4,3,2,1,0:T(8,128)S(1)}, f32[4,18,2,8,128]{4,3,2,1,0:T(8,128)S(1)}, u32[]{:S(2)}, u32[]{:S(2)}) %collective-permute-start.23) | collective-permute-done | bytes 589856 | tf_op jit(solution)/shard_map/ppermute | solution.py:456
  67.7 5.6 %collective-permute-done.25.one = f32[2,16,8,128]{3,2,1,0:T(8,128)S(1)} collective-permute-done((f32[2,16,8,128]{3,2,1,0:T(8,128)S(1)}, f32[2,16,8,128]{3,2,1,0:T(8,128)S(1)}, u32[]{:S(2)}, u32[]{:S(2)}) %collective-permute-start.25) | collective-permute-done | bytes 131104 | tf_op jit(solution)/shard_map/ppermute | solution.py:461
  73.3 4.2 %collective-permute-start.26 = (f32[2,16,8,128]{3,2,1,0:T(8,128)S(1)}, f32[2,16,8,128]{3,2,1,0:T(8,128)S(1)}, u32[]{:S(2)}, u32[]{:S(2)}) collective-permute-start(f32[2,16,8,128]{3,2,1,0:T(8,128)S(1)} %collective-permute-done.25.one), channel_id=1, source_target_pairs={{0,1},{1,0},{2,3},{3,2},{4,5},{5,4},{6,7},{7,6},{8,9},{9,8},{10,11... | collective-permute-start | bytes 393224 | tf_op jit(solution)/shard_map/ppermute | solution.py:451
  79.9 6.2 %collective-permute-done.29.one = f32[2,16,8,128]{3,2,1,0:T(8,128)S(1)} collective-permute-done((f32[2,16,8,128]{3,2,1,0:T(8,128)S(1)}, f32[2,16,8,128]{3,2,1,0:T(8,128)S(1)}, u32[]{:S(2)}, u32[]{:S(2)}) %collective-permute-start.29) | collective-permute-done | bytes 131104 | tf_op jit(solution)/shard_map/ppermute | solution.py:461
  86.1 3.1 %collective-permute-start.30 = (f32[2,16,8,128]{3,2,1,0:T(8,128)S(1)}, f32[2,16,8,128]{3,2,1,0:T(8,128)S(1)}, u32[]{:S(2)}, u32[]{:S(2)}) collective-permute-start(f32[2,16,8,128]{3,2,1,0:T(8,128)S(1)} %collective-permute-done.29.one), channel_id=1, source_target_pairs={{0,1},{1,0},{2,3},{3,2},{4,5},{5,4},{6,7},{7,6},{8,9},{9,8},{10,11... | collective-permute-start | bytes 393224 | tf_op jit(solution)/shard_map/ppermute | solution.py:451
  92.7 4.4 %collective-permute-done.33.one = f32[2,16,8,128]{3,2,1,0:T(8,128)S(1)} collective-permute-done((f32[2,16,8,128]{3,2,1,0:T(8,128)S(1)}, f32[2,16,8,128]{3,2,1,0:T(8,128)S(1)}, u32[]{:S(2)}, u32[]{:S(2)}) %collective-permute-start.33) | collective-permute-done | bytes 131104 | tf_op jit(solution)/shard_map/ppermute | solution.py:461
  97.1 3.4 %collective-permute-start.34 = (f32[2,16,8,128]{3,2,1,0:T(8,128)S(1)}, f32[2,16,8,128]{3,2,1,0:T(8,128)S(1)}, u32[]{:S(2)}, u32[]{:S(2)}) collective-permute-start(f32[2,16,8,128]{3,2,1,0:T(8,128)S(1)} %collective-permute-done.33.one), channel_id=1, source_target_pairs={{0,1},{1,0},{2,3},{3,2},{4,5},{5,4},{6,7},{7,6},{8,9},{9,8},{10,11... | collective-permute-start | bytes 393224 | tf_op jit(solution)/shard_map/ppermute | solution.py:451
  102.6 5.8 %collective-permute-done.35.near = f32[2,2,16,8,128]{4,3,2,1,0:T(8,128)S(1)} collective-permute-done((f32[2,2,16,8,128]{4,3,2,1,0:T(8,128)S(1)}, f32[2,2,16,8,128]{4,3,2,1,0:T(8,128)S(1)}, u32[]{:S(2)}, u32[]{:S(2)}) %collective-permute-start.35) | collective-permute-done | bytes 262176 | tf_op jit(solution)/shard_map/ppermute | solution.py:456
  108.4 3.5 %collective-permute-start.36 = (f32[2,2,16,8,128]{4,3,2,1,0:T(8,128)S(1)}, f32[2,2,16,8,128]{4,3,2,1,0:T(8,128)S(1)}, u32[]{:S(2)}, u32[]{:S(2)}) collective-permute-start(f32[2,2,16,8,128]{4,3,2,1,0:T(8,128)S(1)} %collective-permute-done.35.near), channel_id=1, source_target_pairs={{0,1},{1,0},{2,3},{3,2},{4,5},{5,4},{6,7},{7,6},{8,9},{9,8},{10,11... | collective-permute-start | bytes 786440 | tf_op jit(solution)/shard_map/ppermute | solution.py:451
  113.5 1.5 %finish.1 = f32[2,2,256,256]{3,2,1,0:T(8,128)} custom-call(f32[2,16,8,128]{3,2,1,0:T(8,128)S(1)} %get-tuple-element.34.end, f32[2,16,8,128]{3,2,1,0:T(8,128)S(1)} %walk1.1.chained, f32[4,2,2,8,128]{4,3,2,1,0:T(8,128)S(1)} %heun_a3.1.after.refs_0_, f32[4,8,2,8,128]{4,3,2,1,0:T(8,128)S(1)} %heun_b3.1.after.refs_1_, f32[4,22,2,8,128]{4,3,2,1,0:T(8,128)S(1)} %heun_c3.1.refs_2_), custom_call_target="tpu_custom_call" | custom-call | tf_op jit(solution)/shard_map/finish/pallas_call | solution.py:434
  (80 shorter events, 27.3 us)
Async XLA Ops:
  3.1 7.9 %collective-permute-start = (f32[6,18,2,8,128]{4,3,2,1,0:T(8,128)S(1)}, f32[6,18,2,8,128]{4,3,2,1,0:T(8,128)S(1)}, u32[]{:S(2)}, u32[]{:S(2)}) collective-permute-start(f32[6,18,2,8,128]{4,3,2,1,0:T(8,128)S(1)} %get-tuple-element.27.refs_0_.after.refs_4_.refs_7_.refs_10_.refs_5_), channel_id=1, source_target_pairs={{0,1},{1,0},{2,3},{3,2},{4,5},{5,4},{6,7},{7,6},{8,9},{9,8},{10,11... | collective-permute-start | bytes 2654216 | tf_op jit(solution)/shard_map/ppermute | solution.py:451
  3.8 12.8 %collective-permute-start.3 = (f32[6,18,2,8,128]{4,3,2,1,0:T(8,128)S(1)}, f32[6,18,2,8,128]{4,3,2,1,0:T(8,128)S(1)}, u32[]{:S(2)}, u32[]{:S(2)}) collective-permute-start(f32[6,18,2,8,128]{4,3,2,1,0:T(8,128)S(1)} %get-tuple-element.30.refs_3_.refs_6_.refs_9_.refs_4_), channel_id=1, source_target_pairs={{0,31},{1,2},{2,1},{3,4},{4,3},{5,6},{6,5},{7,8},{8,7},{9,10},{10,... | collective-permute-start | bytes 2654216 | tf_op jit(solution)/shard_map/ppermute | solution.py:456
  5.5 13.7 %collective-permute-start.1 = (f32[6,8,2,8,128]{4,3,2,1,0:T(8,128)S(1)}, f32[6,8,2,8,128]{4,3,2,1,0:T(8,128)S(1)}, u32[]{:S(2)}, u32[]{:S(2)}) collective-permute-start(f32[6,8,2,8,128]{4,3,2,1,0:T(8,128)S(1)} %get-tuple-element.28.refs_1_.refs_3_.refs_11_.refs_14_), channel_id=1, source_target_pairs={{0,1},{1,0},{2,3},{3,2},{4,5},{5,4},{6,7},{7,6},{8,9},{9,8},{10,11... | collective-permute-start | bytes 1179656 | tf_op jit(solution)/shard_map/ppermute | solution.py:451
  10.4 17.0 %collective-permute-start.4 = (f32[6,8,2,8,128]{4,3,2,1,0:T(8,128)S(1)}, f32[6,8,2,8,128]{4,3,2,1,0:T(8,128)S(1)}, u32[]{:S(2)}, u32[]{:S(2)}) collective-permute-start(f32[6,8,2,8,128]{4,3,2,1,0:T(8,128)S(1)} %get-tuple-element.31.refs_4_.refs_10_.refs_13_), channel_id=1, source_target_pairs={{0,31},{1,2},{2,1},{3,4},{4,3},{5,6},{6,5},{7,8},{8,7},{9,10},{10,... | collective-permute-start | bytes 1179656 | tf_op jit(solution)/shard_map/ppermute | solution.py:456
  10.5 17.5 %collective-permute-start.2 = (f32[6,6,2,8,128]{4,3,2,1,0:T(8,128)S(1)}, f32[6,6,2,8,128]{4,3,2,1,0:T(8,128)S(1)}, u32[]{:S(2)}, u32[]{:S(2)}) collective-permute-start(f32[6,6,2,8,128]{4,3,2,1,0:T(8,128)S(1)} %get-tuple-element.29.refs_2_.refs_6_.refs_18_), channel_id=1, source_target_pairs={{0,1},{1,0},{2,3},{3,2},{4,5},{5,4},{6,7},{7,6},{8,9},{9,8},{10,11... | collective-permute-start | bytes 884744 | tf_op jit(solution)/shard_map/ppermute | solution.py:451
  11.0 20.0 %collective-permute-start.5 = (f32[6,6,2,8,128]{4,3,2,1,0:T(8,128)S(1)}, f32[6,6,2,8,128]{4,3,2,1,0:T(8,128)S(1)}, u32[]{:S(2)}, u32[]{:S(2)}) collective-permute-start(f32[6,6,2,8,128]{4,3,2,1,0:T(8,128)S(1)} %get-tuple-element.32.refs_5_.refs_17_), channel_id=1, source_target_pairs={{0,31},{1,2},{2,1},{3,4},{4,3},{5,6},{6,5},{7,8},{8,7},{9,10},{10,... | collective-permute-start | bytes 884744 | tf_op jit(solution)/shard_map/ppermute | solution.py:456
  17.7 14.0 %collective-permute-start.6 = (f32[4,14,2,8,128]{4,3,2,1,0:T(8,128)S(1)}, f32[4,14,2,8,128]{4,3,2,1,0:T(8,128)S(1)}, u32[]{:S(2)}, u32[]{:S(2)}) collective-permute-start(f32[4,14,2,8,128]{4,3,2,1,0:T(8,128)S(1)} %heun_a0.1.after.refs_0_), channel_id=1, source_target_pairs={{0,31},{1,2},{2,1},{3,4},{4,3},{5,6},{6,5},{7,8},{8,7},{9,10},{10,... | collective-permute-start | bytes 1376264 | tf_op jit(solution)/shard_map/ppermute | solution.py:456
  19.1 15.4 %collective-permute-start.7 = (f32[4,14,2,8,128]{4,3,2,1,0:T(8,128)S(1)}, f32[4,14,2,8,128]{4,3,2,1,0:T(8,128)S(1)}, u32[]{:S(2)}, u32[]{:S(2)}) collective-permute-start(f32[4,14,2,8,128]{4,3,2,1,0:T(8,128)S(1)} %heun_a0.1.after.refs_0_), channel_id=1, source_target_pairs={{0,1},{1,0},{2,3},{3,2},{4,5},{5,4},{6,7},{7,6},{8,9},{9,8},{10,11... | collective-permute-start | bytes 1376264 | tf_op jit(solution)/shard_map/ppermute | solution.py:451
  27.9 7.7 %collective-permute-start.8 = (f32[4,8,2,8,128]{4,3,2,1,0:T(8,128)S(1)}, f32[4,8,2,8,128]{4,3,2,1,0:T(8,128)S(1)}, u32[]{:S(2)}, u32[]{:S(2)}) collective-permute-start(f32[4,8,2,8,128]{4,3,2,1,0:T(8,128)S(1)} %heun_b0.1.after.refs_3_), channel_id=1, source_target_pairs={{0,31},{1,2},{2,1},{3,4},{4,3},{5,6},{6,5},{7,8},{8,7},{9,10},{10,... | collective-permute-start | bytes 786440 | tf_op jit(solution)/shard_map/ppermute | solution.py:456
  28.0 11.7 %collective-permute-start.9 = (f32[4,8,2,8,128]{4,3,2,1,0:T(8,128)S(1)}, f32[4,8,2,8,128]{4,3,2,1,0:T(8,128)S(1)}, u32[]{:S(2)}, u32[]{:S(2)}) collective-permute-start(f32[4,8,2,8,128]{4,3,2,1,0:T(8,128)S(1)} %heun_b0.1.after.refs_3_), channel_id=1, source_target_pairs={{0,1},{1,0},{2,3},{3,2},{4,5},{5,4},{6,7},{7,6},{8,9},{9,8},{10,11... | collective-permute-start | bytes 786440 | tf_op jit(solution)/shard_map/ppermute | solution.py:451
  31.4 8.8 %collective-permute-start.10 = (f32[4,10,2,8,128]{4,3,2,1,0:T(8,128)S(1)}, f32[4,10,2,8,128]{4,3,2,1,0:T(8,128)S(1)}, u32[]{:S(2)}, u32[]{:S(2)}) collective-permute-start(f32[4,10,2,8,128]{4,3,2,1,0:T(8,128)S(1)} %heun_c0.1.after.refs_6_), channel_id=1, source_target_pairs={{0,31},{1,2},{2,1},{3,4},{4,3},{5,6},{6,5},{7,8},{8,7},{9,10},{10,... | collective-permute-start | bytes 983048 | tf_op jit(solution)/shard_map/ppermute | solution.py:456
  31.8 10.2 %collective-permute-start.11 = (f32[4,10,2,8,128]{4,3,2,1,0:T(8,128)S(1)}, f32[4,10,2,8,128]{4,3,2,1,0:T(8,128)S(1)}, u32[]{:S(2)}, u32[]{:S(2)}) collective-permute-start(f32[4,10,2,8,128]{4,3,2,1,0:T(8,128)S(1)} %heun_c0.1.after.refs_6_), channel_id=1, source_target_pairs={{0,1},{1,0},{2,3},{3,2},{4,5},{5,4},{6,7},{7,6},{8,9},{9,8},{10,11... | collective-permute-start | bytes 983048 | tf_op jit(solution)/shard_map/ppermute | solution.py:451
  35.6 10.5 %collective-permute-start.13 = (f32[4,10,2,8,128]{4,3,2,1,0:T(8,128)S(1)}, f32[4,10,2,8,128]{4,3,2,1,0:T(8,128)S(1)}, u32[]{:S(2)}, u32[]{:S(2)}) collective-permute-start(f32[4,10,2,8,128]{4,3,2,1,0:T(8,128)S(1)} %heun_a1.1.after.refs_1_.refs_0_), channel_id=1, source_target_pairs={{0,1},{1,0},{2,3},{3,2},{4,5},{5,4},{6,7},{7,6},{8,9},{9,8},{10,11... | collective-permute-start | bytes 983048 | tf_op jit(solution)/shard_map/ppermute | solution.py:451
  40.2 9.7 %collective-permute-start.17 = (f32[4,8,2,8,128]{4,3,2,1,0:T(8,128)S(1)}, f32[4,8,2,8,128]{4,3,2,1,0:T(8,128)S(1)}, u32[]{:S(2)}, u32[]{:S(2)}) collective-permute-start(f32[4,8,2,8,128]{4,3,2,1,0:T(8,128)S(1)} %heun_b1.1.after.refs_3_), channel_id=1, source_target_pairs={{0,1},{1,0},{2,3},{3,2},{4,5},{5,4},{6,7},{7,6},{8,9},{9,8},{10,11... | collective-permute-start | bytes 786440 | tf_op jit(solution)/shard_map/ppermute | solution.py:451
  42.6 8.6 %collective-permute-start.18 = (f32[4,14,2,8,128]{4,3,2,1,0:T(8,128)S(1)}, f32[4,14,2,8,128]{4,3,2,1,0:T(8,128)S(1)}, u32[]{:S(2)}, u32[]{:S(2)}) collective-permute-start(f32[4,14,2,8,128]{4,3,2,1,0:T(8,128)S(1)} %heun_c1.1.after.refs_6_), channel_id=1, source_target_pairs={{0,31},{1,2},{2,1},{3,4},{4,3},{5,6},{6,5},{7,8},{8,7},{9,10},{10,... | collective-permute-start | bytes 1376264 | tf_op jit(solution)/shard_map/ppermute | solution.py:456
  42.7 11.5 %collective-permute-start.19 = (f32[4,14,2,8,128]{4,3,2,1,0:T(8,128)S(1)}, f32[4,14,2,8,128]{4,3,2,1,0:T(8,128)S(1)}, u32[]{:S(2)}, u32[]{:S(2)}) collective-permute-start(f32[4,14,2,8,128]{4,3,2,1,0:T(8,128)S(1)} %heun_c1.1.after.refs_6_), channel_id=1, source_target_pairs={{0,1},{1,0},{2,3},{3,2},{4,5},{5,4},{6,7},{7,6},{8,9},{9,8},{10,11... | collective-permute-start | bytes 1376264 | tf_op jit(solution)/shard_map/ppermute | solution.py:451
  46.3 9.8 %collective-permute-start.14 = (f32[112,8,128]{2,1,0:T(8,128)S(1)}, f32[112,8,128]{2,1,0:T(8,128)S(1)}, u32[]{:S(2)}, u32[]{:S(2)}) collective-permute-start(f32[112,8,128]{2,1,0:T(8,128)S(1)} %heun_a2.1.after.refs_0_), channel_id=1, source_target_pairs={{0,31},{1,2},{2,1},{3,4},{4,3},{5,6},{6,5},{7,8},{8,7},{9,10},{10,... | collective-permute-start | bytes 1376264 | tf_op jit(solution)/shard_map/ppermute | solution.py:456
  46.4 12.7 %collective-permute-start.15 = (f32[112,8,128]{2,1,0:T(8,128)S(1)}, f32[112,8,128]{2,1,0:T(8,128)S(1)}, u32[]{:S(2)}, u32[]{:S(2)}) collective-permute-start(f32[112,8,128]{2,1,0:T(8,128)S(1)} %heun_a2.1.after.refs_0_), channel_id=1, source_target_pairs={{0,1},{1,0},{2,3},{3,2},{4,5},{5,4},{6,7},{7,6},{8,9},{9,8},{10,11... | collective-permute-start | bytes 1376264 | tf_op jit(solution)/shard_map/ppermute | solution.py:451
  50.3 9.0 %collective-permute-start.20 = (f32[4,8,2,8,128]{4,3,2,1,0:T(8,128)S(1)}, f32[4,8,2,8,128]{4,3,2,1,0:T(8,128)S(1)}, u32[]{:S(2)}, u32[]{:S(2)}) collective-permute-start(f32[4,8,2,8,128]{4,3,2,1,0:T(8,128)S(1)} %heun_b2.1.after.refs_3_), channel_id=1, source_target_pairs={{0,31},{1,2},{2,1},{3,4},{4,3},{5,6},{6,5},{7,8},{8,7},{9,10},{10,... | collective-permute-start | bytes 786440 | tf_op jit(solution)/shard_map/ppermute | solution.py:456
  51.2 8.2 %collective-permute-start.21 = (f32[4,8,2,8,128]{4,3,2,1,0:T(8,128)S(1)}, f32[4,8,2,8,128]{4,3,2,1,0:T(8,128)S(1)}, u32[]{:S(2)}, u32[]{:S(2)}) collective-permute-start(f32[4,8,2,8,128]{4,3,2,1,0:T(8,128)S(1)} %heun_b2.1.after.refs_3_), channel_id=1, source_target_pairs={{0,1},{1,0},{2,3},{3,2},{4,5},{5,4},{6,7},{7,6},{8,9},{9,8},{10,11... | collective-permute-start | bytes 786440 | tf_op jit(solution)/shard_map/ppermute | solution.py:451
  55.0 10.2 %collective-permute-start.23 = (f32[4,18,2,8,128]{4,3,2,1,0:T(8,128)S(1)}, f32[4,18,2,8,128]{4,3,2,1,0:T(8,128)S(1)}, u32[]{:S(2)}, u32[]{:S(2)}) collective-permute-start(f32[4,18,2,8,128]{4,3,2,1,0:T(8,128)S(1)} %heun_c2.1.after.refs_6_), channel_id=1, source_target_pairs={{0,31},{1,2},{2,1},{3,4},{4,3},{5,6},{6,5},{7,8},{8,7},{9,10},{10,... | collective-permute-start | bytes 1769480 | tf_op jit(solution)/shard_map/ppermute | solution.py:456
  56.1 9.1 %collective-permute-start.24 = (f32[4,18,2,8,128]{4,3,2,1,0:T(8,128)S(1)}, f32[4,18,2,8,128]{4,3,2,1,0:T(8,128)S(1)}, u32[]{:S(2)}, u32[]{:S(2)}) collective-permute-start(f32[4,18,2,8,128]{4,3,2,1,0:T(8,128)S(1)} %heun_c2.1.after.refs_6_), channel_id=1, source_target_pairs={{0,1},{1,0},{2,3},{3,2},{4,5},{5,4},{6,7},{7,6},{8,9},{9,8},{10,11... | collective-permute-start | bytes 1769480 | tf_op jit(solution)/shard_map/ppermute | solution.py:451
  78.5 10.7 %collective-permute-start.27 = (f32[2,2,16,8,128]{4,3,2,1,0:T(8,128)S(1)}, f32[2,2,16,8,128]{4,3,2,1,0:T(8,128)S(1)}, u32[]{:S(2)}, u32[]{:S(2)}) collective-permute-start(f32[2,2,16,8,128]{4,3,2,1,0:T(8,128)S(1)} %pack.3.both), channel_id=1, source_target_pairs={{0,31},{1,2},{2,1},{3,4},{4,3},{5,6},{6,5},{7,8},{8,7},{9,10},{10,... | collective-permute-start | bytes 786440 | tf_op jit(solution)/shard_map/ppermute | solution.py:456
  91.3 9.2 %collective-permute-start.31 = (f32[2,2,16,8,128]{4,3,2,1,0:T(8,128)S(1)}, f32[2,2,16,8,128]{4,3,2,1,0:T(8,128)S(1)}, u32[]{:S(2)}, u32[]{:S(2)}) collective-permute-start(f32[2,2,16,8,128]{4,3,2,1,0:T(8,128)S(1)} %walk3.1.both), channel_id=1, source_target_pairs={{0,31},{1,2},{2,1},{3,4},{4,3},{5,6},{6,5},{7,8},{8,7},{9,10},{10,... | collective-permute-start | bytes 786440 | tf_op jit(solution)/shard_map/ppermute | solution.py:456
  (16 other events, 68.1 us)

commit v5 on v4

--- a/solution.py
+++ b/solution.py
@@ -24,6 +24,7 @@
 PARAMS = pltpu.CompilerParams(vmem_limit_bytes=VMEM_LIMIT)
 COARSE = (2, 16, 8, 128)
 PACK_COST = 10**10
+RATES_COST = 2 * 10**9
 COST = ((2 * 10**9,) * 4, (2 * 10**9,) * 2 + (4 * 10**9,) * 2, (2 * 10**9,) * 4)
 FLAT = 3
 TAIL = 4 * (CUTS[1] - 4 * FLAT) * 2
@@ -77,14 +78,13 @@
             scatter(x[sp, q ^ flip], rows.at[k], mat, [(pair, k), (cross, k)])
 
 
-def prep_rates_kernel(feed, kill, *refs):
-    pair, cross, rows = refs[2 * CHUNKS:3 * CHUNKS], refs[3 * CHUNKS:4 * CHUNKS], refs[-1]
+def prep_rates_kernel(q, feed, kill, *refs):
+    target, rows = refs[CHUNKS:2 * CHUNKS], refs[-1]
     flip = odd()
     mat = splitter(False)
-    for q, target in ((0, cross), (1, pair)):
-        f = feed[q ^ flip]
-        scatter(f, rows.at[2 * q], mat, [(target, 4)])
-        scatter(0.52 - (f + kill[q ^ flip]), rows.at[2 * q + 1], mat, [(target, 5)])
+    f = feed[q ^ flip]
+    scatter(f, rows.at[0], mat, [(target, 4)])
+    scatter(0.52 - (f + kill[q ^ flip]), rows.at[1], mat, [(target, 5)])
 
 
 def prep(x, feed, kill):
@@ -99,16 +99,20 @@
         compiler_params=PARAMS,
         name="prep",
     )(x)
-    return pl.pallas_call(
-        prep_rates_kernel,
-        out_shape=shapes,
-        in_specs=[VM, VM] + [VM] * (2 * CHUNKS),
-        out_specs=[VM] * (2 * CHUNKS),
-        scratch_shapes=scratch,
-        input_output_aliases={2 + i: i for i in range(2 * CHUNKS)},
-        compiler_params=PARAMS,
-        name="prep_rates",
-    )(feed, kill, *sent)
+    rated = []
+    for q, part in ((0, sent[CHUNKS:]), (1, sent[:CHUNKS])):
+        rated.append(pl.pallas_call(
+            functools.partial(prep_rates_kernel, q),
+            out_shape=shapes[:CHUNKS],
+            in_specs=[VM] * (2 + CHUNKS),
+            out_specs=[VM] * CHUNKS,
+            scratch_shapes=[pltpu.VMEM((2, 2, 8 * STRIDE, 128), F32)],
+            input_output_aliases={2 + c: c for c in range(CHUNKS)},
+            compiler_params=PARAMS,
+            cost_estimate=pl.CostEstimate(flops=RATES_COST, bytes_accessed=1000, transcendentals=0),
+            name="prep_inner" if q else "prep_outer",
+        )(feed, kill, *part))
+    return rated[1] + rated[0]
 
 
 LINE = ((1, 1), (1, 0), (0, 0), (0, 1), (2, 1), (2, 0))

time: 115 us -> 115 us (level)
  no operation moved by 1% of the time
where the time goes in v5:
time: 115 us; the launch traced here: 114 us
  starting transfers between devices  64.1 us (56%)
  waiting for transfers between devices  35.9 us (31%)
  Pallas kernels  12.1 us (11%)
  local copies, waits for them, and re-layouts  1.7 us (1%)
    ppermute x19, starting transfers between devices, swap_pair(): return lax.ppermute(x, 'space', [(i, i ^ 1) for i in range(n)])  55.8 us
    ppermute x3, waiting for transfers between devices, later(): lax.ppermute(x, 'tm', [(i, i + distance) for i in range(n - distance)])  16.2 us
    ppermute x15, waiting for transfers between devices, swap_cross(): lax.ppermute(x, 'space', [(i, (i + 1) % n if i % 2 else (i - 1) % n) for...  13.7 us
    pallas_call x12, Pallas kernels, heun(): pl.pallas_call(functools.partial(heun_kernel, step, c), out_shape=jax.Sha...  7.03 us
    ppermute x19, waiting for transfers between devices, swap_pair(): return lax.ppermute(x, 'space', [(i, i ^ 1) for i in range(n)])  5.97 us
    ppermute x15, starting transfers between devices, swap_cross(): lax.ppermute(x, 'space', [(i, (i + 1) % n if i % 2 else (i - 1) % n) for...  4.37 us
    ppermute x3, starting transfers between devices, later(): lax.ppermute(x, 'tm', [(i, i + distance) for i in range(n - distance)])  3.88 us
  transfers between devices with their start and end apart: 37, of which 15 were waited for; matrix products, arithmetic and copies ran while one was open for 0% of the time, Pallas kernels for 6%

profile of v5, /device:TPU:7, one launch (start us, length us, event | category | flops | bytes accessed | tf_op | source)
XLA Modules:
  0.0 114.3 jit_solution(923625544678957241)
XLA Ops:
  2.9 2.3 %collective-permute-start.3 = (f32[6,18,2,8,128]{4,3,2,1,0:T(8,128)S(1)}, f32[6,18,2,8,128]{4,3,2,1,0:T(8,128)S(1)}, u32[]{:S(2)}, u32[]{:S(2)}) collective-permute-start(f32[6,18,2,8,128]{4,3,2,1,0:T(8,128)S(1)} %get-tuple-element.30.refs_3_.refs_6_.refs_9_.refs_4_), channel_id=1, source_target_pairs={{0,31},{1,2},{2,1},{3,4},{4,3},{5,6},{6,5},{7,8},{8,7},{9,10},{10,... | collective-permute-start | bytes 2654216 | tf_op jit(solution)/shard_map/ppermute | solution.py:460
  5.6 4.5 %collective-permute-start = (f32[6,18,2,8,128]{4,3,2,1,0:T(8,128)S(1)}, f32[6,18,2,8,128]{4,3,2,1,0:T(8,128)S(1)}, u32[]{:S(2)}, u32[]{:S(2)}) collective-permute-start(f32[6,18,2,8,128]{4,3,2,1,0:T(8,128)S(1)} %get-tuple-element.24.refs_0_.after.refs_4_.refs_7_.refs_10_.refs_5_), channel_id=1, source_target_pairs={{0,1},{1,0},{2,3},{3,2},{4,5},{5,4},{6,7},{7,6},{8,9},{9,8},{10,11... | collective-permute-start | bytes 2654216 | tf_op jit(solution)/shard_map/ppermute | solution.py:455
  11.8 4.3 %collective-permute-done.3.refs_9_.refs_1_.refs_5_.refs_8_.refs_11_.refs_6_ = f32[6,18,2,8,128]{4,3,2,1,0:T(8,128)S(1)} collective-permute-done((f32[6,18,2,8,128]{4,3,2,1,0:T(8,128)S(1)}, f32[6,18,2,8,128]{4,3,2,1,0:T(8,128)S(1)}, u32[]{:S(2)}, u32[]{:S(2)}) %collective-permute-start.3) | collective-permute-done | bytes 884768 | tf_op jit(solution)/shard_map/ppermute | solution.py:460
  16.2 4.1 %collective-permute-start.2 = (f32[6,6,2,8,128]{4,3,2,1,0:T(8,128)S(1)}, f32[6,6,2,8,128]{4,3,2,1,0:T(8,128)S(1)}, u32[]{:S(2)}, u32[]{:S(2)}) collective-permute-start(f32[6,6,2,8,128]{4,3,2,1,0:T(8,128)S(1)} %get-tuple-element.26.refs_2_.refs_6_.refs_18_), channel_id=1, source_target_pairs={{0,1},{1,0},{2,3},{3,2},{4,5},{5,4},{6,7},{7,6},{8,9},{9,8},{10,11... | collective-permute-start | bytes 884744 | tf_op jit(solution)/shard_map/ppermute | solution.py:455
  21.5 5.0 %collective-permute-start.7 = (f32[4,14,2,8,128]{4,3,2,1,0:T(8,128)S(1)}, f32[4,14,2,8,128]{4,3,2,1,0:T(8,128)S(1)}, u32[]{:S(2)}, u32[]{:S(2)}) collective-permute-start(f32[4,14,2,8,128]{4,3,2,1,0:T(8,128)S(1)} %heun_a0.1.after.refs_0_), channel_id=1, source_target_pairs={{0,1},{1,0},{2,3},{3,2},{4,5},{5,4},{6,7},{7,6},{8,9},{9,8},{10,11... | collective-permute-start | bytes 1376264 | tf_op jit(solution)/shard_map/ppermute | solution.py:455
  27.1 3.0 %collective-permute-start.9 = (f32[4,8,2,8,128]{4,3,2,1,0:T(8,128)S(1)}, f32[4,8,2,8,128]{4,3,2,1,0:T(8,128)S(1)}, u32[]{:S(2)}, u32[]{:S(2)}) collective-permute-start(f32[4,8,2,8,128]{4,3,2,1,0:T(8,128)S(1)} %heun_b0.1.after.refs_3_), channel_id=1, source_target_pairs={{0,1},{1,0},{2,3},{3,2},{4,5},{5,4},{6,7},{7,6},{8,9},{9,8},{10,11... | collective-permute-start | bytes 786440 | tf_op jit(solution)/shard_map/ppermute | solution.py:455
  30.9 2.7 %collective-permute-start.11 = (f32[4,10,2,8,128]{4,3,2,1,0:T(8,128)S(1)}, f32[4,10,2,8,128]{4,3,2,1,0:T(8,128)S(1)}, u32[]{:S(2)}, u32[]{:S(2)}) collective-permute-start(f32[4,10,2,8,128]{4,3,2,1,0:T(8,128)S(1)} %heun_c0.1.after.refs_6_), channel_id=1, source_target_pairs={{0,1},{1,0},{2,3},{3,2},{4,5},{5,4},{6,7},{7,6},{8,9},{9,8},{10,11... | collective-permute-start | bytes 983048 | tf_op jit(solution)/shard_map/ppermute | solution.py:455
  34.7 4.1 %collective-permute-start.13 = (f32[4,10,2,8,128]{4,3,2,1,0:T(8,128)S(1)}, f32[4,10,2,8,128]{4,3,2,1,0:T(8,128)S(1)}, u32[]{:S(2)}, u32[]{:S(2)}) collective-permute-start(f32[4,10,2,8,128]{4,3,2,1,0:T(8,128)S(1)} %heun_a1.1.after.refs_1_.refs_0_), channel_id=1, source_target_pairs={{0,1},{1,0},{2,3},{3,2},{4,5},{5,4},{6,7},{7,6},{8,9},{9,8},{10,11... | collective-permute-start | bytes 983048 | tf_op jit(solution)/shard_map/ppermute | solution.py:455
  39.3 1.8 %collective-permute-start.17 = (f32[4,8,2,8,128]{4,3,2,1,0:T(8,128)S(1)}, f32[4,8,2,8,128]{4,3,2,1,0:T(8,128)S(1)}, u32[]{:S(2)}, u32[]{:S(2)}) collective-permute-start(f32[4,8,2,8,128]{4,3,2,1,0:T(8,128)S(1)} %heun_b1.1.after.refs_3_), channel_id=1, source_target_pairs={{0,1},{1,0},{2,3},{3,2},{4,5},{5,4},{6,7},{7,6},{8,9},{9,8},{10,11... | collective-permute-start | bytes 786440 | tf_op jit(solution)/shard_map/ppermute | solution.py:455
  41.8 3.3 %collective-permute-start.19 = (f32[4,14,2,8,128]{4,3,2,1,0:T(8,128)S(1)}, f32[4,14,2,8,128]{4,3,2,1,0:T(8,128)S(1)}, u32[]{:S(2)}, u32[]{:S(2)}) collective-permute-start(f32[4,14,2,8,128]{4,3,2,1,0:T(8,128)S(1)} %heun_c1.1.after.refs_6_), channel_id=1, source_target_pairs={{0,1},{1,0},{2,3},{3,2},{4,5},{5,4},{6,7},{7,6},{8,9},{9,8},{10,11... | collective-permute-start | bytes 1376264 | tf_op jit(solution)/shard_map/ppermute | solution.py:455
  45.5 3.5 %collective-permute-start.15 = (f32[112,8,128]{2,1,0:T(8,128)S(1)}, f32[112,8,128]{2,1,0:T(8,128)S(1)}, u32[]{:S(2)}, u32[]{:S(2)}) collective-permute-start(f32[112,8,128]{2,1,0:T(8,128)S(1)} %heun_a2.1.after.refs_0_), channel_id=1, source_target_pairs={{0,1},{1,0},{2,3},{3,2},{4,5},{5,4},{6,7},{7,6},{8,9},{9,8},{10,11... | collective-permute-start | bytes 1376264 | tf_op jit(solution)/shard_map/ppermute | solution.py:455
  50.3 3.0 %collective-permute-start.21 = (f32[4,8,2,8,128]{4,3,2,1,0:T(8,128)S(1)}, f32[4,8,2,8,128]{4,3,2,1,0:T(8,128)S(1)}, u32[]{:S(2)}, u32[]{:S(2)}) collective-permute-start(f32[4,8,2,8,128]{4,3,2,1,0:T(8,128)S(1)} %heun_b2.1.after.refs_3_), channel_id=1, source_target_pairs={{0,1},{1,0},{2,3},{3,2},{4,5},{5,4},{6,7},{7,6},{8,9},{9,8},{10,11... | collective-permute-start | bytes 786440 | tf_op jit(solution)/shard_map/ppermute | solution.py:455
  55.2 3.0 %collective-permute-start.24 = (f32[4,18,2,8,128]{4,3,2,1,0:T(8,128)S(1)}, f32[4,18,2,8,128]{4,3,2,1,0:T(8,128)S(1)}, u32[]{:S(2)}, u32[]{:S(2)}) collective-permute-start(f32[4,18,2,8,128]{4,3,2,1,0:T(8,128)S(1)} %heun_c2.1.after.refs_6_), channel_id=1, source_target_pairs={{0,1},{1,0},{2,3},{3,2},{4,5},{5,4},{6,7},{7,6},{8,9},{9,8},{10,11... | collective-permute-start | bytes 1769480 | tf_op jit(solution)/shard_map/ppermute | solution.py:455
  58.9 2.7 %collective-permute-start.22 = (f32[2,16,8,128]{3,2,1,0:T(8,128)S(1)}, f32[2,16,8,128]{3,2,1,0:T(8,128)S(1)}, u32[]{:S(2)}, u32[]{:S(2)}) collective-permute-start(f32[2,16,8,128]{3,2,1,0:T(8,128)S(1)} %get-tuple-element.33.r_cross), channel_id=1, source_target_pairs={{0,1},{1,0},{2,3},{3,2},{4,5},{5,4},{6,7},{7,6},{8,9},{9,8},{10,11... | collective-permute-start | bytes 393224 | tf_op jit(solution)/shard_map/ppermute | solution.py:455
  62.5 1.8 %collective-permute-done.23.refs_7_ = f32[4,18,2,8,128]{4,3,2,1,0:T(8,128)S(1)} collective-permute-done((f32[4,18,2,8,128]{4,3,2,1,0:T(8,128)S(1)}, f32[4,18,2,8,128]{4,3,2,1,0:T(8,128)S(1)}, u32[]{:S(2)}, u32[]{:S(2)}) %collective-permute-start.23) | collective-permute-done | bytes 589856 | tf_op jit(solution)/shard_map/ppermute | solution.py:460
  66.8 5.6 %collective-permute-done.25.one = f32[2,16,8,128]{3,2,1,0:T(8,128)S(1)} collective-permute-done((f32[2,16,8,128]{3,2,1,0:T(8,128)S(1)}, f32[2,16,8,128]{3,2,1,0:T(8,128)S(1)}, u32[]{:S(2)}, u32[]{:S(2)}) %collective-permute-start.25) | collective-permute-done | bytes 131104 | tf_op jit(solution)/shard_map/ppermute | solution.py:465
  72.4 4.2 %collective-permute-start.26 = (f32[2,16,8,128]{3,2,1,0:T(8,128)S(1)}, f32[2,16,8,128]{3,2,1,0:T(8,128)S(1)}, u32[]{:S(2)}, u32[]{:S(2)}) collective-permute-start(f32[2,16,8,128]{3,2,1,0:T(8,128)S(1)} %collective-permute-done.25.one), channel_id=1, source_target_pairs={{0,1},{1,0},{2,3},{3,2},{4,5},{5,4},{6,7},{7,6},{8,9},{9,8},{10,11... | collective-permute-start | bytes 393224 | tf_op jit(solution)/shard_map/ppermute | solution.py:455
  79.0 6.2 %collective-permute-done.29.one = f32[2,16,8,128]{3,2,1,0:T(8,128)S(1)} collective-permute-done((f32[2,16,8,128]{3,2,1,0:T(8,128)S(1)}, f32[2,16,8,128]{3,2,1,0:T(8,128)S(1)}, u32[]{:S(2)}, u32[]{:S(2)}) %collective-permute-start.29) | collective-permute-done | bytes 131104 | tf_op jit(solution)/shard_map/ppermute | solution.py:465
  85.2 3.1 %collective-permute-start.30 = (f32[2,16,8,128]{3,2,1,0:T(8,128)S(1)}, f32[2,16,8,128]{3,2,1,0:T(8,128)S(1)}, u32[]{:S(2)}, u32[]{:S(2)}) collective-permute-start(f32[2,16,8,128]{3,2,1,0:T(8,128)S(1)} %collective-permute-done.29.one), channel_id=1, source_target_pairs={{0,1},{1,0},{2,3},{3,2},{4,5},{5,4},{6,7},{7,6},{8,9},{9,8},{10,11... | collective-permute-start | bytes 393224 | tf_op jit(solution)/shard_map/ppermute | solution.py:455
  91.8 4.4 %collective-permute-done.33.one = f32[2,16,8,128]{3,2,1,0:T(8,128)S(1)} collective-permute-done((f32[2,16,8,128]{3,2,1,0:T(8,128)S(1)}, f32[2,16,8,128]{3,2,1,0:T(8,128)S(1)}, u32[]{:S(2)}, u32[]{:S(2)}) %collective-permute-start.33) | collective-permute-done | bytes 131104 | tf_op jit(solution)/shard_map/ppermute | solution.py:465
  96.2 3.4 %collective-permute-start.34 = (f32[2,16,8,128]{3,2,1,0:T(8,128)S(1)}, f32[2,16,8,128]{3,2,1,0:T(8,128)S(1)}, u32[]{:S(2)}, u32[]{:S(2)}) collective-permute-start(f32[2,16,8,128]{3,2,1,0:T(8,128)S(1)} %collective-permute-done.33.one), channel_id=1, source_target_pairs={{0,1},{1,0},{2,3},{3,2},{4,5},{5,4},{6,7},{7,6},{8,9},{9,8},{10,11... | collective-permute-start | bytes 393224 | tf_op jit(solution)/shard_map/ppermute | solution.py:455
  101.7 5.8 %collective-permute-done.35.near = f32[2,2,16,8,128]{4,3,2,1,0:T(8,128)S(1)} collective-permute-done((f32[2,2,16,8,128]{4,3,2,1,0:T(8,128)S(1)}, f32[2,2,16,8,128]{4,3,2,1,0:T(8,128)S(1)}, u32[]{:S(2)}, u32[]{:S(2)}) %collective-permute-start.35) | collective-permute-done | bytes 262176 | tf_op jit(solution)/shard_map/ppermute | solution.py:460
  107.5 3.5 %collective-permute-start.36 = (f32[2,2,16,8,128]{4,3,2,1,0:T(8,128)S(1)}, f32[2,2,16,8,128]{4,3,2,1,0:T(8,128)S(1)}, u32[]{:S(2)}, u32[]{:S(2)}) collective-permute-start(f32[2,2,16,8,128]{4,3,2,1,0:T(8,128)S(1)} %collective-permute-done.35.near), channel_id=1, source_target_pairs={{0,1},{1,0},{2,3},{3,2},{4,5},{5,4},{6,7},{7,6},{8,9},{9,8},{10,11... | collective-permute-start | bytes 786440 | tf_op jit(solution)/shard_map/ppermute | solution.py:455
  112.6 1.5 %finish.1 = f32[2,2,256,256]{3,2,1,0:T(8,128)} custom-call(f32[2,16,8,128]{3,2,1,0:T(8,128)S(1)} %get-tuple-element.34.end, f32[2,16,8,128]{3,2,1,0:T(8,128)S(1)} %walk1.1.chained, f32[4,2,2,8,128]{4,3,2,1,0:T(8,128)S(1)} %heun_a3.1.after.refs_0_, f32[4,8,2,8,128]{4,3,2,1,0:T(8,128)S(1)} %heun_b3.1.after.refs_1_, f32[4,22,2,8,128]{4,3,2,1,0:T(8,128)S(1)} %heun_c3.1.refs_2_), custom_call_target="tpu_custom_call" | custom-call | tf_op jit(solution)/shard_map/finish/pallas_call | solution.py:438
  (81 shorter events, 26.9 us)
Async XLA Ops:
  2.9 13.3 %collective-permute-start.3 = (f32[6,18,2,8,128]{4,3,2,1,0:T(8,128)S(1)}, f32[6,18,2,8,128]{4,3,2,1,0:T(8,128)S(1)}, u32[]{:S(2)}, u32[]{:S(2)}) collective-permute-start(f32[6,18,2,8,128]{4,3,2,1,0:T(8,128)S(1)} %get-tuple-element.30.refs_3_.refs_6_.refs_9_.refs_4_), channel_id=1, source_target_pairs={{0,31},{1,2},{2,1},{3,4},{4,3},{5,6},{6,5},{7,8},{8,7},{9,10},{10,... | collective-permute-start | bytes 2654216 | tf_op jit(solution)/shard_map/ppermute | solution.py:460
  5.6 14.7 %collective-permute-start = (f32[6,18,2,8,128]{4,3,2,1,0:T(8,128)S(1)}, f32[6,18,2,8,128]{4,3,2,1,0:T(8,128)S(1)}, u32[]{:S(2)}, u32[]{:S(2)}) collective-permute-start(f32[6,18,2,8,128]{4,3,2,1,0:T(8,128)S(1)} %get-tuple-element.24.refs_0_.after.refs_4_.refs_7_.refs_10_.refs_5_), channel_id=1, source_target_pairs={{0,1},{1,0},{2,3},{3,2},{4,5},{5,4},{6,7},{7,6},{8,9},{9,8},{10,11... | collective-permute-start | bytes 2654216 | tf_op jit(solution)/shard_map/ppermute | solution.py:455
  10.1 11.4 %collective-permute-start.4 = (f32[6,8,2,8,128]{4,3,2,1,0:T(8,128)S(1)}, f32[6,8,2,8,128]{4,3,2,1,0:T(8,128)S(1)}, u32[]{:S(2)}, u32[]{:S(2)}) collective-permute-start(f32[6,8,2,8,128]{4,3,2,1,0:T(8,128)S(1)} %get-tuple-element.31.refs_4_.refs_10_.refs_13_), channel_id=1, source_target_pairs={{0,31},{1,2},{2,1},{3,4},{4,3},{5,6},{6,5},{7,8},{8,7},{9,10},{10,... | collective-permute-start | bytes 1179656 | tf_op jit(solution)/shard_map/ppermute | solution.py:460
  10.1 16.5 %collective-permute-start.1 = (f32[6,8,2,8,128]{4,3,2,1,0:T(8,128)S(1)}, f32[6,8,2,8,128]{4,3,2,1,0:T(8,128)S(1)}, u32[]{:S(2)}, u32[]{:S(2)}) collective-permute-start(f32[6,8,2,8,128]{4,3,2,1,0:T(8,128)S(1)} %get-tuple-element.25.refs_1_.refs_3_.refs_11_.refs_14_), channel_id=1, source_target_pairs={{0,1},{1,0},{2,3},{3,2},{4,5},{5,4},{6,7},{7,6},{8,9},{9,8},{10,11... | collective-permute-start | bytes 1179656 | tf_op jit(solution)/shard_map/ppermute | solution.py:455
  10.8 16.3 %collective-permute-start.5 = (f32[6,6,2,8,128]{4,3,2,1,0:T(8,128)S(1)}, f32[6,6,2,8,128]{4,3,2,1,0:T(8,128)S(1)}, u32[]{:S(2)}, u32[]{:S(2)}) collective-permute-start(f32[6,6,2,8,128]{4,3,2,1,0:T(8,128)S(1)} %get-tuple-element.32.refs_5_.refs_17_), channel_id=1, source_target_pairs={{0,31},{1,2},{2,1},{3,4},{4,3},{5,6},{6,5},{7,8},{8,7},{9,10},{10,... | collective-permute-start | bytes 884744 | tf_op jit(solution)/shard_map/ppermute | solution.py:460
  16.2 13.9 %collective-permute-start.2 = (f32[6,6,2,8,128]{4,3,2,1,0:T(8,128)S(1)}, f32[6,6,2,8,128]{4,3,2,1,0:T(8,128)S(1)}, u32[]{:S(2)}, u32[]{:S(2)}) collective-permute-start(f32[6,6,2,8,128]{4,3,2,1,0:T(8,128)S(1)} %get-tuple-element.26.refs_2_.refs_6_.refs_18_), channel_id=1, source_target_pairs={{0,1},{1,0},{2,3},{3,2},{4,5},{5,4},{6,7},{7,6},{8,9},{9,8},{10,11... | collective-permute-start | bytes 884744 | tf_op jit(solution)/shard_map/ppermute | solution.py:455
  21.4 9.5 %collective-permute-start.6 = (f32[4,14,2,8,128]{4,3,2,1,0:T(8,128)S(1)}, f32[4,14,2,8,128]{4,3,2,1,0:T(8,128)S(1)}, u32[]{:S(2)}, u32[]{:S(2)}) collective-permute-start(f32[4,14,2,8,128]{4,3,2,1,0:T(8,128)S(1)} %heun_a0.1.after.refs_0_), channel_id=1, source_target_pairs={{0,31},{1,2},{2,1},{3,4},{4,3},{5,6},{6,5},{7,8},{8,7},{9,10},{10,... | collective-permute-start | bytes 1376264 | tf_op jit(solution)/shard_map/ppermute | solution.py:460
  21.5 12.1 %collective-permute-start.7 = (f32[4,14,2,8,128]{4,3,2,1,0:T(8,128)S(1)}, f32[4,14,2,8,128]{4,3,2,1,0:T(8,128)S(1)}, u32[]{:S(2)}, u32[]{:S(2)}) collective-permute-start(f32[4,14,2,8,128]{4,3,2,1,0:T(8,128)S(1)} %heun_a0.1.after.refs_0_), channel_id=1, source_target_pairs={{0,1},{1,0},{2,3},{3,2},{4,5},{5,4},{6,7},{7,6},{8,9},{9,8},{10,11... | collective-permute-start | bytes 1376264 | tf_op jit(solution)/shard_map/ppermute | solution.py:455
  27.0 7.7 %collective-permute-start.8 = (f32[4,8,2,8,128]{4,3,2,1,0:T(8,128)S(1)}, f32[4,8,2,8,128]{4,3,2,1,0:T(8,128)S(1)}, u32[]{:S(2)}, u32[]{:S(2)}) collective-permute-start(f32[4,8,2,8,128]{4,3,2,1,0:T(8,128)S(1)} %heun_b0.1.after.refs_3_), channel_id=1, source_target_pairs={{0,31},{1,2},{2,1},{3,4},{4,3},{5,6},{6,5},{7,8},{8,7},{9,10},{10,... | collective-permute-start | bytes 786440 | tf_op jit(solution)/shard_map/ppermute | solution.py:460
  27.1 11.7 %collective-permute-start.9 = (f32[4,8,2,8,128]{4,3,2,1,0:T(8,128)S(1)}, f32[4,8,2,8,128]{4,3,2,1,0:T(8,128)S(1)}, u32[]{:S(2)}, u32[]{:S(2)}) collective-permute-start(f32[4,8,2,8,128]{4,3,2,1,0:T(8,128)S(1)} %heun_b0.1.after.refs_3_), channel_id=1, source_target_pairs={{0,1},{1,0},{2,3},{3,2},{4,5},{5,4},{6,7},{7,6},{8,9},{9,8},{10,11... | collective-permute-start | bytes 786440 | tf_op jit(solution)/shard_map/ppermute | solution.py:455
  30.5 8.8 %collective-permute-start.10 = (f32[4,10,2,8,128]{4,3,2,1,0:T(8,128)S(1)}, f32[4,10,2,8,128]{4,3,2,1,0:T(8,128)S(1)}, u32[]{:S(2)}, u32[]{:S(2)}) collective-permute-start(f32[4,10,2,8,128]{4,3,2,1,0:T(8,128)S(1)} %heun_c0.1.after.refs_6_), channel_id=1, source_target_pairs={{0,31},{1,2},{2,1},{3,4},{4,3},{5,6},{6,5},{7,8},{8,7},{9,10},{10,... | collective-permute-start | bytes 983048 | tf_op jit(solution)/shard_map/ppermute | solution.py:460
  30.9 10.2 %collective-permute-start.11 = (f32[4,10,2,8,128]{4,3,2,1,0:T(8,128)S(1)}, f32[4,10,2,8,128]{4,3,2,1,0:T(8,128)S(1)}, u32[]{:S(2)}, u32[]{:S(2)}) collective-permute-start(f32[4,10,2,8,128]{4,3,2,1,0:T(8,128)S(1)} %heun_c0.1.after.refs_6_), channel_id=1, source_target_pairs={{0,1},{1,0},{2,3},{3,2},{4,5},{5,4},{6,7},{7,6},{8,9},{9,8},{10,11... | collective-permute-start | bytes 983048 | tf_op jit(solution)/shard_map/ppermute | solution.py:455
  34.7 10.5 %collective-permute-start.13 = (f32[4,10,2,8,128]{4,3,2,1,0:T(8,128)S(1)}, f32[4,10,2,8,128]{4,3,2,1,0:T(8,128)S(1)}, u32[]{:S(2)}, u32[]{:S(2)}) collective-permute-start(f32[4,10,2,8,128]{4,3,2,1,0:T(8,128)S(1)} %heun_a1.1.after.refs_1_.refs_0_), channel_id=1, source_target_pairs={{0,1},{1,0},{2,3},{3,2},{4,5},{5,4},{6,7},{7,6},{8,9},{9,8},{10,11... | collective-permute-start | bytes 983048 | tf_op jit(solution)/shard_map/ppermute | solution.py:455
  39.3 9.7 %collective-permute-start.17 = (f32[4,8,2,8,128]{4,3,2,1,0:T(8,128)S(1)}, f32[4,8,2,8,128]{4,3,2,1,0:T(8,128)S(1)}, u32[]{:S(2)}, u32[]{:S(2)}) collective-permute-start(f32[4,8,2,8,128]{4,3,2,1,0:T(8,128)S(1)} %heun_b1.1.after.refs_3_), channel_id=1, source_target_pairs={{0,1},{1,0},{2,3},{3,2},{4,5},{5,4},{6,7},{7,6},{8,9},{9,8},{10,11... | collective-permute-start | bytes 786440 | tf_op jit(solution)/shard_map/ppermute | solution.py:455
  41.7 8.6 %collective-permute-start.18 = (f32[4,14,2,8,128]{4,3,2,1,0:T(8,128)S(1)}, f32[4,14,2,8,128]{4,3,2,1,0:T(8,128)S(1)}, u32[]{:S(2)}, u32[]{:S(2)}) collective-permute-start(f32[4,14,2,8,128]{4,3,2,1,0:T(8,128)S(1)} %heun_c1.1.after.refs_6_), channel_id=1, source_target_pairs={{0,31},{1,2},{2,1},{3,4},{4,3},{5,6},{6,5},{7,8},{8,7},{9,10},{10,... | collective-permute-start | bytes 1376264 | tf_op jit(solution)/shard_map/ppermute | solution.py:460
  41.8 11.5 %collective-permute-start.19 = (f32[4,14,2,8,128]{4,3,2,1,0:T(8,128)S(1)}, f32[4,14,2,8,128]{4,3,2,1,0:T(8,128)S(1)}, u32[]{:S(2)}, u32[]{:S(2)}) collective-permute-start(f32[4,14,2,8,128]{4,3,2,1,0:T(8,128)S(1)} %heun_c1.1.after.refs_6_), channel_id=1, source_target_pairs={{0,1},{1,0},{2,3},{3,2},{4,5},{5,4},{6,7},{7,6},{8,9},{9,8},{10,11... | collective-permute-start | bytes 1376264 | tf_op jit(solution)/shard_map/ppermute | solution.py:455
  45.4 9.8 %collective-permute-start.14 = (f32[112,8,128]{2,1,0:T(8,128)S(1)}, f32[112,8,128]{2,1,0:T(8,128)S(1)}, u32[]{:S(2)}, u32[]{:S(2)}) collective-permute-start(f32[112,8,128]{2,1,0:T(8,128)S(1)} %heun_a2.1.after.refs_0_), channel_id=1, source_target_pairs={{0,31},{1,2},{2,1},{3,4},{4,3},{5,6},{6,5},{7,8},{8,7},{9,10},{10,... | collective-permute-start | bytes 1376264 | tf_op jit(solution)/shard_map/ppermute | solution.py:460
  45.5 12.7 %collective-permute-start.15 = (f32[112,8,128]{2,1,0:T(8,128)S(1)}, f32[112,8,128]{2,1,0:T(8,128)S(1)}, u32[]{:S(2)}, u32[]{:S(2)}) collective-permute-start(f32[112,8,128]{2,1,0:T(8,128)S(1)} %heun_a2.1.after.refs_0_), channel_id=1, source_target_pairs={{0,1},{1,0},{2,3},{3,2},{4,5},{5,4},{6,7},{7,6},{8,9},{9,8},{10,11... | collective-permute-start | bytes 1376264 | tf_op jit(solution)/shard_map/ppermute | solution.py:455
  49.4 9.0 %collective-permute-start.20 = (f32[4,8,2,8,128]{4,3,2,1,0:T(8,128)S(1)}, f32[4,8,2,8,128]{4,3,2,1,0:T(8,128)S(1)}, u32[]{:S(2)}, u32[]{:S(2)}) collective-permute-start(f32[4,8,2,8,128]{4,3,2,1,0:T(8,128)S(1)} %heun_b2.1.after.refs_3_), channel_id=1, source_target_pairs={{0,31},{1,2},{2,1},{3,4},{4,3},{5,6},{6,5},{7,8},{8,7},{9,10},{10,... | collective-permute-start | bytes 786440 | tf_op jit(solution)/shard_map/ppermute | solution.py:460
  50.3 8.2 %collective-permute-start.21 = (f32[4,8,2,8,128]{4,3,2,1,0:T(8,128)S(1)}, f32[4,8,2,8,128]{4,3,2,1,0:T(8,128)S(1)}, u32[]{:S(2)}, u32[]{:S(2)}) collective-permute-start(f32[4,8,2,8,128]{4,3,2,1,0:T(8,128)S(1)} %heun_b2.1.after.refs_3_), channel_id=1, source_target_pairs={{0,1},{1,0},{2,3},{3,2},{4,5},{5,4},{6,7},{7,6},{8,9},{9,8},{10,11... | collective-permute-start | bytes 786440 | tf_op jit(solution)/shard_map/ppermute | solution.py:455
  54.2 10.2 %collective-permute-start.23 = (f32[4,18,2,8,128]{4,3,2,1,0:T(8,128)S(1)}, f32[4,18,2,8,128]{4,3,2,1,0:T(8,128)S(1)}, u32[]{:S(2)}, u32[]{:S(2)}) collective-permute-start(f32[4,18,2,8,128]{4,3,2,1,0:T(8,128)S(1)} %heun_c2.1.after.refs_6_), channel_id=1, source_target_pairs={{0,31},{1,2},{2,1},{3,4},{4,3},{5,6},{6,5},{7,8},{8,7},{9,10},{10,... | collective-permute-start | bytes 1769480 | tf_op jit(solution)/shard_map/ppermute | solution.py:460
  55.2 9.1 %collective-permute-start.24 = (f32[4,18,2,8,128]{4,3,2,1,0:T(8,128)S(1)}, f32[4,18,2,8,128]{4,3,2,1,0:T(8,128)S(1)}, u32[]{:S(2)}, u32[]{:S(2)}) collective-permute-start(f32[4,18,2,8,128]{4,3,2,1,0:T(8,128)S(1)} %heun_c2.1.after.refs_6_), channel_id=1, source_target_pairs={{0,1},{1,0},{2,3},{3,2},{4,5},{5,4},{6,7},{7,6},{8,9},{9,8},{10,11... | collective-permute-start | bytes 1769480 | tf_op jit(solution)/shard_map/ppermute | solution.py:455
  77.6 10.7 %collective-permute-start.27 = (f32[2,2,16,8,128]{4,3,2,1,0:T(8,128)S(1)}, f32[2,2,16,8,128]{4,3,2,1,0:T(8,128)S(1)}, u32[]{:S(2)}, u32[]{:S(2)}) collective-permute-start(f32[2,2,16,8,128]{4,3,2,1,0:T(8,128)S(1)} %pack.3.both), channel_id=1, source_target_pairs={{0,31},{1,2},{2,1},{3,4},{4,3},{5,6},{6,5},{7,8},{8,7},{9,10},{10,... | collective-permute-start | bytes 786440 | tf_op jit(solution)/shard_map/ppermute | solution.py:460
  90.4 9.2 %collective-permute-start.31 = (f32[2,2,16,8,128]{4,3,2,1,0:T(8,128)S(1)}, f32[2,2,16,8,128]{4,3,2,1,0:T(8,128)S(1)}, u32[]{:S(2)}, u32[]{:S(2)}) collective-permute-start(f32[2,2,16,8,128]{4,3,2,1,0:T(8,128)S(1)} %walk3.1.both), channel_id=1, source_target_pairs={{0,31},{1,2},{2,1},{3,4},{4,3},{5,6},{6,5},{7,8},{8,7},{9,10},{10,... | collective-permute-start | bytes 786440 | tf_op jit(solution)/shard_map/ppermute | solution.py:460
  (16 other events, 68.1 us)

commit v6 on v5

--- a/solution.py
+++ b/solution.py
@@ -89,7 +89,7 @@
 
 def prep(x, feed, kill):
     shapes = [jax.ShapeDtypeStruct((6, CUTS[c + 1] - CUTS[c], 2, 8, 128), F32) for c in range(CHUNKS)] * 2
-    scratch = [pltpu.VMEM((4, 2, 8 * STRIDE, 128), F32)]
+    scratch = [pltpu.VMEM((4, 2, 9 * STRIDE, 128), F32)]
     sent = pl.pallas_call(
         prep_kernel,
         out_shape=shapes,
@@ -106,7 +106,7 @@
             out_shape=shapes[:CHUNKS],
             in_specs=[VM] * (2 + CHUNKS),
             out_specs=[VM] * CHUNKS,
-            scratch_shapes=[pltpu.VMEM((2, 2, 8 * STRIDE, 128), F32)],
+            scratch_shapes=[pltpu.VMEM((2, 2, 9 * STRIDE, 128), F32)],
             input_output_aliases={2 + c: c for c in range(CHUNKS)},
             compiler_params=PARAMS,
             cost_estimate=pl.CostEstimate(flops=RATES_COST, bytes_accessed=1000, transcendentals=0),
@@ -441,7 +441,7 @@
         in_specs=[VM] * (2 + CHUNKS),
         out_specs=pl.BlockSpec(memory_space=pltpu.HBM),
         scratch_shapes=[
-            pltpu.VMEM((4, 2, 8 * STRIDE, 128), F32),
+            pltpu.VMEM((4, 2, 9 * STRIDE, 128), F32),
             pltpu.VMEM((4, 256, 256), F32),
             pltpu.SemaphoreType.DMA((4,)),
         ],

time: 115 us -> 115 us (level)
  no operation moved by 1% of the time
where the time goes in v6:
time: 115 us; the launch traced here: 114 us
  starting transfers between devices  64.1 us (56%)
  waiting for transfers between devices  35.9 us (31%)
  Pallas kernels  12.1 us (11%)
  local copies, waits for them, and re-layouts  1.7 us (1%)
    ppermute x19, starting transfers between devices, swap_pair(): return lax.ppermute(x, 'space', [(i, i ^ 1) for i in range(n)])  55.8 us
    ppermute x3, waiting for transfers between devices, later(): lax.ppermute(x, 'tm', [(i, i + distance) for i in range(n - distance)])  16.2 us
    ppermute x15, waiting for transfers between devices, swap_cross(): lax.ppermute(x, 'space', [(i, (i + 1) % n if i % 2 else (i - 1) % n) for...  13.7 us
    pallas_call x12, Pallas kernels, heun(): pl.pallas_call(functools.partial(heun_kernel, step, c), out_shape=jax.Sha...  7.03 us
    ppermute x19, waiting for transfers between devices, swap_pair(): return lax.ppermute(x, 'space', [(i, i ^ 1) for i in range(n)])  5.97 us
    ppermute x15, starting transfers between devices, swap_cross(): lax.ppermute(x, 'space', [(i, (i + 1) % n if i % 2 else (i - 1) % n) for...  4.37 us
    ppermute x3, starting transfers between devices, later(): lax.ppermute(x, 'tm', [(i, i + distance) for i in range(n - distance)])  3.88 us
  transfers between devices with their start and end apart: 37, of which 15 were waited for; matrix products, arithmetic and copies ran while one was open for 0% of the time, Pallas kernels for 6%

profile of v6, /device:TPU:7, one launch (start us, length us, event | category | flops | bytes accessed | tf_op | source)
XLA Modules:
  0.0 114.3 jit_solution(1141700401399169906)
XLA Ops:
  2.9 2.3 %collective-permute-start.3 = (f32[6,18,2,8,128]{4,3,2,1,0:T(8,128)S(1)}, f32[6,18,2,8,128]{4,3,2,1,0:T(8,128)S(1)}, u32[]{:S(2)}, u32[]{:S(2)}) collective-permute-start(f32[6,18,2,8,128]{4,3,2,1,0:T(8,128)S(1)} %get-tuple-element.30.refs_3_.refs_6_.refs_9_.refs_4_), channel_id=1, source_target_pairs={{0,31},{1,2},{2,1},{3,4},{4,3},{5,6},{6,5},{7,8},{8,7},{9,10},{10,... | collective-permute-start | bytes 2654216 | tf_op jit(solution)/shard_map/ppermute | solution.py:460
  5.6 4.5 %collective-permute-start = (f32[6,18,2,8,128]{4,3,2,1,0:T(8,128)S(1)}, f32[6,18,2,8,128]{4,3,2,1,0:T(8,128)S(1)}, u32[]{:S(2)}, u32[]{:S(2)}) collective-permute-start(f32[6,18,2,8,128]{4,3,2,1,0:T(8,128)S(1)} %get-tuple-element.24.refs_0_.after.refs_4_.refs_7_.refs_10_.refs_5_), channel_id=1, source_target_pairs={{0,1},{1,0},{2,3},{3,2},{4,5},{5,4},{6,7},{7,6},{8,9},{9,8},{10,11... | collective-permute-start | bytes 2654216 | tf_op jit(solution)/shard_map/ppermute | solution.py:455
  11.8 4.3 %collective-permute-done.3.refs_9_.refs_1_.refs_5_.refs_8_.refs_11_.refs_6_ = f32[6,18,2,8,128]{4,3,2,1,0:T(8,128)S(1)} collective-permute-done((f32[6,18,2,8,128]{4,3,2,1,0:T(8,128)S(1)}, f32[6,18,2,8,128]{4,3,2,1,0:T(8,128)S(1)}, u32[]{:S(2)}, u32[]{:S(2)}) %collective-permute-start.3) | collective-permute-done | bytes 884768 | tf_op jit(solution)/shard_map/ppermute | solution.py:460
  16.2 4.1 %collective-permute-start.2 = (f32[6,6,2,8,128]{4,3,2,1,0:T(8,128)S(1)}, f32[6,6,2,8,128]{4,3,2,1,0:T(8,128)S(1)}, u32[]{:S(2)}, u32[]{:S(2)}) collective-permute-start(f32[6,6,2,8,128]{4,3,2,1,0:T(8,128)S(1)} %get-tuple-element.26.refs_2_.refs_6_.refs_18_), channel_id=1, source_target_pairs={{0,1},{1,0},{2,3},{3,2},{4,5},{5,4},{6,7},{7,6},{8,9},{9,8},{10,11... | collective-permute-start | bytes 884744 | tf_op jit(solution)/shard_map/ppermute | solution.py:455
  21.5 5.0 %collective-permute-start.7 = (f32[4,14,2,8,128]{4,3,2,1,0:T(8,128)S(1)}, f32[4,14,2,8,128]{4,3,2,1,0:T(8,128)S(1)}, u32[]{:S(2)}, u32[]{:S(2)}) collective-permute-start(f32[4,14,2,8,128]{4,3,2,1,0:T(8,128)S(1)} %heun_a0.1.after.refs_0_), channel_id=1, source_target_pairs={{0,1},{1,0},{2,3},{3,2},{4,5},{5,4},{6,7},{7,6},{8,9},{9,8},{10,11... | collective-permute-start | bytes 1376264 | tf_op jit(solution)/shard_map/ppermute | solution.py:455
  27.1 3.0 %collective-permute-start.9 = (f32[4,8,2,8,128]{4,3,2,1,0:T(8,128)S(1)}, f32[4,8,2,8,128]{4,3,2,1,0:T(8,128)S(1)}, u32[]{:S(2)}, u32[]{:S(2)}) collective-permute-start(f32[4,8,2,8,128]{4,3,2,1,0:T(8,128)S(1)} %heun_b0.1.after.refs_3_), channel_id=1, source_target_pairs={{0,1},{1,0},{2,3},{3,2},{4,5},{5,4},{6,7},{7,6},{8,9},{9,8},{10,11... | collective-permute-start | bytes 786440 | tf_op jit(solution)/shard_map/ppermute | solution.py:455
  30.9 2.7 %collective-permute-start.11 = (f32[4,10,2,8,128]{4,3,2,1,0:T(8,128)S(1)}, f32[4,10,2,8,128]{4,3,2,1,0:T(8,128)S(1)}, u32[]{:S(2)}, u32[]{:S(2)}) collective-permute-start(f32[4,10,2,8,128]{4,3,2,1,0:T(8,128)S(1)} %heun_c0.1.after.refs_6_), channel_id=1, source_target_pairs={{0,1},{1,0},{2,3},{3,2},{4,5},{5,4},{6,7},{7,6},{8,9},{9,8},{10,11... | collective-permute-start | bytes 983048 | tf_op jit(solution)/shard_map/ppermute | solution.py:455
  34.7 4.1 %collective-permute-start.13 = (f32[4,10,2,8,128]{4,3,2,1,0:T(8,128)S(1)}, f32[4,10,2,8,128]{4,3,2,1,0:T(8,128)S(1)}, u32[]{:S(2)}, u32[]{:S(2)}) collective-permute-start(f32[4,10,2,8,128]{4,3,2,1,0:T(8,128)S(1)} %heun_a1.1.after.refs_1_.refs_0_), channel_id=1, source_target_pairs={{0,1},{1,0},{2,3},{3,2},{4,5},{5,4},{6,7},{7,6},{8,9},{9,8},{10,11... | collective-permute-start | bytes 983048 | tf_op jit(solution)/shard_map/ppermute | solution.py:455
  39.3 1.8 %collective-permute-start.17 = (f32[4,8,2,8,128]{4,3,2,1,0:T(8,128)S(1)}, f32[4,8,2,8,128]{4,3,2,1,0:T(8,128)S(1)}, u32[]{:S(2)}, u32[]{:S(2)}) collective-permute-start(f32[4,8,2,8,128]{4,3,2,1,0:T(8,128)S(1)} %heun_b1.1.after.refs_3_), channel_id=1, source_target_pairs={{0,1},{1,0},{2,3},{3,2},{4,5},{5,4},{6,7},{7,6},{8,9},{9,8},{10,11... | collective-permute-start | bytes 786440 | tf_op jit(solution)/shard_map/ppermute | solution.py:455
  41.8 3.3 %collective-permute-start.19 = (f32[4,14,2,8,128]{4,3,2,1,0:T(8,128)S(1)}, f32[4,14,2,8,128]{4,3,2,1,0:T(8,128)S(1)}, u32[]{:S(2)}, u32[]{:S(2)}) collective-permute-start(f32[4,14,2,8,128]{4,3,2,1,0:T(8,128)S(1)} %heun_c1.1.after.refs_6_), channel_id=1, source_target_pairs={{0,1},{1,0},{2,3},{3,2},{4,5},{5,4},{6,7},{7,6},{8,9},{9,8},{10,11... | collective-permute-start | bytes 1376264 | tf_op jit(solution)/shard_map/ppermute | solution.py:455
  45.5 3.5 %collective-permute-start.15 = (f32[112,8,128]{2,1,0:T(8,128)S(1)}, f32[112,8,128]{2,1,0:T(8,128)S(1)}, u32[]{:S(2)}, u32[]{:S(2)}) collective-permute-start(f32[112,8,128]{2,1,0:T(8,128)S(1)} %heun_a2.1.after.refs_0_), channel_id=1, source_target_pairs={{0,1},{1,0},{2,3},{3,2},{4,5},{5,4},{6,7},{7,6},{8,9},{9,8},{10,11... | collective-permute-start | bytes 1376264 | tf_op jit(solution)/shard_map/ppermute | solution.py:455
  50.3 3.0 %collective-permute-start.21 = (f32[4,8,2,8,128]{4,3,2,1,0:T(8,128)S(1)}, f32[4,8,2,8,128]{4,3,2,1,0:T(8,128)S(1)}, u32[]{:S(2)}, u32[]{:S(2)}) collective-permute-start(f32[4,8,2,8,128]{4,3,2,1,0:T(8,128)S(1)} %heun_b2.1.after.refs_3_), channel_id=1, source_target_pairs={{0,1},{1,0},{2,3},{3,2},{4,5},{5,4},{6,7},{7,6},{8,9},{9,8},{10,11... | collective-permute-start | bytes 786440 | tf_op jit(solution)/shard_map/ppermute | solution.py:455
  55.2 3.0 %collective-permute-start.24 = (f32[4,18,2,8,128]{4,3,2,1,0:T(8,128)S(1)}, f32[4,18,2,8,128]{4,3,2,1,0:T(8,128)S(1)}, u32[]{:S(2)}, u32[]{:S(2)}) collective-permute-start(f32[4,18,2,8,128]{4,3,2,1,0:T(8,128)S(1)} %heun_c2.1.after.refs_6_), channel_id=1, source_target_pairs={{0,1},{1,0},{2,3},{3,2},{4,5},{5,4},{6,7},{7,6},{8,9},{9,8},{10,11... | collective-permute-start | bytes 1769480 | tf_op jit(solution)/shard_map/ppermute | solution.py:455
  58.9 2.7 %collective-permute-start.22 = (f32[2,16,8,128]{3,2,1,0:T(8,128)S(1)}, f32[2,16,8,128]{3,2,1,0:T(8,128)S(1)}, u32[]{:S(2)}, u32[]{:S(2)}) collective-permute-start(f32[2,16,8,128]{3,2,1,0:T(8,128)S(1)} %get-tuple-element.33.r_cross), channel_id=1, source_target_pairs={{0,1},{1,0},{2,3},{3,2},{4,5},{5,4},{6,7},{7,6},{8,9},{9,8},{10,11... | collective-permute-start | bytes 393224 | tf_op jit(solution)/shard_map/ppermute | solution.py:455
  62.5 1.8 %collective-permute-done.23.refs_7_ = f32[4,18,2,8,128]{4,3,2,1,0:T(8,128)S(1)} collective-permute-done((f32[4,18,2,8,128]{4,3,2,1,0:T(8,128)S(1)}, f32[4,18,2,8,128]{4,3,2,1,0:T(8,128)S(1)}, u32[]{:S(2)}, u32[]{:S(2)}) %collective-permute-start.23) | collective-permute-done | bytes 589856 | tf_op jit(solution)/shard_map/ppermute | solution.py:460
  66.8 5.6 %collective-permute-done.25.one = f32[2,16,8,128]{3,2,1,0:T(8,128)S(1)} collective-permute-done((f32[2,16,8,128]{3,2,1,0:T(8,128)S(1)}, f32[2,16,8,128]{3,2,1,0:T(8,128)S(1)}, u32[]{:S(2)}, u32[]{:S(2)}) %collective-permute-start.25) | collective-permute-done | bytes 131104 | tf_op jit(solution)/shard_map/ppermute | solution.py:465
  72.4 4.2 %collective-permute-start.26 = (f32[2,16,8,128]{3,2,1,0:T(8,128)S(1)}, f32[2,16,8,128]{3,2,1,0:T(8,128)S(1)}, u32[]{:S(2)}, u32[]{:S(2)}) collective-permute-start(f32[2,16,8,128]{3,2,1,0:T(8,128)S(1)} %collective-permute-done.25.one), channel_id=1, source_target_pairs={{0,1},{1,0},{2,3},{3,2},{4,5},{5,4},{6,7},{7,6},{8,9},{9,8},{10,11... | collective-permute-start | bytes 393224 | tf_op jit(solution)/shard_map/ppermute | solution.py:455
  79.0 6.2 %collective-permute-done.29.one = f32[2,16,8,128]{3,2,1,0:T(8,128)S(1)} collective-permute-done((f32[2,16,8,128]{3,2,1,0:T(8,128)S(1)}, f32[2,16,8,128]{3,2,1,0:T(8,128)S(1)}, u32[]{:S(2)}, u32[]{:S(2)}) %collective-permute-start.29) | collective-permute-done | bytes 131104 | tf_op jit(solution)/shard_map/ppermute | solution.py:465
  85.2 3.1 %collective-permute-start.30 = (f32[2,16,8,128]{3,2,1,0:T(8,128)S(1)}, f32[2,16,8,128]{3,2,1,0:T(8,128)S(1)}, u32[]{:S(2)}, u32[]{:S(2)}) collective-permute-start(f32[2,16,8,128]{3,2,1,0:T(8,128)S(1)} %collective-permute-done.29.one), channel_id=1, source_target_pairs={{0,1},{1,0},{2,3},{3,2},{4,5},{5,4},{6,7},{7,6},{8,9},{9,8},{10,11... | collective-permute-start | bytes 393224 | tf_op jit(solution)/shard_map/ppermute | solution.py:455
  91.8 4.4 %collective-permute-done.33.one = f32[2,16,8,128]{3,2,1,0:T(8,128)S(1)} collective-permute-done((f32[2,16,8,128]{3,2,1,0:T(8,128)S(1)}, f32[2,16,8,128]{3,2,1,0:T(8,128)S(1)}, u32[]{:S(2)}, u32[]{:S(2)}) %collective-permute-start.33) | collective-permute-done | bytes 131104 | tf_op jit(solution)/shard_map/ppermute | solution.py:465
  96.2 3.4 %collective-permute-start.34 = (f32[2,16,8,128]{3,2,1,0:T(8,128)S(1)}, f32[2,16,8,128]{3,2,1,0:T(8,128)S(1)}, u32[]{:S(2)}, u32[]{:S(2)}) collective-permute-start(f32[2,16,8,128]{3,2,1,0:T(8,128)S(1)} %collective-permute-done.33.one), channel_id=1, source_target_pairs={{0,1},{1,0},{2,3},{3,2},{4,5},{5,4},{6,7},{7,6},{8,9},{9,8},{10,11... | collective-permute-start | bytes 393224 | tf_op jit(solution)/shard_map/ppermute | solution.py:455
  101.7 5.8 %collective-permute-done.35.near = f32[2,2,16,8,128]{4,3,2,1,0:T(8,128)S(1)} collective-permute-done((f32[2,2,16,8,128]{4,3,2,1,0:T(8,128)S(1)}, f32[2,2,16,8,128]{4,3,2,1,0:T(8,128)S(1)}, u32[]{:S(2)}, u32[]{:S(2)}) %collective-permute-start.35) | collective-permute-done | bytes 262176 | tf_op jit(solution)/shard_map/ppermute | solution.py:460
  107.5 3.5 %collective-permute-start.36 = (f32[2,2,16,8,128]{4,3,2,1,0:T(8,128)S(1)}, f32[2,2,16,8,128]{4,3,2,1,0:T(8,128)S(1)}, u32[]{:S(2)}, u32[]{:S(2)}) collective-permute-start(f32[2,2,16,8,128]{4,3,2,1,0:T(8,128)S(1)} %collective-permute-done.35.near), channel_id=1, source_target_pairs={{0,1},{1,0},{2,3},{3,2},{4,5},{5,4},{6,7},{7,6},{8,9},{9,8},{10,11... | collective-permute-start | bytes 786440 | tf_op jit(solution)/shard_map/ppermute | solution.py:455
  112.6 1.5 %finish.1 = f32[2,2,256,256]{3,2,1,0:T(8,128)} custom-call(f32[2,16,8,128]{3,2,1,0:T(8,128)S(1)} %get-tuple-element.34.end, f32[2,16,8,128]{3,2,1,0:T(8,128)S(1)} %walk1.1.chained, f32[4,2,2,8,128]{4,3,2,1,0:T(8,128)S(1)} %heun_a3.1.after.refs_0_, f32[4,8,2,8,128]{4,3,2,1,0:T(8,128)S(1)} %heun_b3.1.after.refs_1_, f32[4,22,2,8,128]{4,3,2,1,0:T(8,128)S(1)} %heun_c3.1.refs_2_), custom_call_target="tpu_custom_call" | custom-call | tf_op jit(solution)/shard_map/finish/pallas_call | solution.py:438
  (81 shorter events, 26.9 us)
Async XLA Ops:
  2.9 13.3 %collective-permute-start.3 = (f32[6,18,2,8,128]{4,3,2,1,0:T(8,128)S(1)}, f32[6,18,2,8,128]{4,3,2,1,0:T(8,128)S(1)}, u32[]{:S(2)}, u32[]{:S(2)}) collective-permute-start(f32[6,18,2,8,128]{4,3,2,1,0:T(8,128)S(1)} %get-tuple-element.30.refs_3_.refs_6_.refs_9_.refs_4_), channel_id=1, source_target_pairs={{0,31},{1,2},{2,1},{3,4},{4,3},{5,6},{6,5},{7,8},{8,7},{9,10},{10,... | collective-permute-start | bytes 2654216 | tf_op jit(solution)/shard_map/ppermute | solution.py:460
  5.6 14.7 %collective-permute-start = (f32[6,18,2,8,128]{4,3,2,1,0:T(8,128)S(1)}, f32[6,18,2,8,128]{4,3,2,1,0:T(8,128)S(1)}, u32[]{:S(2)}, u32[]{:S(2)}) collective-permute-start(f32[6,18,2,8,128]{4,3,2,1,0:T(8,128)S(1)} %get-tuple-element.24.refs_0_.after.refs_4_.refs_7_.refs_10_.refs_5_), channel_id=1, source_target_pairs={{0,1},{1,0},{2,3},{3,2},{4,5},{5,4},{6,7},{7,6},{8,9},{9,8},{10,11... | collective-permute-start | bytes 2654216 | tf_op jit(solution)/shard_map/ppermute | solution.py:455
  10.1 11.4 %collective-permute-start.4 = (f32[6,8,2,8,128]{4,3,2,1,0:T(8,128)S(1)}, f32[6,8,2,8,128]{4,3,2,1,0:T(8,128)S(1)}, u32[]{:S(2)}, u32[]{:S(2)}) collective-permute-start(f32[6,8,2,8,128]{4,3,2,1,0:T(8,128)S(1)} %get-tuple-element.31.refs_4_.refs_10_.refs_13_), channel_id=1, source_target_pairs={{0,31},{1,2},{2,1},{3,4},{4,3},{5,6},{6,5},{7,8},{8,7},{9,10},{10,... | collective-permute-start | bytes 1179656 | tf_op jit(solution)/shard_map/ppermute | solution.py:460
  10.1 16.5 %collective-permute-start.1 = (f32[6,8,2,8,128]{4,3,2,1,0:T(8,128)S(1)}, f32[6,8,2,8,128]{4,3,2,1,0:T(8,128)S(1)}, u32[]{:S(2)}, u32[]{:S(2)}) collective-permute-start(f32[6,8,2,8,128]{4,3,2,1,0:T(8,128)S(1)} %get-tuple-element.25.refs_1_.refs_3_.refs_11_.refs_14_), channel_id=1, source_target_pairs={{0,1},{1,0},{2,3},{3,2},{4,5},{5,4},{6,7},{7,6},{8,9},{9,8},{10,11... | collective-permute-start | bytes 1179656 | tf_op jit(solution)/shard_map/ppermute | solution.py:455
  10.8 16.3 %collective-permute-start.5 = (f32[6,6,2,8,128]{4,3,2,1,0:T(8,128)S(1)}, f32[6,6,2,8,128]{4,3,2,1,0:T(8,128)S(1)}, u32[]{:S(2)}, u32[]{:S(2)}) collective-permute-start(f32[6,6,2,8,128]{4,3,2,1,0:T(8,128)S(1)} %get-tuple-element.32.refs_5_.refs_17_), channel_id=1, source_target_pairs={{0,31},{1,2},{2,1},{3,4},{4,3},{5,6},{6,5},{7,8},{8,7},{9,10},{10,... | collective-permute-start | bytes 884744 | tf_op jit(solution)/shard_map/ppermute | solution.py:460
  16.2 13.9 %collective-permute-start.2 = (f32[6,6,2,8,128]{4,3,2,1,0:T(8,128)S(1)}, f32[6,6,2,8,128]{4,3,2,1,0:T(8,128)S(1)}, u32[]{:S(2)}, u32[]{:S(2)}) collective-permute-start(f32[6,6,2,8,128]{4,3,2,1,0:T(8,128)S(1)} %get-tuple-element.26.refs_2_.refs_6_.refs_18_), channel_id=1, source_target_pairs={{0,1},{1,0},{2,3},{3,2},{4,5},{5,4},{6,7},{7,6},{8,9},{9,8},{10,11... | collective-permute-start | bytes 884744 | tf_op jit(solution)/shard_map/ppermute | solution.py:455
  21.4 9.5 %collective-permute-start.6 = (f32[4,14,2,8,128]{4,3,2,1,0:T(8,128)S(1)}, f32[4,14,2,8,128]{4,3,2,1,0:T(8,128)S(1)}, u32[]{:S(2)}, u32[]{:S(2)}) collective-permute-start(f32[4,14,2,8,128]{4,3,2,1,0:T(8,128)S(1)} %heun_a0.1.after.refs_0_), channel_id=1, source_target_pairs={{0,31},{1,2},{2,1},{3,4},{4,3},{5,6},{6,5},{7,8},{8,7},{9,10},{10,... | collective-permute-start | bytes 1376264 | tf_op jit(solution)/shard_map/ppermute | solution.py:460
  21.5 12.1 %collective-permute-start.7 = (f32[4,14,2,8,128]{4,3,2,1,0:T(8,128)S(1)}, f32[4,14,2,8,128]{4,3,2,1,0:T(8,128)S(1)}, u32[]{:S(2)}, u32[]{:S(2)}) collective-permute-start(f32[4,14,2,8,128]{4,3,2,1,0:T(8,128)S(1)} %heun_a0.1.after.refs_0_), channel_id=1, source_target_pairs={{0,1},{1,0},{2,3},{3,2},{4,5},{5,4},{6,7},{7,6},{8,9},{9,8},{10,11... | collective-permute-start | bytes 1376264 | tf_op jit(solution)/shard_map/ppermute | solution.py:455
  27.0 7.7 %collective-permute-start.8 = (f32[4,8,2,8,128]{4,3,2,1,0:T(8,128)S(1)}, f32[4,8,2,8,128]{4,3,2,1,0:T(8,128)S(1)}, u32[]{:S(2)}, u32[]{:S(2)}) collective-permute-start(f32[4,8,2,8,128]{4,3,2,1,0:T(8,128)S(1)} %heun_b0.1.after.refs_3_), channel_id=1, source_target_pairs={{0,31},{1,2},{2,1},{3,4},{4,3},{5,6},{6,5},{7,8},{8,7},{9,10},{10,... | collective-permute-start | bytes 786440 | tf_op jit(solution)/shard_map/ppermute | solution.py:460
  27.1 11.7 %collective-permute-start.9 = (f32[4,8,2,8,128]{4,3,2,1,0:T(8,128)S(1)}, f32[4,8,2,8,128]{4,3,2,1,0:T(8,128)S(1)}, u32[]{:S(2)}, u32[]{:S(2)}) collective-permute-start(f32[4,8,2,8,128]{4,3,2,1,0:T(8,128)S(1)} %heun_b0.1.after.refs_3_), channel_id=1, source_target_pairs={{0,1},{1,0},{2,3},{3,2},{4,5},{5,4},{6,7},{7,6},{8,9},{9,8},{10,11... | collective-permute-start | bytes 786440 | tf_op jit(solution)/shard_map/ppermute | solution.py:455
  30.5 8.8 %collective-permute-start.10 = (f32[4,10,2,8,128]{4,3,2,1,0:T(8,128)S(1)}, f32[4,10,2,8,128]{4,3,2,1,0:T(8,128)S(1)}, u32[]{:S(2)}, u32[]{:S(2)}) collective-permute-start(f32[4,10,2,8,128]{4,3,2,1,0:T(8,128)S(1)} %heun_c0.1.after.refs_6_), channel_id=1, source_target_pairs={{0,31},{1,2},{2,1},{3,4},{4,3},{5,6},{6,5},{7,8},{8,7},{9,10},{10,... | collective-permute-start | bytes 983048 | tf_op jit(solution)/shard_map/ppermute | solution.py:460
  30.9 10.2 %collective-permute-start.11 = (f32[4,10,2,8,128]{4,3,2,1,0:T(8,128)S(1)}, f32[4,10,2,8,128]{4,3,2,1,0:T(8,128)S(1)}, u32[]{:S(2)}, u32[]{:S(2)}) collective-permute-start(f32[4,10,2,8,128]{4,3,2,1,0:T(8,128)S(1)} %heun_c0.1.after.refs_6_), channel_id=1, source_target_pairs={{0,1},{1,0},{2,3},{3,2},{4,5},{5,4},{6,7},{7,6},{8,9},{9,8},{10,11... | collective-permute-start | bytes 983048 | tf_op jit(solution)/shard_map/ppermute | solution.py:455
  34.7 10.5 %collective-permute-start.13 = (f32[4,10,2,8,128]{4,3,2,1,0:T(8,128)S(1)}, f32[4,10,2,8,128]{4,3,2,1,0:T(8,128)S(1)}, u32[]{:S(2)}, u32[]{:S(2)}) collective-permute-start(f32[4,10,2,8,128]{4,3,2,1,0:T(8,128)S(1)} %heun_a1.1.after.refs_1_.refs_0_), channel_id=1, source_target_pairs={{0,1},{1,0},{2,3},{3,2},{4,5},{5,4},{6,7},{7,6},{8,9},{9,8},{10,11... | collective-permute-start | bytes 983048 | tf_op jit(solution)/shard_map/ppermute | solution.py:455
  39.3 9.7 %collective-permute-start.17 = (f32[4,8,2,8,128]{4,3,2,1,0:T(8,128)S(1)}, f32[4,8,2,8,128]{4,3,2,1,0:T(8,128)S(1)}, u32[]{:S(2)}, u32[]{:S(2)}) collective-permute-start(f32[4,8,2,8,128]{4,3,2,1,0:T(8,128)S(1)} %heun_b1.1.after.refs_3_), channel_id=1, source_target_pairs={{0,1},{1,0},{2,3},{3,2},{4,5},{5,4},{6,7},{7,6},{8,9},{9,8},{10,11... | collective-permute-start | bytes 786440 | tf_op jit(solution)/shard_map/ppermute | solution.py:455
  41.7 8.6 %collective-permute-start.18 = (f32[4,14,2,8,128]{4,3,2,1,0:T(8,128)S(1)}, f32[4,14,2,8,128]{4,3,2,1,0:T(8,128)S(1)}, u32[]{:S(2)}, u32[]{:S(2)}) collective-permute-start(f32[4,14,2,8,128]{4,3,2,1,0:T(8,128)S(1)} %heun_c1.1.after.refs_6_), channel_id=1, source_target_pairs={{0,31},{1,2},{2,1},{3,4},{4,3},{5,6},{6,5},{7,8},{8,7},{9,10},{10,... | collective-permute-start | bytes 1376264 | tf_op jit(solution)/shard_map/ppermute | solution.py:460
  41.8 11.5 %collective-permute-start.19 = (f32[4,14,2,8,128]{4,3,2,1,0:T(8,128)S(1)}, f32[4,14,2,8,128]{4,3,2,1,0:T(8,128)S(1)}, u32[]{:S(2)}, u32[]{:S(2)}) collective-permute-start(f32[4,14,2,8,128]{4,3,2,1,0:T(8,128)S(1)} %heun_c1.1.after.refs_6_), channel_id=1, source_target_pairs={{0,1},{1,0},{2,3},{3,2},{4,5},{5,4},{6,7},{7,6},{8,9},{9,8},{10,11... | collective-permute-start | bytes 1376264 | tf_op jit(solution)/shard_map/ppermute | solution.py:455
  45.4 9.8 %collective-permute-start.14 = (f32[112,8,128]{2,1,0:T(8,128)S(1)}, f32[112,8,128]{2,1,0:T(8,128)S(1)}, u32[]{:S(2)}, u32[]{:S(2)}) collective-permute-start(f32[112,8,128]{2,1,0:T(8,128)S(1)} %heun_a2.1.after.refs_0_), channel_id=1, source_target_pairs={{0,31},{1,2},{2,1},{3,4},{4,3},{5,6},{6,5},{7,8},{8,7},{9,10},{10,... | collective-permute-start | bytes 1376264 | tf_op jit(solution)/shard_map/ppermute | solution.py:460
  45.5 12.7 %collective-permute-start.15 = (f32[112,8,128]{2,1,0:T(8,128)S(1)}, f32[112,8,128]{2,1,0:T(8,128)S(1)}, u32[]{:S(2)}, u32[]{:S(2)}) collective-permute-start(f32[112,8,128]{2,1,0:T(8,128)S(1)} %heun_a2.1.after.refs_0_), channel_id=1, source_target_pairs={{0,1},{1,0},{2,3},{3,2},{4,5},{5,4},{6,7},{7,6},{8,9},{9,8},{10,11... | collective-permute-start | bytes 1376264 | tf_op jit(solution)/shard_map/ppermute | solution.py:455
  49.4 9.0 %collective-permute-start.20 = (f32[4,8,2,8,128]{4,3,2,1,0:T(8,128)S(1)}, f32[4,8,2,8,128]{4,3,2,1,0:T(8,128)S(1)}, u32[]{:S(2)}, u32[]{:S(2)}) collective-permute-start(f32[4,8,2,8,128]{4,3,2,1,0:T(8,128)S(1)} %heun_b2.1.after.refs_3_), channel_id=1, source_target_pairs={{0,31},{1,2},{2,1},{3,4},{4,3},{5,6},{6,5},{7,8},{8,7},{9,10},{10,... | collective-permute-start | bytes 786440 | tf_op jit(solution)/shard_map/ppermute | solution.py:460
  50.3 8.2 %collective-permute-start.21 = (f32[4,8,2,8,128]{4,3,2,1,0:T(8,128)S(1)}, f32[4,8,2,8,128]{4,3,2,1,0:T(8,128)S(1)}, u32[]{:S(2)}, u32[]{:S(2)}) collective-permute-start(f32[4,8,2,8,128]{4,3,2,1,0:T(8,128)S(1)} %heun_b2.1.after.refs_3_), channel_id=1, source_target_pairs={{0,1},{1,0},{2,3},{3,2},{4,5},{5,4},{6,7},{7,6},{8,9},{9,8},{10,11... | collective-permute-start | bytes 786440 | tf_op jit(solution)/shard_map/ppermute | solution.py:455
  54.2 10.2 %collective-permute-start.23 = (f32[4,18,2,8,128]{4,3,2,1,0:T(8,128)S(1)}, f32[4,18,2,8,128]{4,3,2,1,0:T(8,128)S(1)}, u32[]{:S(2)}, u32[]{:S(2)}) collective-permute-start(f32[4,18,2,8,128]{4,3,2,1,0:T(8,128)S(1)} %heun_c2.1.after.refs_6_), channel_id=1, source_target_pairs={{0,31},{1,2},{2,1},{3,4},{4,3},{5,6},{6,5},{7,8},{8,7},{9,10},{10,... | collective-permute-start | bytes 1769480 | tf_op jit(solution)/shard_map/ppermute | solution.py:460
  55.2 9.1 %collective-permute-start.24 = (f32[4,18,2,8,128]{4,3,2,1,0:T(8,128)S(1)}, f32[4,18,2,8,128]{4,3,2,1,0:T(8,128)S(1)}, u32[]{:S(2)}, u32[]{:S(2)}) collective-permute-start(f32[4,18,2,8,128]{4,3,2,1,0:T(8,128)S(1)} %heun_c2.1.after.refs_6_), channel_id=1, source_target_pairs={{0,1},{1,0},{2,3},{3,2},{4,5},{5,4},{6,7},{7,6},{8,9},{9,8},{10,11... | collective-permute-start | bytes 1769480 | tf_op jit(solution)/shard_map/ppermute | solution.py:455
  77.6 10.7 %collective-permute-start.27 = (f32[2,2,16,8,128]{4,3,2,1,0:T(8,128)S(1)}, f32[2,2,16,8,128]{4,3,2,1,0:T(8,128)S(1)}, u32[]{:S(2)}, u32[]{:S(2)}) collective-permute-start(f32[2,2,16,8,128]{4,3,2,1,0:T(8,128)S(1)} %pack.3.both), channel_id=1, source_target_pairs={{0,31},{1,2},{2,1},{3,4},{4,3},{5,6},{6,5},{7,8},{8,7},{9,10},{10,... | collective-permute-start | bytes 786440 | tf_op jit(solution)/shard_map/ppermute | solution.py:460
  90.4 9.2 %collective-permute-start.31 = (f32[2,2,16,8,128]{4,3,2,1,0:T(8,128)S(1)}, f32[2,2,16,8,128]{4,3,2,1,0:T(8,128)S(1)}, u32[]{:S(2)}, u32[]{:S(2)}) collective-permute-start(f32[2,2,16,8,128]{4,3,2,1,0:T(8,128)S(1)} %walk3.1.both), channel_id=1, source_target_pairs={{0,31},{1,2},{2,1},{3,4},{4,3},{5,6},{6,5},{7,8},{8,7},{9,10},{10,... | collective-permute-start | bytes 786440 | tf_op jit(solution)/shard_map/ppermute | solution.py:460
  (16 other events, 68.1 us)
